TPU v7x, 128 devices: a whole 4x4x4 slice. The times are simulated.
128 devices in a mesh: list: 16 (over y, z), expert: 8 (over x, core).
Axes of the slice: x: 4, y: 4, z: 4, core: 2. Of those that a mesh axis runs over, the one named last changes fastest.
Arguments:
- hidden: bfloat16 [16384, 4096], P(('list', 'expert')), may hold values from -100 to 100
- query: bfloat16 [16384, 4096], P('list', 'expert'), may hold values from -32 to 32
- candidate_key_value: bfloat16 [16384, 2, 256], P('list'), may hold values from -6 to 6
- prefix_key_value: bfloat16 [1536, 2, 256], P('list'), may hold values from -36 to 36
- segment_ids: int32 [16, 1024], P('list'), may hold values from 0 to 15, never falling along the last dimension, each value on 1 to 128 neighbouring positions
- o_weight: bfloat16 [4096, 4096], P('expert', 'list'), may hold values from -3 to 3
- norm_gain: bfloat16 [4096], replicated, may hold values from 0.099609375 to 1.8984375
- routes: int32 [16384, 2], P(('list', 'expert')), may hold values from 0 to 63, all different within a row; in each aligned block of 128 rows (0 to 127, 128 to 255, ...) at most 8 rows name the same one
- route_weights: float32 [16384, 2], P(('list', 'expert')), may hold values from 0.1 to 1
- w_gate: bfloat16 [128, 4096, 768], P(('list', 'expert')), may hold values from -0.09375 to 0.09375
- w_up: bfloat16 [128, 4096, 768], P(('list', 'expert')), may hold values from -0.09375 to 0.09375
- w_down: bfloat16 [128, 768, 4096], P(('list', 'expert')), may hold values from -0.15625 to 0.15625
Outputs:
- attended: bfloat16 [16384, 4096], P(('list', 'expert'))
- moe_out: bfloat16 [16384, 4096], P(('list', 'expert'))
Inputs may be any that keep to these rules, and one draw needn't show every extreme that they name: `segment_ids`: each row numbers the 16 candidates of one list in order. `routes`: among the 128 tokens of one device no expert is named more than 8 times, and in every draw some expert is named exactly 8 times by the tokens of some device.
All inputs are finite; a program needn't handle non-finite values.
Results may differ from a plain program's by a relative error of at most 0.03.
Values may be sent and summed in bfloat16 or wider, within the bound.
No kernel may reach another device: no remote copies, remote signals or barrier semaphores. Data moves between devices by JAX's collectives and lax.ppermute only.
A program may use at most 192 MiB of HBM per device.

v0:
```python
import math

import jax
import jax.numpy as jnp
from jax import lax
from jax.sharding import PartitionSpec as P

D = 4096
QUERY_HEADS = 32
KEY_VALUE_HEADS = 2
HEAD_SIZE = 128
TOP = 2


masked_score = -1e30


def local(
    hidden,
    query,
    candidate_key_value,
    prefix_key_value,
    segment_ids,
    o_weight,
    norm_gain,
    routes,
    route_weights,
    w_gate,
    w_up,
    w_down,
):
    list_tok = query.shape[0]
    heads_dev = query.shape[1] // HEAD_SIZE
    tok_dev = hidden.shape[0]
    scale = 1.0 / math.sqrt(HEAD_SIZE)
    leading_head = lax.axis_index("expert") * heads_dev
    key_value_index = leading_head // (QUERY_HEADS // KEY_VALUE_HEADS)
    queries = query.reshape(list_tok, heads_dev, HEAD_SIZE)
    cand_head = lax.dynamic_slice_in_dim(
        candidate_key_value, key_value_index * HEAD_SIZE, HEAD_SIZE, 2
    )
    segment = segment_ids[0]
    position = jnp.arange(list_tok)
    allowed = (segment[:, None] == segment[None, :]) & (position[None, :] <= position[:, None])
    scores = (
        jnp.einsum("qhd,kd->qhk", queries, cand_head[:, 0], preferred_element_type=jnp.float32)
        * scale
    )
    scores = jnp.where(allowed[:, None, :], scores, masked_score)
    run_max = jnp.max(scores, axis=-1)
    expo = jnp.exp(scores - run_max[..., None])
    run_sum = jnp.sum(expo, axis=-1)
    run_acc = jnp.einsum(
        "qhk,kd->qhd",
        expo.astype(jnp.bfloat16),
        cand_head[:, 1],
        preferred_element_type=jnp.float32,
    )
    own_prefix = lax.dynamic_slice_in_dim(
        prefix_key_value, key_value_index * HEAD_SIZE, HEAD_SIZE, 2
    )
    shard_piece = lax.all_gather(own_prefix, "list", axis=0, tiled=True)
    piece_scores = (
        jnp.einsum("qhd,kd->qhk", queries, shard_piece[:, 0], preferred_element_type=jnp.float32)
        * scale
    )
    new_max = jnp.maximum(run_max, jnp.max(piece_scores, axis=-1))
    fade_factor = jnp.exp(run_max - new_max)
    piece_expo = jnp.exp(piece_scores - new_max[..., None])
    new_sum = run_sum * fade_factor + jnp.sum(piece_expo, axis=-1)
    new_acc = run_acc * fade_factor[..., None] + jnp.einsum(
        "qhk,kd->qhd",
        piece_expo.astype(jnp.bfloat16),
        shard_piece[:, 1],
        preferred_element_type=jnp.float32,
    )
    heads_out = (
        (new_acc / new_sum[..., None]).astype(jnp.bfloat16).reshape(list_tok, heads_dev * HEAD_SIZE)
    )
    wo_full = lax.all_gather(o_weight, "list", axis=1, tiled=True)
    attn = lax.psum_scatter(
        jnp.dot(heads_out, wo_full, preferred_element_type=jnp.float32).astype(jnp.bfloat16),
        "expert",
        scatter_dimension=0,
        tiled=True,
    ).astype(jnp.float32)
    attended = (hidden.astype(jnp.float32) + attn).astype(jnp.bfloat16)
    widened = attended.astype(jnp.float32)
    mean_square = jnp.mean(widened * widened, axis=-1, keepdims=True)
    normed = (widened * lax.rsqrt(mean_square + 1e-06) * norm_gain.astype(jnp.float32)).astype(
        jnp.bfloat16
    )
    n_list = lax.axis_size("list")
    n_expert_axis = lax.axis_size("expert")
    devices_all = n_list * n_expert_axis
    n_experts = devices_all // 2
    capacity = 2 * tok_dev * TOP // n_experts
    flat_routes = routes.reshape(-1)
    matched = (flat_routes[:, None] == jnp.arange(n_experts, dtype=jnp.int32)[None, :]).astype(
        jnp.int32
    )
    slot_index = jnp.sum((jnp.cumsum(matched, axis=0) - matched) * matched, axis=1)
    pair_token = jnp.arange(tok_dev * TOP, dtype=jnp.int32) // TOP
    target_row = flat_routes * capacity + slot_index
    packed = (
        jnp.zeros((n_experts * capacity, D), jnp.bfloat16).at[target_row].set(normed[pair_token])
    )
    outgoing = jnp.broadcast_to(
        packed.reshape(n_experts, 1, capacity, D), (n_experts, 2, capacity, D)
    ).reshape(devices_all, capacity, D)
    arrived_rows = lax.all_to_all(
        outgoing, ("list", "expert"), split_axis=0, concat_axis=0, tiled=True
    )
    flat_rows = arrived_rows.reshape(-1, D)
    gated = jnp.dot(flat_rows, w_gate[0], preferred_element_type=jnp.float32)
    upward = jnp.dot(flat_rows, w_up[0], preferred_element_type=jnp.float32)
    activ = (jax.nn.silu(gated) * upward).astype(jnp.bfloat16)
    result = jnp.dot(activ, w_down[0], preferred_element_type=jnp.float32).astype(jnp.bfloat16)
    produced = result.reshape(arrived_rows.shape)
    returned = lax.all_to_all(produced, ("list", "expert"), split_axis=0, concat_axis=0, tiled=True)
    returned_flat = returned.reshape(devices_all * capacity, D)
    first_half = 2 * flat_routes * capacity + slot_index
    second_half = first_half + capacity
    summed = returned_flat[first_half].astype(jnp.float32) + returned_flat[second_half].astype(
        jnp.float32
    )
    weighted = summed * route_weights.reshape(-1)[:, None]
    moe_out = jnp.sum(weighted.reshape(tok_dev, TOP, D), axis=1).astype(jnp.bfloat16)
    return (attended, moe_out)


def solution(mesh):
    placed = (
        P(("list", "expert"), None),
        P("list", "expert"),
        P("list", None, None),
        P("list", None, None),
        P("list", None),
        P("expert", "list"),
        P(),
        P(("list", "expert"), None),
        P(("list", "expert"), None),
        P(("list", "expert"), None, None),
        P(("list", "expert"), None, None),
        P(("list", "expert"), None, None),
    )
    return jax.shard_map(
        local,
        mesh=mesh,
        in_specs=placed,
        out_specs=(P(("list", "expert"), None), P(("list", "expert"), None)),
        check_vma=False,
    )
```

profile of v0, /device:TPU:0, one launch (start us, length us, event | category | flops | bytes accessed | tf_op | source)
XLA Modules:
  0.0 461.7 jit_solution(6484087146991598084)
XLA Ops:
  7.2 0.0 copy-start
  7.2 0.0 all-gather.2.cloned.1.call-start
  7.2 0.7 all-gather.2.cloned.1.call-update
  7.9 0.0 reduce-scatter.2.cloned.1.call-start
  8.0 0.8 constant_dynamic-slice_fusion.1
  8.8 28.9 %all_gather.6 = bf16[1536,2,128]{2,0,1:T(8,128)(2,1)} all-gather(bf16[96,2,128]{2,0,1:T(8,128)(2,1)S(1)} %copy.46), channel_id=1, replica_groups=mesh['list'=16,'expert'=8] {'list'}, dimensions={0}, use_global_device_ids=true | all-gather | bytes 835584 | tf_op jit(solution)/shard_map/all_gather | solution.py:62
  37.7 3.1 constant_dynamic-slice_fusion.2
  40.9 1.4 fusion.18
  42.2 0.0 copy-done
  42.2 8.0 %fusion.5 = (f32[1024,4]{0,1:T(4,128)S(1)}, f32[1024,1024,4]{1,0,2:T(8,128)}) fusion(pred[1024,1024]{0,1:T(8,128)(4,1)S(1)} %fusion.18, bf16[1024,1,128]{2,1,0:T(2,128)(2,1)S(1)} %get-tuple-element.7, bf16[1024,512]{1,0:T(8,128)(2,1)S(1)} %copy-done), kind=kOutput, calls=%fused_computation.13 | convolution fusion | flops 1086320640 | bytes 19152896 | tf_op jit(solution)/shard_map/qhd,kd->qhk/dot_general | solution.py:46
  50.3 4.4 bitcast_reduce_fusion
  54.7 16.0 %fusion.3 = f32[1024,4]{0,1:T(4,128)S(1)} fusion(f32[1024,1024,4]{1,0,2:T(8,128)} %get-tuple-element.14, f32[1024,4]{0,1:T(4,128)S(1)} %get-tuple-element.13, pred[1024,1024]{0,1:T(8,128)(4,1)S(1)} %fusion.18), kind=kLoop, calls=%fused_computation.11 | loop fusion | flops 16773120 | bytes 17858560 | tf_op jit(solution)/shard_map/reduce_sum | solution.py:52
  70.7 0.0 copy-start.4
  70.7 4.3 fusion.1
  75.0 0.0 copy-done.2
  75.0 0.0 copy-done.4
  75.1 0.0 copy-start.6
  75.1 10.7 %fusion.6 = f32[1024,4,128]{0,2,1:T(8,128)S(1)} fusion(f32[1536,1024,4]{1,0,2:T(8,128)} %copy-done.2, f32[1024,4]{0,1:T(4,128)S(1)} %max.13, bf16[1536,2,128]{2,0,1:T(8,128)(2,1)S(1)} %copy-done.4), kind=kOutput, calls=%fused_computation.14 | convolution fusion | flops 1629487104 | bytes 27672576 | tf_op jit(solution)/shard_map/qhk,kd->qhd/dot_general | solution.py:71
  85.7 0.0 copy-done.6
  85.7 8.6 %divide_convert_fusion = bf16[1024,4,128]{0,2,1:T(8,128)(2,1)S(1)} fusion(f32[1024,4,128]{0,2,1:T(8,128)S(1)} %fusion.6, f32[1024,1024,4]{1,0,2:T(8,128)} %get-tuple-element.14, f32[1024,4]{0,1:T(4,128)S(1)} %get-tuple-element.13, pred[1024,1024]{0,1:T(8,128)(4,1)S(1)} %fusion.18, f32[1024,4]{0,1:T(4,128)S(1)} %get-tuple-element.4, ...), kind=kOutput, calls=%fused_computation.40 | convolution fusion | flops 1092616192 | bytes 21282816 | tf_op jit(solution)/shard_map/qhk,kd->qhd/dot_general | solution.py:53
  94.4 0.0 all-gather.2.cloned.1.call-done
  94.4 9.4 %convolution_convert_fusion = bf16[1024,4096]{1,0:T(8,128)(2,1)} fusion(bf16[1024,512]{0,1:T(8,128)(2,1)S(1)} %bitcast.125, bf16[512,4096]{1,0:T(8,128)(2,1)} %all-gather.2.cloned.1.call-done), kind=kOutput, calls=%fused_computation.22 | convolution fusion | flops 4299161600 | bytes 13631488 | tf_op jit(solution)/shard_map/dot_general | solution.py:82
  103.8 0.0 reduce-scatter.2.cloned.1.call-update
  103.9 0.6 copy-done.8
  104.5 0.1 copy.32
  104.6 0.1 eq.48
  104.8 0.1 eq.52
  104.9 0.1 copy.35
  105.0 0.1 mul.135
  105.2 0.6 reduce-window.6
  105.8 0.2 slice_reduce_fusion
  106.0 0.1 copy.31
  106.2 0.1 mul.124
  106.3 0.0 copy-done.7
  106.3 0.1 fusion.39
  106.5 48.7 %reduce-scatter.2.cloned.1.call-done = bf16[128,4096]{1,0:T(8,128)(2,1)} async-done(((bf16[1024,4096]{1,0:T(8,128)(2,1)}), bf16[128,4096]{1,0:T(8,128)(2,1)}) %reduce-scatter.2.cloned.1.call-update) | async-done | bytes 1048592 | tf_op jit(solution)/shard_map/reduce_scatter | solution.py:81
  155.2 0.0 copy-done.5
  155.2 1.7 fusion.23
  156.8 0.0 copy-start.3
  156.9 0.3 fusion.25
  157.2 12.3 %scatter_custom_fusion = bf16[512,4096]{1,0:T(8,128)(2,1)} fusion(s32[256]{0:T(256)S(1)} %bitcast.118, bf16[128,4096]{1,0:T(8,128)(2,1)S(1)} %fusion.25, s32[1024]{0:T(1024)S(1)} %pad_clamp_fusion.2, bf16[]{:T(256)} %constant.66.clone.1), kind=kCustom, calls=%fused_computation.36 | custom fusion | bytes 4194306 | tf_op jit(solution)/shard_map/scatter | solution.py:106
  169.5 6.6 %broadcast_in_dim.22 = bf16[64,2,8,4096]{3,2,1,0:T(8,128)(2,1)} broadcast(bf16[64,8,4096]{2,1,0:T(8,128)(2,1)} %bitcast.112), dimensions={0,2,3} | broadcast | bytes 12582912 | tf_op jit(solution)/shard_map/broadcast_in_dim | solution.py:108
  176.1 0.0 copy-done.3
  176.1 106.1 %all_to_all.10 = bf16[128,8,4096]{2,1,0:T(8,128)(2,1)S(1)} all-to-all(bf16[128,8,4096]{2,1,0:T(8,128)(2,1)} %bitcast.111), channel_id=1, replica_groups=mesh['list'=16,'expert'=8] {'list','expert'}, dimensions={0} | all-to-all | bytes 16777216 | tf_op jit(solution)/shard_map/all_to_all | solution.py:111
  282.2 0.0 slice-done
  282.2 0.0 slice-done.1
  282.2 0.0 slice-start.4
  282.2 8.3 %fusion.8 = f32[1024,768]{1,0:T(8,128)} fusion(bf16[128,8,4096]{2,1,0:T(8,128)(2,1)S(1)} %all_to_all.10, bf16[1,4096,768]{2,1,0:T(8,128)(2,1)S(1)} %bitcast.120), kind=kOutput, calls=%fused_computation.15 | convolution fusion | flops 6442450944 | bytes 17825792 | tf_op jit(solution)/shard_map/dot_general | solution.py:116
  290.6 0.0 slice-done.2
  290.6 0.0 slice-done.3
  290.6 8.8 %multiply_convert_fusion = bf16[1024,768]{1,0:T(8,128)(2,1)S(1)} fusion(f32[1024,768]{1,0:T(8,128)} %fusion.8, bf16[1,4096,768]{2,1,0:T(8,128)(2,1)S(1)} %bitcast.122, bf16[128,8,4096]{2,1,0:T(8,128)(2,1)S(1)} %all_to_all.10), kind=kOutput, calls=%fused_computation.30 | convolution fusion | flops 6447169536 | bytes 19398656 | tf_op jit(solution)/shard_map/dot_general | solution.py:115
  299.4 0.0 slice-done.4
  299.4 0.0 slice-done.5
  299.4 8.9 %convert_bitcast_fusion = bf16[128,8,4096]{2,1,0:T(8,128)(2,1)} fusion(bf16[1024,768]{1,0:T(8,128)(2,1)S(1)} %multiply_convert_fusion, bf16[1,768,4096]{2,1,0:T(8,128)(2,1)S(1)} %bitcast.124), kind=kOutput, calls=%fused_computation.19 | convolution fusion | flops 6446645248 | bytes 16252928 | tf_op jit(solution)/shard_map/dot_general | solution.py:118
  308.3 7.7 %all-to-all-start.1 = ((bf16[128,8,4096]{2,1,0:T(8,128)(2,1)}), bf16[128,8,4096]{2,1,0:T(8,128)(2,1)}, u32[]{:S(2)}, u32[]{:S(2)}) async-start(bf16[128,8,4096]{2,1,0:T(8,128)(2,1)} %convert_bitcast_fusion), calls=%async_computation.2 | async-start | bytes 16777216 | tf_op jit(solution)/shard_map/all_to_all | solution.py:120
  316.0 0.0 copy-done.9
  316.0 0.1 copy.36
  316.1 100.2 %all-to-all-done.1 = bf16[128,8,4096]{2,1,0:T(8,128)(2,1)} async-done(((bf16[128,8,4096]{2,1,0:T(8,128)(2,1)}), bf16[128,8,4096]{2,1,0:T(8,128)(2,1)}, u32[]{:S(2)}, u32[]{:S(2)}) %all-to-all-start.1) | async-done | bytes 8388640 | tf_op jit(solution)/shard_map/all_to_all | solution.py:120
  416.3 8.3 %gather_fusion.1 = bf16[256,4096]{1,0:T(8,128)(2,1)S(1)} fusion(bf16[1024,4096]{1,0:T(8,128)(2,1)} %bitcast.23, s32[1024]{0:T(1024)S(1)} %pad_clamp_fusion), kind=kCustom, calls=%fused_computation.2 | custom fusion | bytes 4195328 | tf_op jit(solution)/shard_map/gather | solution.py:124
  424.7 9.7 %gather_fusion = bf16[256,4096]{1,0:T(8,128)(2,1)} fusion(bf16[1024,4096]{1,0:T(8,128)(2,1)} %bitcast.23, s32[1024]{0:T(1024)S(1)} %pad_clamp_fusion.1), kind=kCustom, calls=%fused_computation.1 | custom fusion | bytes 4195328 | tf_op jit(solution)/shard_map/gather | solution.py:124
  434.4 4.2 convert_add_fusion
  438.6 6.1 %add.152 = f32[128,2,4096]{2,1,0:T(2,128)} reshape(f32[256,4096]{1,0:T(8,128)} %convert_add_fusion) | data formatting | bytes 8388608 | tf_op jit(solution)/shard_map/add | solution.py:124
  444.7 9.6 %multiply_reduce_fusion = bf16[128,4096]{1,0:T(8,128)(2,1)} fusion(f32[128,2,4096]{2,1,0:T(2,128)} %add.152, f32[128,2]{1,0:T(8,128)S(1)} %copy.36), kind=kLoop, calls=%fused_computation.26 | loop fusion | flops 1572864 | bytes 5243904 | tf_op jit(solution)/shard_map/reduce_sum | solution.py:128
  454.4 0.0 copy-done.1
  (27 shorter events, 0.1 us)
Async XLA Ops:
  7.2 35.1 %copy-start = (bf16[1024,512]{1,0:T(8,128)(2,1)S(1)}, bf16[1024,512]{1,0:T(8,128)(2,1)}, u32[]{:S(2)}) copy-start(bf16[1024,512]{1,0:T(8,128)(2,1)} %param.13) | copy-start | bytes 3145732
  7.2 87.2 %all-gather.2.cloned.1.call-start = ((), (), s32[]{:S(2)}) async-start(), calls=%async_computation.3 | async-start | bytes 4456448 | tf_op jit(solution)/shard_map/all_gather | solution.py:80
  7.9 147.2 %reduce-scatter.2.cloned.1.call-start = ((), (), s32[]{:S(2)}) async-start(), calls=%async_computation.4 | async-start | bytes 9437184 | tf_op jit(solution)/shard_map/reduce_scatter | solution.py:81
  54.7 20.3 %copy-start.2 = (f32[1536,1024,4]{1,0,2:T(8,128)}, f32[1536,1024,4]{1,0,2:T(8,128)S(1)}, u32[]{:S(2)}) copy-start(f32[1536,1024,4]{1,0,2:T(8,128)S(1)} %get-tuple-element.16) | copy-start | bytes 75497472
  70.7 4.3 copy-start.4
  75.1 10.7 %copy-start.6 = (bf16[1024,1,128]{2,1,0:T(2,128)(2,1)S(1)}, bf16[1024,1,128]{2,1,0:T(2,128)(2,1)}, u32[]{:S(2)}) copy-start(bf16[1024,1,128]{2,1,0:T(2,128)(2,1)} %get-tuple-element.6) | copy-start | bytes 786436
  103.8 0.7 copy-start.8
  103.8 2.5 copy-start.7
  103.8 51.3 %copy-start.5 = (bf16[128,4096]{1,0:T(8,128)(2,1)S(1)}, bf16[128,4096]{1,0:T(8,128)(2,1)}, u32[]{:S(2)}) copy-start(bf16[128,4096]{1,0:T(8,128)(2,1)} %param.12) | copy-start | bytes 3145732
  156.8 19.3 %copy-start.3 = (bf16[128,4096]{1,0:T(8,128)(2,1)}, bf16[128,4096]{1,0:T(8,128)(2,1)S(1)}, u32[]{:S(2)}) copy-start(bf16[128,4096]{1,0:T(8,128)(2,1)S(1)} %get-tuple-element.3) | copy-start | bytes 3145732
  169.5 112.7 %slice-start = ((s8[6291456]{0:T(1024)(128)(4,1)}), s8[2097152]{0:T(1024)(128)(4,1)S(1)}, s32[]{:S(2)}) async-start(s8[6291456]{0:T(1024)(128)(4,1)} %bitcast.119), calls=%async_computation.5 | async-start | bytes 4194304
  176.1 106.1 %slice-start.1 = ((s8[6291456]{0:T(1024)(128)(4,1)}), s8[4194304]{0:T(1024)(128)(4,1)S(1)}, s32[]{:S(2)}) async-start(s8[6291456]{0:T(1024)(128)(4,1)} %bitcast.119), calls=%async_computation.6 | async-start | bytes 8388608
  176.1 114.4 %slice-start.2 = ((s8[6291456]{0:T(1024)(128)(4,1)}), s8[4194304]{0:T(1024)(128)(4,1)S(1)}, s32[]{:S(2)}) async-start(s8[6291456]{0:T(1024)(128)(4,1)} %bitcast.121), calls=%async_computation.7 | async-start | bytes 8388608
  282.2 8.3 %slice-start.3 = ((s8[6291456]{0:T(1024)(128)(4,1)}), s8[2097152]{0:T(1024)(128)(4,1)S(1)}, s32[]{:S(2)}) async-start(s8[6291456]{0:T(1024)(128)(4,1)} %bitcast.121), calls=%async_computation.8 | async-start | bytes 4194304
  282.2 17.1 %slice-start.4 = ((s8[6291456]{0:T(1024)(128)(4,1)}), s8[4194304]{0:T(1024)(128)(4,1)S(1)}, s32[]{:S(2)}) async-start(s8[6291456]{0:T(1024)(128)(4,1)} %bitcast.123), calls=%async_computation.9 | async-start | bytes 8388608
  290.6 8.8 %slice-start.5 = ((s8[6291456]{0:T(1024)(128)(4,1)}), s8[2097152]{0:T(1024)(128)(4,1)S(1)}, s32[]{:S(2)}) async-start(s8[6291456]{0:T(1024)(128)(4,1)} %bitcast.123), calls=%async_computation.10 | async-start | bytes 4194304
  308.3 7.7 %copy-start.9 = (f32[128,2]{0,1:T(2,128)S(1)}, f32[128,2]{0,1:T(2,128)}, u32[]{:S(2)}) copy-start(f32[128,2]{0,1:T(2,128)} %param.20) | copy-start | bytes 3076
  308.3 108.0 %all-to-all-start.1 = ((bf16[128,8,4096]{2,1,0:T(8,128)(2,1)}), bf16[128,8,4096]{2,1,0:T(8,128)(2,1)}, u32[]{:S(2)}, u32[]{:S(2)}) async-start(bf16[128,8,4096]{2,1,0:T(8,128)(2,1)} %convert_bitcast_fusion), calls=%async_computation.2 | async-start | bytes 16777216 | tf_op jit(solution)/shard_map/all_to_all | solution.py:120
  438.6 15.8 %copy-start.1 = (bf16[1024,512]{1,0:T(8,128)(2,1)S(1)}, bf16[1024,512]{1,0:T(8,128)(2,1)}, u32[]{:S(2)}) copy-start(bf16[1024,512]{1,0:T(8,128)(2,1)} %param.13) | copy-start | bytes 3145732
Sparse Core Ops, SparseCore 0:
  10.1 61.3 all-gather.1
  104.0 51.1 reduce-scatter.1
where the time goes:
time: 470 us; the launch traced here: 462 us
  waiting for transfers between devices  150 us (32%)
  blocking collectives  135 us (29%)
  matrix products  67.2 us (14%)
  local copies, waits for them, and re-layouts  49 us (10%)
  other arithmetic  38.3 us (8%)
  between operations  14.8 us (3%)
  starting transfers between devices  7.73 us (2%)
    all_to_all x1, blocking collectives, local(): lax.all_to_all(outgoing, ('list', 'expert'), split_axis=0, concat_axis=0,...  106 us
    all_to_all x1, waiting for transfers between devices, local(): lax.all_to_all(produced, ('list', 'expert'), split_axis=0, concat_axis=0,...  100 us
    reduce_scatter x1, waiting for transfers between devices, local(): lax.psum_scatter(jnp.dot(heads_out, wo_full, preferred_element_type=jnp.f...  48.7 us
    all_gather x1, blocking collectives, local(): shard_piece = lax.all_gather(own_prefix, 'list', axis=0, tiled=True)  28.9 us
    reduce_sum x1, other arithmetic, local(): run_sum = jnp.sum(expo, axis=-1)  16 us
    scatter x1, local copies, waits for them, and re-layouts, local(): jnp.zeros((n_experts * capacity, D), jnp.bfloat16).at[target_row]  12.3 us
    dot_general x1, matrix products, local(): jnp.einsum('qhk,kd->qhd', piece_expo.astype(jnp.bfloat16), shard_piece[:,...  10.7 us
    gather x1, local copies, waits for them, and re-layouts, local(): returned_flat[first_half].astype(jnp.float32)  9.72 us
  transfers between devices with their start and end apart: 3, of which 2 were waited for; matrix products, arithmetic and copies ran while one was open for 13% of the time, Pallas kernels for 0%

commit v1 on v0

v1 whole, which is shorter than its diff:
```python
import math

import jax
import jax.numpy as jnp
from jax import lax
from jax.experimental import pallas as pl
from jax.experimental.pallas import tpu as pltpu
from jax.sharding import Mesh
from jax.sharding import PartitionSpec as P

D = 4096
QUERY_HEADS = 32
KEY_VALUE_HEADS = 2
HEAD_SIZE = 128
TOP = 2
BLOCK = 128
CAP = 8

LIST = ("y", "z")
EXPERT = ("x", "core")
CHIP = ("y", "z", "x")
ALL = ("y", "z", "x", "core")
SWAP = [(0, 1), (1, 0)]

masked_score = -1e30
MIB = 1 << 20


def attention_kernel(q_ref, prefix_ref, cand_ref, segment_col_ref, segment_row_ref, out_ref):
    block = pl.program_id(0)
    heads = q_ref.shape[1] // HEAD_SIZE
    factor = math.log2(math.e) / math.sqrt(HEAD_SIZE)
    start = pl.multiple_of(jnp.maximum(block - 1, 0) * BLOCK, BLOCK)
    window = cand_ref[pl.ds(start, 2 * BLOCK), :]
    query_at = block * BLOCK + lax.broadcasted_iota(jnp.int32, (BLOCK, 2 * BLOCK), 0)
    key_at = start + lax.broadcasted_iota(jnp.int32, (BLOCK, 2 * BLOCK), 1)
    key_segment = segment_row_ref[:, pl.ds(start, 2 * BLOCK)]
    allowed = (segment_col_ref[...] == key_segment) & (key_at <= query_at)
    prefix = prefix_ref[...]

    def with_ones(value):
        return jnp.concatenate([value, jnp.ones_like(value)], axis=1)

    prefix_key, prefix_value = prefix[:, :HEAD_SIZE], with_ones(prefix[:, HEAD_SIZE:])
    window_key, window_value = window[:, :HEAD_SIZE], with_ones(window[:, HEAD_SIZE:])
    contract = (((1,), (1,)), ((), ()))
    for head in range(heads):
        columns = slice(head * HEAD_SIZE, (head + 1) * HEAD_SIZE)
        q = q_ref[:, columns]
        far = lax.dot_general(q, prefix_key, contract, preferred_element_type=jnp.float32)
        near = lax.dot_general(q, window_key, contract, preferred_element_type=jnp.float32)
        near = jnp.where(allowed, near, masked_score)
        top = jnp.maximum(
            jnp.max(far, axis=-1, keepdims=True), jnp.max(near, axis=-1, keepdims=True)
        )
        far = jnp.exp2((far - top) * factor).astype(jnp.bfloat16)
        near = jnp.exp2((near - top) * factor).astype(jnp.bfloat16)
        total = jnp.dot(far, prefix_value, preferred_element_type=jnp.float32) + jnp.dot(
            near, window_value, preferred_element_type=jnp.float32
        )
        out_ref[:, columns] = (total[:, :HEAD_SIZE] / total[:, HEAD_SIZE:]).astype(jnp.bfloat16)


def attention(query, prefix, cand, segment):
    tokens, width = query.shape
    return pl.pallas_call(
        attention_kernel,
        out_shape=jax.ShapeDtypeStruct((tokens, width), jnp.bfloat16),
        grid=(tokens // BLOCK,),
        in_specs=[
            pl.BlockSpec((BLOCK, width), lambda i: (i, 0)),
            pl.BlockSpec(prefix.shape, lambda i: (0, 0)),
            pl.BlockSpec(cand.shape, lambda i: (0, 0)),
            pl.BlockSpec((BLOCK, 1), lambda i: (i, 0)),
            pl.BlockSpec((1, tokens), lambda i: (0, 0)),
        ],
        out_specs=pl.BlockSpec((BLOCK, width), lambda i: (i, 0)),
        compiler_params=pltpu.CompilerParams(vmem_limit_bytes=40 * MIB),
        name="attention",
    )(query, prefix, cand, segment.reshape(tokens, 1), segment.reshape(1, tokens))


def norm_pack_kernel(hidden_ref, attn_ref, gain_ref, row_ref, attended_ref, packed_ref):
    attended = (hidden_ref[...].astype(jnp.float32) + attn_ref[...].astype(jnp.float32)).astype(
        jnp.bfloat16
    )
    attended_ref[...] = attended
    widened = attended.astype(jnp.float32)
    mean_square = jnp.mean(widened * widened, axis=-1, keepdims=True)
    normed = (widened * lax.rsqrt(mean_square + 1e-06) * gain_ref[...].astype(jnp.float32)).astype(
        jnp.bfloat16
    )
    rows = packed_ref.shape[0]
    tokens = normed.shape[0]
    at = lax.broadcasted_iota(jnp.int32, (rows, tokens), 0)
    pick = (at == row_ref[0:1, :]) | (at == row_ref[1:2, :])
    pick = pick.astype(jnp.float32).astype(jnp.bfloat16)
    packed_ref[...] = jnp.dot(pick, normed, preferred_element_type=jnp.float32).astype(jnp.bfloat16)


def norm_pack(hidden, attn, gain, rows):
    tokens, width = hidden.shape
    slots = 64 * CAP
    return pl.pallas_call(
        norm_pack_kernel,
        out_shape=(
            jax.ShapeDtypeStruct((tokens, width), jnp.bfloat16),
            jax.ShapeDtypeStruct((slots, width), jnp.bfloat16),
        ),
        compiler_params=pltpu.CompilerParams(vmem_limit_bytes=40 * MIB),
        name="norm_pack",
    )(hidden, attn, gain.reshape(1, width), rows.T)


def combine_kernel(back_ref, row_ref, weight_ref, out_ref):
    tokens, slots = out_ref.shape[0], back_ref.shape[0]
    at = lax.broadcasted_iota(jnp.int32, (tokens, slots), 1)
    back = back_ref[...]
    total = None
    for k in range(TOP):
        pick = (at == row_ref[:, k : k + 1]).astype(jnp.float32).astype(jnp.bfloat16)
        term = weight_ref[:, k : k + 1] * jnp.dot(pick, back, preferred_element_type=jnp.float32)
        total = term if total is None else total + term
    out_ref[...] = total.astype(jnp.bfloat16)


def combine(back, rows, weights):
    slots, width = back.shape
    tokens = rows.shape[0]
    step = 1024
    return pl.pallas_call(
        combine_kernel,
        out_shape=jax.ShapeDtypeStruct((tokens, width), jnp.bfloat16),
        grid=(width // step,),
        in_specs=[
            pl.BlockSpec((slots, step), lambda i: (0, i)),
            pl.BlockSpec((tokens, TOP), lambda i: (0, 0)),
            pl.BlockSpec((tokens, TOP), lambda i: (0, 0)),
        ],
        out_specs=pl.BlockSpec((tokens, step), lambda i: (0, i)),
        compiler_params=pltpu.CompilerParams(vmem_limit_bytes=40 * MIB),
        name="combine",
    )(back, rows, weights)


def half_expert(rows, w_gate, w_up, w_down):
    gated = jnp.dot(rows, w_gate, preferred_element_type=jnp.float32)
    upward = jnp.dot(rows, w_up, preferred_element_type=jnp.float32)
    activ = (jax.nn.silu(gated) * upward).astype(jnp.bfloat16)
    return jnp.dot(activ, w_down, preferred_element_type=jnp.float32)


def slots_of(routes):
    tok_dev = routes.shape[0]
    flat_routes = routes.reshape(-1)
    matched = (flat_routes[:, None] == jnp.arange(64, dtype=jnp.int32)[None, :]).astype(jnp.int32)
    slot_index = jnp.sum((jnp.cumsum(matched, axis=0) - matched) * matched, axis=1)
    return (flat_routes * CAP + slot_index).reshape(tok_dev, TOP)


def local(
    hidden,
    query,
    candidate_key_value,
    prefix_key_value,
    segment_ids,
    o_weight,
    norm_gain,
    routes,
    route_weights,
    w_gate,
    w_up,
    w_down,
):
    heads_dev = query.shape[1] // HEAD_SIZE
    expert_index = lax.axis_index("x") * 2 + lax.axis_index("core")
    head = (expert_index * heads_dev) // (QUERY_HEADS // KEY_VALUE_HEADS)

    def of_head(key_value):
        part = lax.dynamic_slice_in_dim(key_value, head * HEAD_SIZE, HEAD_SIZE, 2)
        return part.reshape(key_value.shape[0], 2 * HEAD_SIZE)

    own_prefix = of_head(prefix_key_value)
    n_list = lax.axis_size(LIST)
    prefix = lax.all_to_all(
        jnp.broadcast_to(own_prefix[None], (n_list,) + own_prefix.shape),
        LIST,
        split_axis=0,
        concat_axis=0,
        tiled=True,
    ).reshape(-1, 2 * HEAD_SIZE)
    wo_full = lax.all_gather(o_weight, LIST, axis=1, tiled=True)
    heads_out = attention(query, prefix, of_head(candidate_key_value), segment_ids[0])
    attn = lax.psum_scatter(
        jnp.dot(heads_out, wo_full, preferred_element_type=jnp.float32).astype(jnp.bfloat16),
        EXPERT,
        scatter_dimension=0,
        tiled=True,
    )
    rows = slots_of(routes)
    attended, packed = norm_pack(hidden, attn, norm_gain, rows)

    def across(slots):
        return lax.all_to_all(
            slots.reshape(64, CAP, D), CHIP, split_axis=0, concat_axis=0, tiled=True
        ).reshape(64 * CAP, D)

    mine = across(packed)
    other = lax.ppermute(mine, "core", SWAP)
    other_part = half_expert(other, w_gate[0], w_up[0], w_down[0]).astype(jnp.bfloat16)
    mine_part = half_expert(mine, w_gate[0], w_up[0], w_down[0])
    both = mine_part + lax.ppermute(other_part, "core", SWAP).astype(jnp.float32)
    back = across(both.astype(jnp.bfloat16))
    return attended, combine(back, rows, route_weights)


def solution(mesh):
    fine = Mesh(mesh.devices.reshape(4, 4, 4, 2), ALL)
    placed = (
        P(ALL, None),
        P(LIST, EXPERT),
        P(LIST, None, None),
        P(LIST, None, None),
        P(LIST, None),
        P(EXPERT, LIST),
        P(),
        P(ALL, None),
        P(ALL, None),
        P(ALL, None, None),
        P(ALL, None, None),
        P(ALL, None, None),
    )
    return jax.shard_map(
        local,
        mesh=fine,
        in_specs=placed,
        out_specs=(P(ALL, None), P(ALL, None)),
        check_vma=False,
    )
```

time: 470 us -> 332 us (0.71); the launches traced: 462 us -> 332 us
  blocking collectives: 135 us -> 62.2 us
  local copies, waits for them, and re-layouts: 49 us -> 10.3 us
  other arithmetic: 38.3 us -> 0.78 us
  Pallas kernels: 0 us -> 20 us
  matrix products: 67.2 us -> 57.2 us
  starting transfers between devices: 7.73 us -> 14.9 us
    all_to_all x1, blocking collectives: 106 us -> 62.2 us  [across(): lax.all_to_all(slots.reshape(64, CAP, D), CHIP, split_axis=0, concat_axis...]
    reduce_sum x5 -> x1, other arithmetic: 31.7 us -> 0.11 us  [slots_of(): jnp.sum((jnp.cumsum(matched, axis=0) - matched) * matched, axis=1)]
    all_to_all x1 -> x2, waiting for transfers between devices: 100 us -> 69.9 us  [the longest x1 54.9 us: across(): lax.all_to_all(slots.reshape(64, CAP, D), CHIP, split_axis=0, concat_axis...]
    all_gather x1 -> x0, blocking collectives: 28.9 us -> none  [local(): shard_piece = lax.all_gather(own_prefix, 'list', axis=0, tiled=True)]
    all_gather x1, waiting for transfers between devices: 0.02 us -> 24.8 us  [local(): wo_full = lax.all_gather(o_weight, LIST, axis=1, tiled=True)]
    pallas_call x0 -> x3, Pallas kernels: none -> 20 us  [the longest x1 13.3 us: attention(): pl.pallas_call(attention_kernel, out_shape=jax.ShapeDtypeStruct((tokens,...]
    gather x2 -> x0, local copies, waits for them, and re-layouts: 18.1 us -> none  [the longest x1 9.72 us: local(): returned_flat[first_half].astype(jnp.float32)]
    scatter x1 -> x0, local copies, waits for them, and re-layouts: 12.3 us -> none  [local(): jnp.zeros((n_experts * capacity, D), jnp.bfloat16).at[target_row]]
  transfers between devices with their start and end apart: 3 -> 6, of which waited for: 2 -> 6; matrix products, arithmetic and copies ran while one was open for 13% -> 3% of each run, Pallas kernels for 0% -> 4%
where the time goes in v1:
time: 332 us
  waiting for transfers between devices  152 us (46%)
  blocking collectives  62.2 us (19%)
  matrix products  57.2 us (17%)
  Pallas kernels  20 us (6%)
  starting transfers between devices  14.9 us (4%)
  between operations  14.3 us (4%)
  local copies, waits for them, and re-layouts  10.3 us (3%)
    all_to_all x1, blocking collectives, across(): lax.all_to_all(slots.reshape(64, CAP, D), CHIP, split_axis=0, concat_axis...  62.2 us
    all_to_all x1, waiting for transfers between devices, across(): lax.all_to_all(slots.reshape(64, CAP, D), CHIP, split_axis=0, concat_axis...  54.9 us
    reduce_scatter x1, waiting for transfers between devices, local(): lax.psum_scatter(jnp.dot(heads_out, wo_full, preferred_element_type=jnp.f...  49.4 us
    dot_general x2, matrix products, half_expert(): return jnp.dot(activ, w_down, preferred_element_type=jnp.float32)  34.4 us
    all_gather x1, waiting for transfers between devices, local(): wo_full = lax.all_gather(o_weight, LIST, axis=1, tiled=True)  24.8 us
    all_to_all x1, waiting for transfers between devices, local(): lax.all_to_all(jnp.broadcast_to(own_prefix[None], (n_list,) + own_prefix....  14.9 us
    pallas_call x1, Pallas kernels, attention(): pl.pallas_call(attention_kernel, out_shape=jax.ShapeDtypeStruct((tokens,...  13.3 us
    dot_general x1, matrix products, local(): jnp.dot(heads_out, wo_full, preferred_element_type=jnp.float32)  10.3 us
  transfers between devices with their start and end apart: 6, of which 6 were waited for; matrix products, arithmetic and copies ran while one was open for 3% of the time, Pallas kernels for 4%

profile of v1, /device:TPU:0, one launch (start us, length us, event | category | flops | bytes accessed | tf_op | source)
XLA Modules:
  0.0 331.9 jit_solution(268763364542267929)
XLA Ops:
  7.2 0.0 copy-start
  7.2 0.0 copy-start.6
  7.2 0.0 copy-start.2
  7.2 0.0 all-gather.2.cloned.1.call-start
  7.2 0.7 all-gather.2.cloned.1.call-update
  8.0 0.8 constant_dynamic-slice_fusion.1
  8.8 1.0 broadcast_in_dim.9
  9.8 8.1 %all-to-all-start = ((bf16[16,96,256]{2,1,0:T(8,128)(2,1)}), bf16[16,96,256]{2,1,0:T(8,128)(2,1)S(1)}, u32[]{:S(2)}, u32[]{:S(2)}) async-start(bf16[16,96,256]{2,1,0:T(8,128)(2,1)} %broadcast_in_dim.9), calls=%async_computation | async-start | bytes 1572864 | tf_op jit(solution)/shard_map/all_to_all | solution.py:185
  17.9 0.0 reduce-scatter.2.cloned.1.call-start
  18.0 0.0 copy-done
  18.0 0.4 constant_dynamic-slice_fusion
  18.4 0.1 copy.39
  18.4 0.0 copy-done.6
  18.5 0.2 copy.26.segment_col_ref
  18.7 14.9 %all-to-all-done = bf16[16,96,256]{2,1,0:T(8,128)(2,1)S(1)} async-done(((bf16[16,96,256]{2,1,0:T(8,128)(2,1)}), bf16[16,96,256]{2,1,0:T(8,128)(2,1)S(1)}, u32[]{:S(2)}, u32[]{:S(2)}) %all-to-all-start) | async-done | bytes 786464 | tf_op jit(solution)/shard_map/all_to_all | solution.py:185
  33.6 0.0 copy-done.2
  33.6 13.3 %attention.1 = bf16[1024,512]{1,0:T(8,128)(2,1)S(1)} custom-call(bf16[1024,512]{1,0:T(8,128)(2,1)S(1)} %copy-done.2, bf16[1536,256]{1,0:T(8,128)(2,1)S(1)} %bitcast.74, bf16[1024,256]{1,0:T(8,128)(2,1)S(1)} %bitcast.75, s32[1024,1]{1,0:T(8,128)S(1)} %copy.26.segment_col_ref, s32[1,1024]{1,0:T(1,128)S(1)} %copy-done.6), custom_call_target="tpu_custom_call" | custom-call | tf_op jit(solution)/shard_map/attention/pallas_call | solution.py:66
  46.9 0.0 copy-start.3
  46.9 1.0 copy-done.3
  47.9 24.8 %all-gather.2.cloned.1.call-done = bf16[512,4096]{1,0:T(8,128)(2,1)} async-done(((bf16[512,256]{1,0:T(8,128)(2,1)}), bf16[512,4096]{1,0:T(8,128)(2,1)}) %all-gather.2.cloned.1.call-update) | async-done | bytes 4194320 | tf_op jit(solution)/shard_map/all_gather | solution.py:192
  72.7 10.3 %convolution_convert_fusion = bf16[1024,4096]{1,0:T(8,128)(2,1)} fusion(bf16[1024,512]{1,0:T(8,128)(2,1)} %copy-done.3, bf16[512,4096]{1,0:T(8,128)(2,1)} %all-gather.2.cloned.1.call-done), kind=kOutput, calls=%fused_computation.1 | convolution fusion | flops 4299161600 | bytes 13631488 | tf_op jit(solution)/shard_map/dot_general | solution.py:195
  83.0 0.0 copy-start.9
  83.0 0.0 copy-start.8
  83.0 0.0 copy-start.4
  83.0 0.0 reduce-scatter.2.cloned.1.call-update
  83.0 0.6 copy-done.9
  83.7 0.1 copy.27
  83.8 0.1 eq.25
  83.9 0.1 eq.29
  84.0 0.0 copy-done.8
  84.1 0.1 copy.30
  84.2 0.6 reduce-window.6
  84.8 0.2 slice_reduce_fusion
  85.1 0.1 fusion.32
  85.2 0.1 reduce_sum.12
  85.3 0.1 copy.31.row_ref
  85.4 49.4 %reduce-scatter.2.cloned.1.call-done.attn_ref = bf16[128,4096]{1,0:T(8,128)(2,1)} async-done(((bf16[1024,4096]{1,0:T(8,128)(2,1)}), bf16[128,4096]{1,0:T(8,128)(2,1)}) %reduce-scatter.2.cloned.1.call-update) | async-done | bytes 1048592 | tf_op jit(solution)/shard_map/reduce_scatter | solution.py:194
  134.8 0.0 copy-done.4
  134.8 0.0 copy-start.5
  134.8 1.2 copy-done.5
  136.0 1.8 norm_pack.1
  137.8 62.2 %all_to_all.15 = bf16[64,8,4096]{2,1,0:T(8,128)(2,1)S(1)} all-to-all(bf16[64,8,4096]{2,1,0:T(8,128)(2,1)S(1)} %bitcast.73), channel_id=1, replica_groups=mesh['y'=4,'z'=4,'x'=4,'core'=2] {'y','z','x'}, dimensions={0} | all-to-all | bytes 8388608 | tf_op jit(solution)/shard_map/all_to_all | solution.py:204
  200.0 0.0 copy-start.7
  200.0 1.9 copy-done.7
  202.0 0.0 collective-permute-start
  202.0 7.2 %collective-permute-done = bf16[512,4096]{1,0:T(8,128)(2,1)S(1)} collective-permute-done((bf16[512,4096]{1,0:T(8,128)(2,1)S(1)}, bf16[512,4096]{1,0:T(8,128)(2,1)S(1)}, u32[]{:S(2)}, u32[]{:S(2)}) %collective-permute-start) | collective-permute-done | bytes 4194336 | tf_op jit(solution)/shard_map/ppermute | solution.py:209
  209.1 0.0 copy-start.11
  209.1 2.0 copy-done.11
  211.1 5.5 %fusion.4 = f32[512,768]{1,0:T(8,128)S(1)} fusion(bf16[512,4096]{1,0:T(8,128)(2,1)S(1)} %collective-permute-done, bf16[1,4096,768]{2,1,0:T(8,128)(2,1)} %param.22), kind=kOutput, calls=%fused_computation.6 | convolution fusion | flops 3221225472 | bytes 12058624 | tf_op jit(solution)/shard_map/dot_general | solution.py:148
  216.6 16.6 %fusion.12 = bf16[512,4096]{1,0:T(8,128)(2,1)} fusion(bf16[1,768,4096]{2,1,0:T(8,128)(2,1)} %param.23, f32[512,768]{1,0:T(8,128)S(1)} %fusion.4, bf16[512,4096]{1,0:T(8,128)(2,1)} %copy-done.11, bf16[1,4096,768]{2,1,0:T(8,128)(2,1)} %param.21), kind=kOutput, calls=%fused_computation.14 | convolution fusion | flops 6446907392 | bytes 22544384 | tf_op jit(solution)/shard_map/dot_general | solution.py:150
  233.2 0.1 collective-permute-start.1
  233.3 7.0 %fusion.10 = f32[512,768]{1,0:T(8,128)S(1)} fusion(bf16[1,4096,768]{2,1,0:T(8,128)(2,1)} %param.21, bf16[64,8,4096]{2,1,0:T(8,128)(2,1)} %copy-done.7), kind=kOutput, calls=%fused_computation.12 | convolution fusion | flops 3221225472 | bytes 12058624 | tf_op jit(solution)/shard_map/dot_general | solution.py:147
  240.4 0.3 collective-permute-done.1
  240.7 17.8 %fusion.17 = bf16[64,8,4096]{2,1,0:T(8,128)(2,1)} fusion(bf16[512,4096]{1,0:T(8,128)(2,1)} %collective-permute-done.1, bf16[1,768,4096]{2,1,0:T(8,128)(2,1)} %param.23, f32[512,768]{1,0:T(8,128)S(1)} %fusion.10, bf16[1,4096,768]{2,1,0:T(8,128)(2,1)} %param.22, bf16[64,8,4096]{2,1,0:T(8,128)(2,1)} %copy-done.7), kind=kOutput, calls=%fused_computation.15 | convolution fusion | flops 6451101696 | bytes 26738688 | tf_op jit(solution)/shard_map/dot_general | solution.py:150
  258.5 0.0 copy-start.10
  258.5 6.6 %all-to-all-start.2 = ((bf16[64,8,4096]{2,1,0:T(8,128)(2,1)}), bf16[64,8,4096]{2,1,0:T(8,128)(2,1)}, u32[]{:S(2)}, u32[]{:S(2)}) async-start(bf16[64,8,4096]{2,1,0:T(8,128)(2,1)} %fusion.17), calls=%async_computation.3 | async-start | bytes 8388608 | tf_op jit(solution)/shard_map/all_to_all | solution.py:204
  265.1 0.0 copy-done.10
  265.1 0.0 copy-start.1
  265.1 0.1 copy.32.weight_ref
  265.2 54.9 %all-to-all-done.2 = bf16[64,8,4096]{2,1,0:T(8,128)(2,1)} async-done(((bf16[64,8,4096]{2,1,0:T(8,128)(2,1)}), bf16[64,8,4096]{2,1,0:T(8,128)(2,1)}, u32[]{:S(2)}, u32[]{:S(2)}) %all-to-all-start.2) | async-done | bytes 4194336 | tf_op jit(solution)/shard_map/all_to_all | solution.py:204
  320.1 4.9 %combine.1 = bf16[128,4096]{1,0:T(8,128)(2,1)} custom-call(bf16[512,4096]{1,0:T(8,128)(2,1)} %bitcast.10.back_ref, s32[128,2]{1,0:T(8,128)S(1)} %add.26.row_ref, f32[128,2]{1,0:T(8,128)S(1)} %copy.32.weight_ref), custom_call_target="tpu_custom_call" | custom-call | tf_op jit(solution)/shard_map/combine/pallas_call | solution.py:131
  325.0 0.0 copy-done.1
  (7 shorter events, 0.1 us)
Async XLA Ops:
  7.2 10.8 %copy-start = (bf16[1024,2,256]{2,1,0:T(2,128)(2,1)S(1)}, bf16[1024,2,256]{2,1,0:T(2,128)(2,1)}, u32[]{:S(2)}) copy-start(bf16[1024,2,256]{2,1,0:T(2,128)(2,1)} %param.14) | copy-start | bytes 3145732
  7.2 11.3 %copy-start.6 = (s32[1,1024]{1,0:T(1,128)S(1)}, s32[1,1024]{1,0:T(1,128)}, u32[]{:S(2)}) copy-start(s32[1,1024]{1,0:T(1,128)} %segment_row_ref.1) | copy-start | bytes 12292
  7.2 26.4 %copy-start.2 = (bf16[1024,512]{1,0:T(8,128)(2,1)S(1)}, bf16[1024,512]{1,0:T(8,128)(2,1)}, u32[]{:S(2)}) copy-start(bf16[1024,512]{1,0:T(8,128)(2,1)} %q_ref.1) | copy-start | bytes 3145732
  7.2 65.5 %all-gather.2.cloned.1.call-start = ((), (), s32[]{:S(2)}) async-start(), calls=%async_computation.4 | async-start | bytes 4456448 | tf_op jit(solution)/shard_map/all_gather | solution.py:192
  9.8 23.8 %all-to-all-start = ((bf16[16,96,256]{2,1,0:T(8,128)(2,1)}), bf16[16,96,256]{2,1,0:T(8,128)(2,1)S(1)}, u32[]{:S(2)}, u32[]{:S(2)}) async-start(bf16[16,96,256]{2,1,0:T(8,128)(2,1)} %broadcast_in_dim.9), calls=%async_computation | async-start | bytes 1572864 | tf_op jit(solution)/shard_map/all_to_all | solution.py:185
  17.9 116.9 %reduce-scatter.2.cloned.1.call-start = ((), (), s32[]{:S(2)}) async-start(), calls=%async_computation.5 | async-start | bytes 9437184 | tf_op jit(solution)/shard_map/reduce_scatter | solution.py:194
  46.9 1.0 copy-start.3
  83.0 0.7 copy-start.9
  83.0 1.1 copy-start.8
  83.0 51.8 %copy-start.4 = (bf16[128,4096]{1,0:T(8,128)(2,1)S(1)}, bf16[128,4096]{1,0:T(8,128)(2,1)}, u32[]{:S(2)}) copy-start(bf16[128,4096]{1,0:T(8,128)(2,1)} %hidden_ref.1) | copy-start | bytes 3145732
  134.8 1.2 copy-start.5
  200.0 1.9 copy-start.7
  202.0 7.2 %collective-permute-start = (bf16[512,4096]{1,0:T(8,128)(2,1)S(1)}, bf16[512,4096]{1,0:T(8,128)(2,1)S(1)}, u32[]{:S(2)}, u32[]{:S(2)}) collective-permute-start(bf16[512,4096]{1,0:T(8,128)(2,1)S(1)} %bitcast.78), channel_id=1, source_target_pairs={{0,1},{1,0},{2,3},{3,2},{4,5},{5,4},{6,7},{7,6},{8,9},{9,8},{10,11... | collective-permute-start | bytes 12582920 | tf_op jit(solution)/shard_map/ppermute | solution.py:209
  209.1 2.0 copy-start.11
  233.2 7.5 %collective-permute-start.1 = (bf16[512,4096]{1,0:T(8,128)(2,1)}, bf16[512,4096]{1,0:T(8,128)(2,1)}, u32[]{:S(2)}, u32[]{:S(2)}) collective-permute-start(bf16[512,4096]{1,0:T(8,128)(2,1)} %fusion.12), channel_id=1, source_target_pairs={{0,1},{1,0},{2,3},{3,2},{4,5},{5,4},{6,7},{7,6},{8,9},{9,8},{10,11... | collective-permute-start | bytes 12582920 | tf_op jit(solution)/shard_map/ppermute | solution.py:212
  258.5 6.6 %copy-start.10 = (f32[128,2]{0,1:T(2,128)S(1)}, f32[128,2]{0,1:T(2,128)}, u32[]{:S(2)}) copy-start(f32[128,2]{0,1:T(2,128)} %param.20) | copy-start | bytes 3076
  258.5 61.6 %all-to-all-start.2 = ((bf16[64,8,4096]{2,1,0:T(8,128)(2,1)}), bf16[64,8,4096]{2,1,0:T(8,128)(2,1)}, u32[]{:S(2)}, u32[]{:S(2)}) async-start(bf16[64,8,4096]{2,1,0:T(8,128)(2,1)} %fusion.17), calls=%async_computation.3 | async-start | bytes 8388608 | tf_op jit(solution)/shard_map/all_to_all | solution.py:204
  265.1 60.0 %copy-start.1 = (bf16[1024,2,256]{2,1,0:T(2,128)(2,1)S(1)}, bf16[1024,2,256]{2,1,0:T(2,128)(2,1)}, u32[]{:S(2)}) copy-start(bf16[1024,2,256]{2,1,0:T(2,128)(2,1)} %param.14) | copy-start | bytes 3145732
Sparse Core Ops, SparseCore 0:
  10.2 62.5 all-gather.1
  83.1 51.5 reduce-scatter.1

commit v2 on v1

--- a/solution.py
+++ b/solution.py
@@ -75,7 +75,7 @@
             pl.BlockSpec((1, tokens), lambda i: (0, 0)),
         ],
         out_specs=pl.BlockSpec((BLOCK, width), lambda i: (i, 0)),
-        compiler_params=pltpu.CompilerParams(vmem_limit_bytes=40 * MIB),
+        compiler_params=pltpu.CompilerParams(vmem_limit_bytes=58 * MIB),
         name="attention",
     )(query, prefix, cand, segment.reshape(tokens, 1), segment.reshape(1, tokens))
 
@@ -107,7 +107,7 @@
             jax.ShapeDtypeStruct((tokens, width), jnp.bfloat16),
             jax.ShapeDtypeStruct((slots, width), jnp.bfloat16),
         ),
-        compiler_params=pltpu.CompilerParams(vmem_limit_bytes=40 * MIB),
+        compiler_params=pltpu.CompilerParams(vmem_limit_bytes=58 * MIB),
         name="norm_pack",
     )(hidden, attn, gain.reshape(1, width), rows.T)
 
@@ -138,16 +138,141 @@
             pl.BlockSpec((tokens, TOP), lambda i: (0, 0)),
         ],
         out_specs=pl.BlockSpec((tokens, step), lambda i: (0, i)),
-        compiler_params=pltpu.CompilerParams(vmem_limit_bytes=40 * MIB),
+        compiler_params=pltpu.CompilerParams(vmem_limit_bytes=58 * MIB),
         name="combine",
     )(back, rows, weights)
 
 
-def half_expert(rows, w_gate, w_up, w_down):
-    gated = jnp.dot(rows, w_gate, preferred_element_type=jnp.float32)
-    upward = jnp.dot(rows, w_up, preferred_element_type=jnp.float32)
-    activ = (jax.nn.silu(gated) * upward).astype(jnp.bfloat16)
-    return jnp.dot(activ, w_down, preferred_element_type=jnp.float32)
+def expert_kernel(
+    x_hbm,
+    gate_hbm,
+    up_hbm,
+    down_hbm,
+    gate2_hbm,
+    up2_hbm,
+    down2_hbm,
+    out_hbm,
+    x_ref,
+    gate_ref,
+    up_ref,
+    down_ref,
+    act_ref,
+    out_ref,
+    x_sem,
+    in_sem,
+    down_sem,
+    out_sem,
+):
+    hidden_units = gate_hbm.shape[1]
+    width = x_hbm.shape[1]
+    step, wide = 256, 1024
+    per_half = hidden_units // step
+
+    def first_copies(j):
+        half, at = j // per_half, pl.ds((j % per_half) * step, step)
+        to = pl.ds(j * step, step)
+        gate, up = ((gate_hbm, up_hbm), (gate2_hbm, up2_hbm))[half]
+        return (
+            pltpu.make_async_copy(gate.at[:, at], gate_ref.at[:, to], in_sem.at[0, j]),
+            pltpu.make_async_copy(up.at[:, at], up_ref.at[:, to], in_sem.at[1, j]),
+        )
+
+    def second_copies(j):
+        at = pl.ds(j * wide, wide)
+        return tuple(
+            pltpu.make_async_copy(
+                down.at[:, at],
+                down_ref.at[pl.ds(half * hidden_units, hidden_units), at],
+                down_sem.at[half, j],
+            )
+            for half, down in enumerate((down_hbm, down2_hbm))
+        )
+
+    def out_copy(j):
+        at = pl.ds(j * wide, wide)
+        return pltpu.make_async_copy(out_ref.at[:, at], out_hbm.at[:, at], out_sem.at[j])
+
+    x_copy = pltpu.make_async_copy(x_hbm, x_ref, x_sem)
+    loads = [first_copies(j) for j in range(2 * per_half)]
+    loads += [second_copies(j) for j in range(width // wide)]
+    ahead = 2
+    x_copy.start()
+    for copies in loads[:ahead]:
+        for copy in copies:
+            copy.start()
+    x_copy.wait()
+    for j, copies in enumerate(loads):
+        for copy in loads[j + ahead] if j + ahead < len(loads) else ():
+            copy.start()
+        for copy in copies:
+            copy.wait()
+        if j < 2 * per_half:
+            at = slice(j * step, (j + 1) * step)
+            x = x_ref[...]
+            gated = jnp.dot(x, gate_ref[:, at], preferred_element_type=jnp.float32)
+            upward = jnp.dot(x, up_ref[:, at], preferred_element_type=jnp.float32)
+            act_ref[:, at] = (gated / (1.0 + jnp.exp(-gated)) * upward).astype(jnp.bfloat16)
+        else:
+            j -= 2 * per_half
+            at = slice(j * wide, (j + 1) * wide)
+            out_ref[:, at] = jnp.dot(
+                act_ref[...], down_ref[:, at], preferred_element_type=jnp.float32
+            ).astype(jnp.bfloat16)
+            out_copy(j).start()
+    for j in range(width // wide):
+        out_copy(j).wait()
+
+
+def whole_expert(rows, own, swapped):
+    slots, width = rows.shape
+    both = 2 * own[0].shape[1]
+    anywhere = pl.BlockSpec(memory_space=pl.ANY)
+    return pl.pallas_call(
+        expert_kernel,
+        out_shape=jax.ShapeDtypeStruct(rows.shape, jnp.bfloat16),
+        in_specs=[anywhere] * 7,
+        out_specs=anywhere,
+        scratch_shapes=[
+            pltpu.VMEM((slots, width), jnp.bfloat16),
+            pltpu.VMEM((width, both), jnp.bfloat16),
+            pltpu.VMEM((width, both), jnp.bfloat16),
+            pltpu.VMEM((both, width), jnp.bfloat16),
+            pltpu.VMEM((slots, both), jnp.bfloat16),
+            pltpu.VMEM((slots, width), jnp.bfloat16),
+            pltpu.SemaphoreType.DMA,
+            pltpu.SemaphoreType.DMA((2, 6)),
+            pltpu.SemaphoreType.DMA((2, 4)),
+            pltpu.SemaphoreType.DMA((4,)),
+        ],
+        compiler_params=pltpu.CompilerParams(vmem_limit_bytes=58 * MIB),
+        name="whole_expert",
+    )(rows, *own, *swapped)
+
+
+def project_kernel(heads_ref, weight_ref, out_ref):
+    wide = weight_ref.shape[2]
+    for piece in range(weight_ref.shape[0]):
+        out_ref[:, piece * wide : (piece + 1) * wide] = jnp.dot(
+            heads_ref[...], weight_ref[piece], preferred_element_type=jnp.float32
+        ).astype(jnp.bfloat16)
+
+
+def project(heads, weight):
+    tokens, width = heads.shape
+    pieces, _, wide = weight.shape
+    step = 2
+    return pl.pallas_call(
+        project_kernel,
+        out_shape=jax.ShapeDtypeStruct((tokens, pieces * wide), jnp.bfloat16),
+        grid=(pieces // step,),
+        in_specs=[
+            pl.BlockSpec((tokens, width), lambda i: (0, 0)),
+            pl.BlockSpec((step, width, wide), lambda i: (i, 0, 0)),
+        ],
+        out_specs=pl.BlockSpec((tokens, step * wide), lambda i: (0, i)),
+        compiler_params=pltpu.CompilerParams(vmem_limit_bytes=58 * MIB),
+        name="project",
+    )(heads, weight)
 
 
 def slots_of(routes):
@@ -189,10 +314,10 @@
         concat_axis=0,
         tiled=True,
     ).reshape(-1, 2 * HEAD_SIZE)
-    wo_full = lax.all_gather(o_weight, LIST, axis=1, tiled=True)
+    wo_pieces = lax.all_gather(o_weight, LIST, axis=0, tiled=False)
     heads_out = attention(query, prefix, of_head(candidate_key_value), segment_ids[0])
     attn = lax.psum_scatter(
-        jnp.dot(heads_out, wo_full, preferred_element_type=jnp.float32).astype(jnp.bfloat16),
+        project(heads_out, wo_pieces),
         EXPERT,
         scatter_dimension=0,
         tiled=True,
@@ -205,12 +330,9 @@
             slots.reshape(64, CAP, D), CHIP, split_axis=0, concat_axis=0, tiled=True
         ).reshape(64 * CAP, D)
 
-    mine = across(packed)
-    other = lax.ppermute(mine, "core", SWAP)
-    other_part = half_expert(other, w_gate[0], w_up[0], w_down[0]).astype(jnp.bfloat16)
-    mine_part = half_expert(mine, w_gate[0], w_up[0], w_down[0])
-    both = mine_part + lax.ppermute(other_part, "core", SWAP).astype(jnp.float32)
-    back = across(both.astype(jnp.bfloat16))
+    own = (w_gate[0], w_up[0], w_down[0])
+    swapped = tuple(lax.ppermute(w, "core", SWAP) for w in own)
+    back = across(whole_expert(across(packed), own, swapped))
     return attended, combine(back, rows, route_weights)
 
 

time: 332 us -> 313 us (0.943)
  blocking collectives: 62.2 us -> 0 us
  matrix products: 57.2 us -> 0 us
  waiting for transfers between devices: 152 us -> 195 us
  Pallas kernels: 20 us -> 62.3 us
  starting transfers between devices: 14.9 us -> 31.5 us
    all_to_all x1 -> x0, blocking collectives: 62.2 us -> none  [across(): lax.all_to_all(slots.reshape(64, CAP, D), CHIP, split_axis=0, concat_axis...]
    dot_general x5 -> x0, matrix products: 57.2 us -> none  [the longest x2 34.4 us: half_expert(): return jnp.dot(activ, w_down, preferred_element_type=jnp.float32)]
    all_to_all x1 -> x2, waiting for transfers between devices: 54.9 us -> 110 us  [across(): lax.all_to_all(slots.reshape(64, CAP, D), CHIP, split_axis=0, concat_axis...]
    pallas_call x0 -> x2, Pallas kernels: none -> 37.2 us  [the longest x1 26.9 us: whole_expert(): pl.pallas_call(expert_kernel, out_shape=jax.ShapeDtypeStruct(rows.shape,...]
    all_to_all x1 -> x2, starting transfers between devices: 6.56 us -> 22.6 us  [across(): lax.all_to_all(slots.reshape(64, CAP, D), CHIP, split_axis=0, concat_axis...]
    all_gather x1, waiting for transfers between devices: 24.8 us -> 16.2 us  [local(): wo_pieces = lax.all_gather(o_weight, LIST, axis=0, tiled=False)]
    ppermute x2 -> x3, waiting for transfers between devices: 7.47 us -> 0.01 us  [local(): swapped = tuple((lax.ppermute(w, 'core', SWAP) for w in own))]
    reduce_scatter x1, waiting for transfers between devices: 49.4 us -> 54.7 us  [local(): lax.psum_scatter(project(heads_out, wo_pieces), EXPERT, scatter_dimension...]
  transfers between devices with their start and end apart: 6 -> 8, of which waited for: 6 -> 5; matrix products, arithmetic and copies ran while one was open for 3% -> 3% of each run, Pallas kernels for 4% -> 6%
where the time goes in v2:
time: 313 us; the launch traced here: 312 us
  waiting for transfers between devices  195 us (62%)
  Pallas kernels  62.3 us (20%)
  starting transfers between devices  31.5 us (10%)
  between operations  14.2 us (5%)
  local copies, waits for them, and re-layouts  8.54 us (3%)
    all_to_all x2, waiting for transfers between devices, across(): lax.all_to_all(slots.reshape(64, CAP, D), CHIP, split_axis=0, concat_axis...  110 us
    reduce_scatter x1, waiting for transfers between devices, local(): lax.psum_scatter(project(heads_out, wo_pieces), EXPERT, scatter_dimension...  54.7 us
    pallas_call x1, Pallas kernels, whole_expert(): pl.pallas_call(expert_kernel, out_shape=jax.ShapeDtypeStruct(rows.shape,...  26.9 us
    all_to_all x2, starting transfers between devices, across(): lax.all_to_all(slots.reshape(64, CAP, D), CHIP, split_axis=0, concat_axis...  22.6 us
    all_gather x1, waiting for transfers between devices, local(): wo_pieces = lax.all_gather(o_weight, LIST, axis=0, tiled=False)  16.2 us
    pallas_call x1, Pallas kernels, attention(): pl.pallas_call(attention_kernel, out_shape=jax.ShapeDtypeStruct((tokens,...  14.9 us
    all_to_all x1, waiting for transfers between devices, local(): lax.all_to_all(jnp.broadcast_to(own_prefix[None], (n_list,) + own_prefix....  13.5 us
    pallas_call x1, Pallas kernels, project(): pl.pallas_call(project_kernel, out_shape=jax.ShapeDtypeStruct((tokens, pi...  10.4 us
  transfers between devices with their start and end apart: 8, of which 5 were waited for; matrix products, arithmetic and copies ran while one was open for 3% of the time, Pallas kernels for 6%

profile of v2, /device:TPU:0, one launch (start us, length us, event | category | flops | bytes accessed | tf_op | source)
XLA Modules:
  0.0 312.2 jit_solution(1060935453914767139)
XLA Ops:
  7.2 0.0 copy-start
  7.2 0.0 all-gather.3.cloned.1.call-start
  7.2 0.7 all-gather.3.cloned.1.call-update
  7.9 0.8 constant_dynamic-slice_fusion.1
  8.8 1.0 broadcast_in_dim.9
  9.8 8.1 %all-to-all-start = ((bf16[16,96,256]{2,1,0:T(8,128)(2,1)}), bf16[16,96,256]{2,1,0:T(8,128)(2,1)S(1)}, u32[]{:S(2)}, u32[]{:S(2)}) async-start(bf16[16,96,256]{2,1,0:T(8,128)(2,1)} %broadcast_in_dim.9), calls=%async_computation | async-start | bytes 1572864 | tf_op jit(solution)/shard_map/all_to_all | solution.py:310
  17.9 0.0 reduce-scatter.2.cloned.1.call-start
  17.9 0.0 copy-done
  18.0 0.4 constant_dynamic-slice_fusion
  18.3 0.9 copy.39
  19.2 1.7 copy.26.segment_col_ref
  20.9 13.5 %all-to-all-done = bf16[16,96,256]{2,1,0:T(8,128)(2,1)S(1)} async-done(((bf16[16,96,256]{2,1,0:T(8,128)(2,1)}), bf16[16,96,256]{2,1,0:T(8,128)(2,1)S(1)}, u32[]{:S(2)}, u32[]{:S(2)}) %all-to-all-start) | async-done | bytes 786464 | tf_op jit(solution)/shard_map/all_to_all | solution.py:310
  34.4 0.0 copy-start.2
  34.4 0.9 copy-done.2
  35.3 14.9 %attention.1.heads_ref = bf16[1024,512]{1,0:T(8,128)(2,1)} custom-call(bf16[1024,512]{1,0:T(8,128)(2,1)} %q_ref.1, bf16[1536,256]{1,0:T(8,128)(2,1)} %bitcast.47, bf16[1024,256]{1,0:T(8,128)(2,1)} %bitcast.48, s32[1024,1]{1,0:T(8,128)} %copy.26.segment_col_ref, s32[1,1024]{1,0:T(1,128)} %segment_row_ref.1), custom_call_target="tpu_custom_call" | custom-call | tf_op jit(solution)/shard_map/attention/pallas_call | solution.py:66
  50.2 16.2 %all-gather.3.cloned.1.call-done = bf16[8192,256]{1,0:T(8,128)(2,1)} async-done(((bf16[512,256]{1,0:T(8,128)(2,1)}), bf16[8192,256]{1,0:T(8,128)(2,1)}) %all-gather.3.cloned.1.call-update) | async-done | bytes 4194320 | tf_op jit(solution)/shard_map/all_gather | solution.py:317
  66.4 10.4 %project.1 = bf16[1024,4096]{1,0:T(8,128)(2,1)} custom-call(bf16[1024,512]{1,0:T(8,128)(2,1)} %attention.1.heads_ref, bf16[16,512,256]{2,1,0:T(8,128)(2,1)} %bitcast.45), custom_call_target="tpu_custom_call" | custom-call | tf_op jit(solution)/shard_map/project/pallas_call | solution.py:264
  76.8 0.0 copy-start.5
  76.8 0.0 copy-start.4
  76.8 0.0 reduce-scatter.2.cloned.1.call-update
  76.8 0.1 collective-permute-start
  76.9 0.5 collective-permute-start.1
  77.4 0.1 collective-permute-start.2
  77.5 0.0 copy-done.5
  77.5 0.1 copy.27
  77.6 0.1 eq.25
  77.8 0.1 eq.29
  77.9 0.0 copy-done.4
  77.9 0.6 reshape.48.gain_ref
  78.5 0.1 copy.30
  78.7 0.6 reduce-window.6
  79.3 0.2 slice_reduce_fusion
  79.5 0.1 fusion.2
  79.6 0.1 reduce_sum.12
  79.8 0.0 copy-start.3
  79.8 0.7 copy.31.row_ref
  80.4 54.7 %reduce-scatter.2.cloned.1.call-done.attn_ref = bf16[128,4096]{1,0:T(8,128)(2,1)} async-done(((bf16[1024,4096]{1,0:T(8,128)(2,1)}), bf16[128,4096]{1,0:T(8,128)(2,1)}) %reduce-scatter.2.cloned.1.call-update) | async-done | bytes 1048592 | tf_op jit(solution)/shard_map/reduce_scatter | solution.py:319
  135.1 5.2 %norm_pack.1 = (bf16[128,4096]{1,0:T(8,128)(2,1)}, bf16[512,4096]{1,0:T(8,128)(2,1)}) custom-call(bf16[128,4096]{1,0:T(8,128)(2,1)} %hidden_ref.1, bf16[128,4096]{1,0:T(8,128)(2,1)} %reduce-scatter.2.cloned.1.call-done.attn_ref, bf16[1,4096]{1,0:T(2,128)(2,1)} %reshape.48.gain_ref, s32[2,128]{1,0:T(2,128)} %copy.31.row_ref), custom_call_target="tpu_custom_call" | custom-call | tf_op jit(solution)/shard_map/norm_pack/pallas_call | solution.py:104
  140.3 11.7 %all-to-all-start.1 = ((bf16[64,8,4096]{2,1,0:T(8,128)(2,1)}), bf16[64,8,4096]{2,1,0:T(8,128)(2,1)}, u32[]{:S(2)}, u32[]{:S(2)}) async-start(bf16[64,8,4096]{2,1,0:T(8,128)(2,1)} %bitcast.46), calls=%async_computation.2 | async-start | bytes 8388608 | tf_op jit(solution)/shard_map/all_to_all | solution.py:329
  152.0 0.0 collective-permute-done.gate2_hbm
  152.1 0.0 collective-permute-done.1.up2_hbm
  152.1 0.0 collective-permute-done.2.down2_hbm
  152.1 56.5 %all-to-all-done.1 = bf16[64,8,4096]{2,1,0:T(8,128)(2,1)} async-done(((bf16[64,8,4096]{2,1,0:T(8,128)(2,1)}), bf16[64,8,4096]{2,1,0:T(8,128)(2,1)}, u32[]{:S(2)}, u32[]{:S(2)}) %all-to-all-start.1) | async-done | bytes 4194336 | tf_op jit(solution)/shard_map/all_to_all | solution.py:329
  208.6 26.9 %whole_expert.1 = bf16[512,4096]{1,0:T(8,128)(2,1)} custom-call(bf16[512,4096]{1,0:T(8,128)(2,1)} %bitcast.6.x_hbm, bf16[4096,768]{1,0:T(8,128)(2,1)} %bitcast.40, bf16[4096,768]{1,0:T(8,128)(2,1)} %bitcast.42, bf16[768,4096]{1,0:T(8,128)(2,1)} %bitcast.44, bf16[4096,768]{1,0:T(8,128)(2,1)} %collective-permute-done.gate2_hbm, ...), custom_call_target="tpu_custom_call" | custom-call | tf_op jit(solution)/shard_map/whole_expert/pallas_call | solution.py:230
  235.5 0.0 copy-done.3
  235.5 0.0 copy-start.6
  235.5 0.0 copy-start.1
  235.5 10.9 %all-to-all-start.2 = ((bf16[64,8,4096]{2,1,0:T(8,128)(2,1)}), bf16[64,8,4096]{2,1,0:T(8,128)(2,1)}, u32[]{:S(2)}, u32[]{:S(2)}) async-start(bf16[64,8,4096]{2,1,0:T(8,128)(2,1)} %bitcast.38), calls=%async_computation.3 | async-start | bytes 8388608 | tf_op jit(solution)/shard_map/all_to_all | solution.py:329
  246.4 0.0 copy-done.6
  246.4 0.7 copy.32.weight_ref
  247.1 53.3 %all-to-all-done.2 = bf16[64,8,4096]{2,1,0:T(8,128)(2,1)} async-done(((bf16[64,8,4096]{2,1,0:T(8,128)(2,1)}), bf16[64,8,4096]{2,1,0:T(8,128)(2,1)}, u32[]{:S(2)}, u32[]{:S(2)}) %all-to-all-start.2) | async-done | bytes 4194336 | tf_op jit(solution)/shard_map/all_to_all | solution.py:329
  300.4 4.9 %combine.1 = bf16[128,4096]{1,0:T(8,128)(2,1)} custom-call(bf16[512,4096]{1,0:T(8,128)(2,1)} %bitcast.11.back_ref, s32[128,2]{1,0:T(8,128)} %copy-done.3, f32[128,2]{1,0:T(8,128)} %copy.32.weight_ref), custom_call_target="tpu_custom_call" | custom-call | tf_op jit(solution)/shard_map/combine/pallas_call | solution.py:131
  305.3 0.0 copy-done.1
  (6 shorter events, 0.1 us)
Async XLA Ops:
  7.2 10.8 %copy-start = (bf16[1024,2,256]{2,1,0:T(2,128)(2,1)S(1)}, bf16[1024,2,256]{2,1,0:T(2,128)(2,1)}, u32[]{:S(2)}) copy-start(bf16[1024,2,256]{2,1,0:T(2,128)(2,1)} %param.14) | copy-start | bytes 3145732
  7.2 59.2 %all-gather.3.cloned.1.call-start = ((), (), s32[]{:S(2)}) async-start(), calls=%async_computation.5 | async-start | bytes 4456448 | tf_op jit(solution)/shard_map/all_gather | solution.py:317
  9.8 24.7 %all-to-all-start = ((bf16[16,96,256]{2,1,0:T(8,128)(2,1)}), bf16[16,96,256]{2,1,0:T(8,128)(2,1)S(1)}, u32[]{:S(2)}, u32[]{:S(2)}) async-start(bf16[16,96,256]{2,1,0:T(8,128)(2,1)} %broadcast_in_dim.9), calls=%async_computation | async-start | bytes 1572864 | tf_op jit(solution)/shard_map/all_to_all | solution.py:310
  17.9 117.2 %reduce-scatter.2.cloned.1.call-start = ((), (), s32[]{:S(2)}) async-start(), calls=%async_computation.4 | async-start | bytes 9437184 | tf_op jit(solution)/shard_map/reduce_scatter | solution.py:319
  34.4 0.9 copy-start.2
  76.8 0.7 copy-start.5
  76.8 1.1 copy-start.4
  76.8 75.2 %collective-permute-start = (bf16[4096,768]{1,0:T(8,128)(2,1)}, bf16[4096,768]{1,0:T(8,128)(2,1)}, u32[]{:S(2)}, u32[]{:S(2)}) collective-permute-start(bf16[4096,768]{1,0:T(8,128)(2,1)} %bitcast.39), channel_id=1, source_target_pairs={{0,1},{1,0},{2,3},{3,2},{4,5},{5,4},{6,7},{7,6},{8,9},{9,8},{10,11... | collective-permute-start | bytes 18874376 | tf_op jit(solution)/shard_map/ppermute | solution.py:334
  76.9 75.2 %collective-permute-start.1 = (bf16[4096,768]{1,0:T(8,128)(2,1)}, bf16[4096,768]{1,0:T(8,128)(2,1)}, u32[]{:S(2)}, u32[]{:S(2)}) collective-permute-start(bf16[4096,768]{1,0:T(8,128)(2,1)} %bitcast.41), channel_id=1, source_target_pairs={{0,1},{1,0},{2,3},{3,2},{4,5},{5,4},{6,7},{7,6},{8,9},{9,8},{10,11... | collective-permute-start | bytes 18874376 | tf_op jit(solution)/shard_map/ppermute | solution.py:334
  77.4 74.7 %collective-permute-start.2 = (bf16[768,4096]{1,0:T(8,128)(2,1)}, bf16[768,4096]{1,0:T(8,128)(2,1)}, u32[]{:S(2)}, u32[]{:S(2)}) collective-permute-start(bf16[768,4096]{1,0:T(8,128)(2,1)} %bitcast.43), channel_id=1, source_target_pairs={{0,1},{1,0},{2,3},{3,2},{4,5},{5,4},{6,7},{7,6},{8,9},{9,8},{10,11... | collective-permute-start | bytes 18874376 | tf_op jit(solution)/shard_map/ppermute | solution.py:334
  79.8 155.7 %copy-start.3 = (s32[128,2]{1,0:T(8,128)}, s32[128,2]{1,0:T(8,128)S(1)}, u32[]{:S(2)}) copy-start(s32[128,2]{1,0:T(8,128)S(1)} %add.16.row_ref) | copy-start | bytes 3076
  140.3 68.2 %all-to-all-start.1 = ((bf16[64,8,4096]{2,1,0:T(8,128)(2,1)}), bf16[64,8,4096]{2,1,0:T(8,128)(2,1)}, u32[]{:S(2)}, u32[]{:S(2)}) async-start(bf16[64,8,4096]{2,1,0:T(8,128)(2,1)} %bitcast.46), calls=%async_computation.2 | async-start | bytes 8388608 | tf_op jit(solution)/shard_map/all_to_all | solution.py:329
  235.5 10.9 %copy-start.6 = (f32[128,2]{0,1:T(2,128)S(1)}, f32[128,2]{0,1:T(2,128)}, u32[]{:S(2)}) copy-start(f32[128,2]{0,1:T(2,128)} %param.20) | copy-start | bytes 3076
  235.5 69.9 %copy-start.1 = (bf16[1024,2,256]{2,1,0:T(2,128)(2,1)S(1)}, bf16[1024,2,256]{2,1,0:T(2,128)(2,1)}, u32[]{:S(2)}) copy-start(bf16[1024,2,256]{2,1,0:T(2,128)(2,1)} %param.14) | copy-start | bytes 3145732
  235.5 64.9 %all-to-all-start.2 = ((bf16[64,8,4096]{2,1,0:T(8,128)(2,1)}), bf16[64,8,4096]{2,1,0:T(8,128)(2,1)}, u32[]{:S(2)}, u32[]{:S(2)}) async-start(bf16[64,8,4096]{2,1,0:T(8,128)(2,1)} %bitcast.38), calls=%async_computation.3 | async-start | bytes 8388608 | tf_op jit(solution)/shard_map/all_to_all | solution.py:329
Sparse Core Ops, SparseCore 0:
  10.2 56.2 all-gather.2
  76.9 58.1 reduce-scatter.1

commit v3 on v2

--- a/solution.py
+++ b/solution.py
@@ -1,3 +1,4 @@
+import functools
 import math
 
 import jax
@@ -24,10 +25,13 @@
 
 masked_score = -1e30
 MIB = 1 << 20
-
-
-def attention_kernel(q_ref, prefix_ref, cand_ref, segment_col_ref, segment_row_ref, out_ref):
-    block = pl.program_id(0)
+EXPERT_MIB = 32
+
+
+def attention_kernel(
+    order_ref, q_ref, prefix_ref, cand_ref, segment_col_ref, segment_row_ref, out_ref
+):
+    block = order_ref[pl.program_id(0)]
     heads = q_ref.shape[1] // HEAD_SIZE
     factor = math.log2(math.e) / math.sqrt(HEAD_SIZE)
     start = pl.multiple_of(jnp.maximum(block - 1, 0) * BLOCK, BLOCK)
@@ -61,29 +65,49 @@
         out_ref[:, columns] = (total[:, :HEAD_SIZE] / total[:, HEAD_SIZE:]).astype(jnp.bfloat16)
 
 
-def attention(query, prefix, cand, segment):
+def attention(query, prefix, cand, segment, order):
     tokens, width = query.shape
     return pl.pallas_call(
         attention_kernel,
         out_shape=jax.ShapeDtypeStruct((tokens, width), jnp.bfloat16),
-        grid=(tokens // BLOCK,),
-        in_specs=[
-            pl.BlockSpec((BLOCK, width), lambda i: (i, 0)),
-            pl.BlockSpec(prefix.shape, lambda i: (0, 0)),
-            pl.BlockSpec(cand.shape, lambda i: (0, 0)),
-            pl.BlockSpec((BLOCK, 1), lambda i: (i, 0)),
-            pl.BlockSpec((1, tokens), lambda i: (0, 0)),
-        ],
-        out_specs=pl.BlockSpec((BLOCK, width), lambda i: (i, 0)),
-        compiler_params=pltpu.CompilerParams(vmem_limit_bytes=58 * MIB),
+        grid_spec=pltpu.PrefetchScalarGridSpec(
+            num_scalar_prefetch=1,
+            grid=(tokens // BLOCK,),
+            in_specs=[
+                pl.BlockSpec((BLOCK, width), lambda i, order: (order[i], 0)),
+                pl.BlockSpec(prefix.shape, lambda i, order: (0, 0)),
+                pl.BlockSpec(cand.shape, lambda i, order: (0, 0)),
+                pl.BlockSpec((BLOCK, 1), lambda i, order: (order[i], 0)),
+                pl.BlockSpec((1, tokens), lambda i, order: (0, 0)),
+            ],
+            out_specs=pl.BlockSpec((BLOCK, width), lambda i, order: (i, 0)),
+        ),
+        compiler_params=pltpu.CompilerParams(vmem_limit_bytes=24 * MIB),
         name="attention",
-    )(query, prefix, cand, segment.reshape(tokens, 1), segment.reshape(1, tokens))
-
-
-def norm_pack_kernel(hidden_ref, attn_ref, gain_ref, row_ref, attended_ref, packed_ref):
-    attended = (hidden_ref[...].astype(jnp.float32) + attn_ref[...].astype(jnp.float32)).astype(
-        jnp.bfloat16
+    )(order, query, prefix, cand, segment.reshape(tokens, 1), segment.reshape(1, tokens))
+
+
+def norm_pack_kernel(
+    hidden_ref,
+    keep_ref,
+    swap_ref,
+    left_up_ref,
+    right_up_ref,
+    left_down_ref,
+    right_down_ref,
+    gain_ref,
+    row_ref,
+    attended_ref,
+    packed_ref,
+):
+    def wide(ref):
+        return ref[...].astype(jnp.float32)
+
+    ringed = jnp.concatenate(
+        [wide(left_up_ref) + wide(left_down_ref), wide(right_up_ref) + wide(right_down_ref)],
+        axis=1,
     )
+    attended = (wide(hidden_ref) + (wide(keep_ref) + wide(swap_ref)) + ringed).astype(jnp.bfloat16)
     attended_ref[...] = attended
     widened = attended.astype(jnp.float32)
     mean_square = jnp.mean(widened * widened, axis=-1, keepdims=True)
@@ -98,7 +122,7 @@
     packed_ref[...] = jnp.dot(pick, normed, preferred_element_type=jnp.float32).astype(jnp.bfloat16)
 
 
-def norm_pack(hidden, attn, gain, rows):
+def norm_pack(hidden, parts, gain, rows):
     tokens, width = hidden.shape
     slots = 64 * CAP
     return pl.pallas_call(
@@ -107,9 +131,9 @@
             jax.ShapeDtypeStruct((tokens, width), jnp.bfloat16),
             jax.ShapeDtypeStruct((slots, width), jnp.bfloat16),
         ),
-        compiler_params=pltpu.CompilerParams(vmem_limit_bytes=58 * MIB),
+        compiler_params=pltpu.CompilerParams(vmem_limit_bytes=24 * MIB),
         name="norm_pack",
-    )(hidden, attn, gain.reshape(1, width), rows.T)
+    )(hidden, *parts, gain.reshape(1, width), rows.T)
 
 
 def combine_kernel(back_ref, row_ref, weight_ref, out_ref):
@@ -138,43 +162,37 @@
             pl.BlockSpec((tokens, TOP), lambda i: (0, 0)),
         ],
         out_specs=pl.BlockSpec((tokens, step), lambda i: (0, i)),
-        compiler_params=pltpu.CompilerParams(vmem_limit_bytes=58 * MIB),
+        compiler_params=pltpu.CompilerParams(vmem_limit_bytes=24 * MIB),
         name="combine",
     )(back, rows, weights)
 
 
 def expert_kernel(
-    x_hbm,
-    gate_hbm,
-    up_hbm,
+    x_ref,
+    gate_ref,
+    up_ref,
     down_hbm,
     gate2_hbm,
     up2_hbm,
     down2_hbm,
-    out_hbm,
-    x_ref,
-    gate_ref,
-    up_ref,
+    out_ref,
+    gate2_ref,
+    up2_ref,
     down_ref,
     act_ref,
-    out_ref,
-    x_sem,
     in_sem,
     down_sem,
-    out_sem,
 ):
-    hidden_units = gate_hbm.shape[1]
-    width = x_hbm.shape[1]
+    hidden_units = gate_ref.shape[1]
+    width = x_ref.shape[1]
     step, wide = 256, 1024
     per_half = hidden_units // step
 
     def first_copies(j):
-        half, at = j // per_half, pl.ds((j % per_half) * step, step)
-        to = pl.ds(j * step, step)
-        gate, up = ((gate_hbm, up_hbm), (gate2_hbm, up2_hbm))[half]
+        at = pl.ds(j * step, step)
         return (
-            pltpu.make_async_copy(gate.at[:, at], gate_ref.at[:, to], in_sem.at[0, j]),
-            pltpu.make_async_copy(up.at[:, at], up_ref.at[:, to], in_sem.at[1, j]),
+            pltpu.make_async_copy(gate2_hbm.at[:, at], gate2_ref.at[:, at], in_sem.at[0, j]),
+            pltpu.make_async_copy(up2_hbm.at[:, at], up2_ref.at[:, at], in_sem.at[1, j]),
         )
 
     def second_copies(j):
@@ -188,91 +206,123 @@
             for half, down in enumerate((down_hbm, down2_hbm))
         )
 
-    def out_copy(j):
-        at = pl.ds(j * wide, wide)
-        return pltpu.make_async_copy(out_ref.at[:, at], out_hbm.at[:, at], out_sem.at[j])
-
-    x_copy = pltpu.make_async_copy(x_hbm, x_ref, x_sem)
-    loads = [first_copies(j) for j in range(2 * per_half)]
+    loads = [()] * per_half + [first_copies(j) for j in range(per_half)]
     loads += [second_copies(j) for j in range(width // wide)]
-    ahead = 2
-    x_copy.start()
-    for copies in loads[:ahead]:
-        for copy in copies:
-            copy.start()
-    x_copy.wait()
+    ahead = 3
     for j, copies in enumerate(loads):
         for copy in loads[j + ahead] if j + ahead < len(loads) else ():
             copy.start()
         for copy in copies:
             copy.wait()
         if j < 2 * per_half:
-            at = slice(j * step, (j + 1) * step)
+            gate, up = (gate_ref, up_ref) if j < per_half else (gate2_ref, up2_ref)
+            at = slice((j % per_half) * step, (j % per_half + 1) * step)
             x = x_ref[...]
-            gated = jnp.dot(x, gate_ref[:, at], preferred_element_type=jnp.float32)
-            upward = jnp.dot(x, up_ref[:, at], preferred_element_type=jnp.float32)
-            act_ref[:, at] = (gated / (1.0 + jnp.exp(-gated)) * upward).astype(jnp.bfloat16)
+            gated = jnp.dot(x, gate[:, at], preferred_element_type=jnp.float32)
+            upward = jnp.dot(x, up[:, at], preferred_element_type=jnp.float32)
+            act_ref[:, j * step : (j + 1) * step] = (
+                gated / (1.0 + jnp.exp(-gated)) * upward
+            ).astype(jnp.bfloat16)
         else:
-            j -= 2 * per_half
-            at = slice(j * wide, (j + 1) * wide)
+            at = slice((j - 2 * per_half) * wide, (j - 2 * per_half + 1) * wide)
             out_ref[:, at] = jnp.dot(
                 act_ref[...], down_ref[:, at], preferred_element_type=jnp.float32
             ).astype(jnp.bfloat16)
-            out_copy(j).start()
-    for j in range(width // wide):
-        out_copy(j).wait()
 
 
 def whole_expert(rows, own, swapped):
     slots, width = rows.shape
-    both = 2 * own[0].shape[1]
+    units = own[0].shape[1]
     anywhere = pl.BlockSpec(memory_space=pl.ANY)
+    whole = pl.BlockSpec(memory_space=pltpu.VMEM)
     return pl.pallas_call(
         expert_kernel,
         out_shape=jax.ShapeDtypeStruct(rows.shape, jnp.bfloat16),
-        in_specs=[anywhere] * 7,
-        out_specs=anywhere,
+        in_specs=[whole] * 3 + [anywhere] * 4,
+        out_specs=whole,
         scratch_shapes=[
-            pltpu.VMEM((slots, width), jnp.bfloat16),
-            pltpu.VMEM((width, both), jnp.bfloat16),
-            pltpu.VMEM((width, both), jnp.bfloat16),
-            pltpu.VMEM((both, width), jnp.bfloat16),
-            pltpu.VMEM((slots, both), jnp.bfloat16),
-            pltpu.VMEM((slots, width), jnp.bfloat16),
-            pltpu.SemaphoreType.DMA,
-            pltpu.SemaphoreType.DMA((2, 6)),
+            pltpu.VMEM((width, units), jnp.bfloat16),
+            pltpu.VMEM((width, units), jnp.bfloat16),
+            pltpu.VMEM((2 * units, width), jnp.bfloat16),
+            pltpu.VMEM((slots, 2 * units), jnp.bfloat16),
+            pltpu.SemaphoreType.DMA((2, 3)),
             pltpu.SemaphoreType.DMA((2, 4)),
-            pltpu.SemaphoreType.DMA((4,)),
         ],
-        compiler_params=pltpu.CompilerParams(vmem_limit_bytes=58 * MIB),
+        compiler_params=pltpu.CompilerParams(vmem_limit_bytes=EXPERT_MIB * MIB),
         name="whole_expert",
     )(rows, *own, *swapped)
 
 
-def project_kernel(heads_ref, weight_ref, out_ref):
+def project_kernel(first, heads_ref, weight_ref, send_ref, keep_ref):
     wide = weight_ref.shape[2]
+    half = send_ref.shape[0]
+    heads = heads_ref[first : first + 2 * half, :]
     for piece in range(weight_ref.shape[0]):
-        out_ref[:, piece * wide : (piece + 1) * wide] = jnp.dot(
-            heads_ref[...], weight_ref[piece], preferred_element_type=jnp.float32
-        ).astype(jnp.bfloat16)
-
-
-def project(heads, weight):
-    tokens, width = heads.shape
+        at = slice(piece * wide, (piece + 1) * wide)
+        out = jnp.dot(heads, weight_ref[piece], preferred_element_type=jnp.float32).astype(
+            jnp.bfloat16
+        )
+        send_ref[:, at] = out[:half]
+        keep_ref[:, at] = out[half:]
+
+
+def project(heads, weight, tokens, first):
+    width = heads.shape[1]
     pieces, _, wide = weight.shape
-    step = 2
+    half = jax.ShapeDtypeStruct((tokens // 2, pieces * wide), jnp.bfloat16)
+    whole = pl.BlockSpec(memory_space=pltpu.VMEM)
     return pl.pallas_call(
-        project_kernel,
-        out_shape=jax.ShapeDtypeStruct((tokens, pieces * wide), jnp.bfloat16),
-        grid=(pieces // step,),
-        in_specs=[
-            pl.BlockSpec((tokens, width), lambda i: (0, 0)),
-            pl.BlockSpec((step, width, wide), lambda i: (i, 0, 0)),
-        ],
-        out_specs=pl.BlockSpec((tokens, step * wide), lambda i: (0, i)),
-        compiler_params=pltpu.CompilerParams(vmem_limit_bytes=58 * MIB),
+        functools.partial(project_kernel, first),
+        out_shape=(half, half),
+        in_specs=[whole, whole],
+        out_specs=(whole, whole),
+        compiler_params=pltpu.CompilerParams(vmem_limit_bytes=24 * MIB),
+        cost_estimate=pl.CostEstimate(
+            flops=2 * tokens * width * pieces * wide,
+            bytes_accessed=2 * (width + tokens) * pieces * wide,
+            transcendentals=0,
+        ),
         name="project",
     )(heads, weight)
+
+
+def added(*terms):
+    total = terms[0].astype(jnp.float32)
+    for term in terms[1:]:
+        total = total + term.astype(jnp.float32)
+    return total.astype(jnp.bfloat16)
+
+
+def reduce_over_experts(heads_out, wo_pieces):
+    mid = D // 2
+
+    def swapped(part):
+        return lax.ppermute(part, "core", SWAP)
+
+    def up(part):
+        return lax.ppermute(part, "x", [(i, (i + 1) % 4) for i in range(4)])
+
+    def down(part):
+        return lax.ppermute(part, "x", [(i, (i - 1) % 4) for i in range(4)])
+
+    far_send, far_keep = project(heads_out, wo_pieces, 2 * BLOCK, 4 * BLOCK)
+    far_send, heads_out = lax.optimization_barrier((far_send, heads_out))
+    far_swap = swapped(far_send)
+    next_send, next_keep = project(heads_out, wo_pieces, 4 * BLOCK, 0)
+    next_send, heads_out = lax.optimization_barrier((next_send, heads_out))
+    next_swap = swapped(next_send)
+    far_up = up(added(far_keep[:, :mid], far_swap[:, :mid]))
+    far_down = down(added(far_keep[:, mid:], far_swap[:, mid:]))
+    right_up = up(added(next_keep[:BLOCK, mid:], next_swap[:BLOCK, mid:]))
+    left_down = down(added(next_keep[BLOCK:, :mid], next_swap[BLOCK:, :mid]))
+    own_send, own_keep = project(heads_out, wo_pieces, 2 * BLOCK, 6 * BLOCK)
+    own_swap = swapped(own_send)
+    far_up, far_down, next_keep, next_swap = lax.optimization_barrier(
+        (far_up, far_down, next_keep, next_swap)
+    )
+    left_up = up(added(next_keep[:BLOCK, :mid], next_swap[:BLOCK, :mid], far_up))
+    right_down = down(added(next_keep[BLOCK:, mid:], next_swap[BLOCK:, mid:], far_down))
+    return own_keep, own_swap, left_up, right_up, left_down, right_down
 
 
 def slots_of(routes):
@@ -315,23 +365,39 @@
         tiled=True,
     ).reshape(-1, 2 * HEAD_SIZE)
     wo_pieces = lax.all_gather(o_weight, LIST, axis=0, tiled=False)
-    heads_out = attention(query, prefix, of_head(candidate_key_value), segment_ids[0])
-    attn = lax.psum_scatter(
-        project(heads_out, wo_pieces),
-        EXPERT,
-        scatter_dimension=0,
-        tiled=True,
-    )
+    at, core = lax.axis_index("x"), lax.axis_index("core")
+
+    def block_of(step, own):
+        return 2 * ((at + step) % 4) + (core if own else 1 - core)
+
+    order = jnp.stack(
+        [
+            block_of(step, own)
+            for step, own in (
+                (1, False),
+                (3, False),
+                (1, True),
+                (3, True),
+                (2, False),
+                (2, True),
+                (0, False),
+                (0, True),
+            )
+        ]
+    ).astype(jnp.int32)
+    heads_out = attention(query, prefix, of_head(candidate_key_value), segment_ids[0], order)
+    own = (w_gate[0], w_up[0], w_down[0])
+    swapped = tuple(lax.ppermute(w, "core", SWAP) for w in own)
+    heads_out, swapped = lax.optimization_barrier((heads_out, swapped))
+    parts = reduce_over_experts(heads_out, wo_pieces)
     rows = slots_of(routes)
-    attended, packed = norm_pack(hidden, attn, norm_gain, rows)
+    attended, packed = norm_pack(hidden, parts, norm_gain, rows)
 
     def across(slots):
         return lax.all_to_all(
             slots.reshape(64, CAP, D), CHIP, split_axis=0, concat_axis=0, tiled=True
         ).reshape(64 * CAP, D)
 
-    own = (w_gate[0], w_up[0], w_down[0])
-    swapped = tuple(lax.ppermute(w, "core", SWAP) for w in own)
     back = across(whole_expert(across(packed), own, swapped))
     return attended, combine(back, rows, route_weights)
 

time: 313 us -> 283 us (0.904)
  waiting for transfers between devices: 195 us -> 123 us
  blocking collectives: 0 us -> 57.4 us
  Pallas kernels: 62.3 us -> 49.6 us
  starting transfers between devices: 31.5 us -> 22 us
  other arithmetic: 0.78 us -> 4.2 us
  local copies, waits for them, and re-layouts: 8.54 us -> 11.9 us
    all_to_all x0 -> x1, blocking collectives: none -> 57.4 us  [across(): lax.all_to_all(slots.reshape(64, CAP, D), CHIP, split_axis=0, concat_axis...]
    all_to_all x2 -> x1, waiting for transfers between devices: 110 us -> 52.9 us  [across(): lax.all_to_all(slots.reshape(64, CAP, D), CHIP, split_axis=0, concat_axis...]
    reduce_scatter x1 -> x0, waiting for transfers between devices: 54.7 us -> none  [local(): lax.psum_scatter(project(heads_out, wo_pieces), EXPERT, scatter_dimension...]
    ppermute x0 -> x9, waiting for transfers between devices: none -> 36.5 us  [the longest x3 24.9 us: down(): return lax.ppermute(part, 'x', [(i, (i - 1) % 4) for i in range(4)])]
    all_to_all x2 -> x1, starting transfers between devices: 22.6 us -> 5.79 us  [across(): lax.all_to_all(slots.reshape(64, CAP, D), CHIP, split_axis=0, concat_axis...]
    ppermute x0 -> x9, starting transfers between devices: none -> 7.4 us  [the longest x3 4.54 us: down(): return lax.ppermute(part, 'x', [(i, (i - 1) % 4) for i in range(4)])]
    unnamed x18 -> x30, local copies, waits for them, and re-layouts: 2.66 us -> 8.58 us
    pallas_call x1, Pallas kernels: 26.9 us -> 21.1 us  [whole_expert(): pl.pallas_call(expert_kernel, out_shape=jax.ShapeDtypeStruct(rows.shape,...]
  transfers between devices with their start and end apart: 8 -> 15, of which waited for: 5 -> 10; matrix products, arithmetic and copies ran while one was open for 3% -> 3% of each run, Pallas kernels for 6% -> 6%
where the time goes in v3:
time: 283 us; the launch traced here: 282 us
  waiting for transfers between devices  123 us (43%)
  blocking collectives  57.4 us (20%)
  Pallas kernels  49.6 us (18%)
  starting transfers between devices  22 us (8%)
  between operations  14.3 us (5%)
  local copies, waits for them, and re-layouts  11.9 us (4%)
  other arithmetic  4.2 us (1%)
    all_to_all x1, blocking collectives, across(): lax.all_to_all(slots.reshape(64, CAP, D), CHIP, split_axis=0, concat_axis...  57.4 us
    all_to_all x1, waiting for transfers between devices, across(): lax.all_to_all(slots.reshape(64, CAP, D), CHIP, split_axis=0, concat_axis...  52.9 us
    ppermute x3, waiting for transfers between devices, down(): return lax.ppermute(part, 'x', [(i, (i - 1) % 4) for i in range(4)])  24.9 us
    pallas_call x1, Pallas kernels, whole_expert(): pl.pallas_call(expert_kernel, out_shape=jax.ShapeDtypeStruct(rows.shape,...  21.1 us
    all_to_all x1, waiting for transfers between devices, local(): lax.all_to_all(jnp.broadcast_to(own_prefix[None], (n_list,) + own_prefix....  16.9 us
    all_gather x1, waiting for transfers between devices, local(): wo_pieces = lax.all_gather(o_weight, LIST, axis=0, tiled=False)  15.5 us
    pallas_call x1, Pallas kernels, attention(): pl.pallas_call(attention_kernel, out_shape=jax.ShapeDtypeStruct((tokens,...  13.8 us
    unnamed x30, local copies, waits for them, and re-layouts  8.58 us
  transfers between devices with their start and end apart: 15, of which 10 were waited for; matrix products, arithmetic and copies ran while one was open for 3% of the time, Pallas kernels for 6%

profile of v3, /device:TPU:0, one launch (start us, length us, event | category | flops | bytes accessed | tf_op | source)
XLA Modules:
  0.0 282.0 jit_solution(15468046320963042790)
XLA Ops:
  7.2 0.0 copy-start
  7.2 0.0 all-gather.3.cloned.1.call-start
  7.2 0.7 all-gather.3.cloned.1.call-update
  7.9 0.1 collective-permute-start
  8.0 0.5 collective-permute-start.1
  8.5 0.1 collective-permute-start.2
  8.6 0.8 constant_dynamic-slice_fusion.1
  9.5 1.0 broadcast_in_dim.9
  10.4 8.1 %all-to-all-start = ((bf16[16,96,256]{2,1,0:T(8,128)(2,1)}), bf16[16,96,256]{2,1,0:T(8,128)(2,1)S(1)}, u32[]{:S(2)}, u32[]{:S(2)}) async-start(bf16[16,96,256]{2,1,0:T(8,128)(2,1)} %broadcast_in_dim.9), calls=%async_computation | async-start | bytes 1572864 | tf_op jit(solution)/shard_map/all_to_all | solution.py:360
  18.6 0.4 constant_dynamic-slice_fusion
  19.0 0.1 copy.39
  19.1 0.2 copy.26.segment_col_ref
  19.3 0.1 stack.35.order_ref
  19.4 16.9 %all-to-all-done = bf16[16,96,256]{2,1,0:T(8,128)(2,1)S(1)} async-done(((bf16[16,96,256]{2,1,0:T(8,128)(2,1)}), bf16[16,96,256]{2,1,0:T(8,128)(2,1)S(1)}, u32[]{:S(2)}, u32[]{:S(2)}) %all-to-all-start) | async-done | bytes 786464 | tf_op jit(solution)/shard_map/all_to_all | solution.py:360
  36.3 1.2 copy-done.5
  37.5 13.8 %attention.1.heads_ref = bf16[1024,512]{1,0:T(8,128)(2,1)S(1)} custom-call(s32[8]{0:T(128)S(1)} %stack.35.order_ref, bf16[1024,512]{1,0:T(8,128)(2,1)S(1)} %copy-done.5, bf16[1536,256]{1,0:T(8,128)(2,1)S(1)} %bitcast.58, bf16[1024,256]{1,0:T(8,128)(2,1)S(1)} %bitcast.59, s32[1024,1]{1,0:T(8,128)S(1)} %copy.26.segment_col_ref, s32[1,1024]{1,0:T(1,128)S(1)} %copy-done.7), custom_call_target="tpu_custom_call" | custom-call | tf_op jit(solution)/shard_map/attention/pallas_call | solution.py:70
  51.3 0.0 collective-permute-done.gate2_hbm
  51.4 0.0 collective-permute-done.1.up2_hbm
  51.4 0.0 collective-permute-done.2.down2_hbm
  51.4 15.5 %all-gather.3.cloned.1.call-done = bf16[8192,256]{1,0:T(8,128)(2,1)} async-done(((bf16[512,256]{1,0:T(8,128)(2,1)}), bf16[8192,256]{1,0:T(8,128)(2,1)}) %all-gather.3.cloned.1.call-update) | async-done | bytes 4194320 | tf_op jit(solution)/shard_map/all_gather | solution.py:367
  66.9 2.2 copy-done.2
  69.1 1.3 project.3
  70.4 2.3 project.4
  72.7 0.1 collective-permute-start.7
  72.8 0.5 collective-permute-start.4
  73.3 5.1 %collective-permute-done.4 = bf16[128,4096]{1,0:T(8,128)(2,1)S(1)} collective-permute-done((bf16[128,4096]{1,0:T(8,128)(2,1)S(1)}, bf16[128,4096]{1,0:T(8,128)(2,1)S(1)}, u32[]{:S(2)}, u32[]{:S(2)}) %collective-permute-start.4) | collective-permute-done | bytes 1048608 | tf_op jit(solution)/shard_map/ppermute | solution.py:300
  78.5 0.5 add_convert_fusion.4
  78.9 2.8 collective-permute-start.6
  81.7 2.2 project.5
  83.9 0.0 collective-permute-start.3
  83.9 9.3 %collective-permute-done.6 = bf16[128,2048]{1,0:T(8,128)(2,1)S(1)} collective-permute-done((bf16[128,2048]{1,0:T(8,128)(2,1)S(1)}, bf16[128,2048]{1,0:T(8,128)(2,1)S(1)}, u32[]{:S(2)}, u32[]{:S(2)}) %collective-permute-start.6) | collective-permute-done | bytes 524320 | tf_op jit(solution)/shard_map/ppermute | solution.py:306
  93.2 3.4 %collective-permute-done.5 = bf16[128,2048]{1,0:T(8,128)(2,1)S(1)} collective-permute-done((bf16[128,2048]{1,0:T(8,128)(2,1)S(1)}, bf16[128,2048]{1,0:T(8,128)(2,1)S(1)}, u32[]{:S(2)}, u32[]{:S(2)}) %collective-permute-start.5) | collective-permute-done | bytes 524320 | tf_op jit(solution)/shard_map/ppermute | solution.py:303
  96.6 0.0 collective-permute-done.7
  96.6 1.6 add_convert_fusion
  98.2 0.3 collective-permute-start.11
  98.4 1.7 collective-permute-start.8
  100.2 1.4 add_convert_fusion.1
  101.6 1.5 collective-permute-start.10
  103.1 0.5 collective-permute-start.9
  103.6 0.1 copy.27
  103.7 0.1 eq.38
  103.9 0.1 eq.34
  104.0 0.1 copy.30
  104.2 0.6 reduce-window.6
  104.8 0.2 slice_reduce_fusion
  105.0 0.1 fusion.2
  105.1 0.1 reduce_sum.12
  105.3 0.1 copy.31.row_ref
  105.3 0.0 collective-permute-done.3.swap_ref
  105.4 8.0 %collective-permute-done.11.right_down_ref = bf16[128,2048]{1,0:T(8,128)(2,1)} collective-permute-done((bf16[128,2048]{1,0:T(8,128)(2,1)}, bf16[128,2048]{1,0:T(8,128)(2,1)}, u32[]{:S(2)}, u32[]{:S(2)}) %collective-permute-start.11) | collective-permute-done | bytes 524320 | tf_op jit(solution)/shard_map/ppermute | solution.py:306
  113.3 1.5 collective-permute-done.8.left_up_ref
  114.8 7.7 %collective-permute-done.10.left_down_ref = bf16[128,2048]{1,0:T(8,128)(2,1)} collective-permute-done((bf16[128,2048]{1,0:T(8,128)(2,1)}, bf16[128,2048]{1,0:T(8,128)(2,1)}, u32[]{:S(2)}, u32[]{:S(2)}) %collective-permute-start.10) | collective-permute-done | bytes 524320 | tf_op jit(solution)/shard_map/ppermute | solution.py:306
  122.5 1.5 collective-permute-done.9.right_up_ref
  124.1 3.9 %norm_pack.1 = (bf16[128,4096]{1,0:T(8,128)(2,1)}, bf16[512,4096]{1,0:T(8,128)(2,1)S(1)}) custom-call(bf16[128,4096]{1,0:T(8,128)(2,1)S(1)} %copy-done.6, bf16[128,4096]{1,0:T(8,128)(2,1)S(1)} %get-tuple-element.27.keep_ref, bf16[128,4096]{1,0:T(8,128)(2,1)S(1)} %collective-permute-done.3.swap_ref, bf16[128,2048]{1,0:T(8,128)(2,1)} %collective-permute-done.8.left_up_ref, ...), custom_call_target="tpu_custom_call" | custom-call | tf_op jit(solution)/shard_map/norm_pack/pallas_call | solution.py:128
  128.0 0.0 slice-start.1
  128.0 57.4 %all_to_all.15 = bf16[64,8,4096]{2,1,0:T(8,128)(2,1)S(1)} all-to-all(bf16[64,8,4096]{2,1,0:T(8,128)(2,1)S(1)} %bitcast.57), channel_id=1, replica_groups=mesh['y'=4,'z'=4,'x'=4,'core'=2] {'y','z','x'}, dimensions={0} | all-to-all | bytes 8388608 | tf_op jit(solution)/shard_map/all_to_all | solution.py:397
  185.4 2.8 copy-done.4
  188.2 21.1 %whole_expert.1 = bf16[512,4096]{1,0:T(8,128)(2,1)S(1)} custom-call(bf16[512,4096]{1,0:T(8,128)(2,1)S(1)} %bitcast.50, bf16[4096,768]{1,0:T(8,128)(2,1)S(1)} %bitcast.54, bf16[4096,768]{1,0:T(8,128)(2,1)S(1)} %bitcast.56, bf16[768,4096]{1,0:T(8,128)(2,1)} %bitcast.63, bf16[4096,768]{1,0:T(8,128)(2,1)} %collective-permute-done.gate2_hbm, ...), custom_call_target="tpu_custom_call" | custom-call | tf_op jit(solution)/shard_map/whole_expert/pallas_call | solution.py:238
  209.3 2.0 copy-done.3
  211.3 5.8 %all-to-all-start.2 = ((bf16[64,8,4096]{2,1,0:T(8,128)(2,1)}), bf16[64,8,4096]{2,1,0:T(8,128)(2,1)}, u32[]{:S(2)}, u32[]{:S(2)}) async-start(bf16[64,8,4096]{2,1,0:T(8,128)(2,1)} %bitcast.49), calls=%async_computation.2 | async-start | bytes 8388608 | tf_op jit(solution)/shard_map/all_to_all | solution.py:397
  217.1 0.0 copy-start.1
  217.2 0.1 copy.32.weight_ref
  217.3 52.9 %all-to-all-done.2 = bf16[64,8,4096]{2,1,0:T(8,128)(2,1)} async-done(((bf16[64,8,4096]{2,1,0:T(8,128)(2,1)}), bf16[64,8,4096]{2,1,0:T(8,128)(2,1)}, u32[]{:S(2)}, u32[]{:S(2)}) %all-to-all-start.2) | async-done | bytes 4194336 | tf_op jit(solution)/shard_map/all_to_all | solution.py:397
  270.2 4.9 %combine.1 = bf16[128,4096]{1,0:T(8,128)(2,1)} custom-call(bf16[512,4096]{1,0:T(8,128)(2,1)} %bitcast.19.back_ref, s32[128,2]{1,0:T(8,128)S(1)} %add.114.row_ref, f32[128,2]{1,0:T(8,128)S(1)} %copy.32.weight_ref), custom_call_target="tpu_custom_call" | custom-call | tf_op jit(solution)/shard_map/combine/pallas_call | solution.py:155
  (28 shorter events, 0.1 us)
Async XLA Ops:
  7.2 11.5 %copy-start = (bf16[1024,2,256]{2,1,0:T(2,128)(2,1)S(1)}, bf16[1024,2,256]{2,1,0:T(2,128)(2,1)}, u32[]{:S(2)}) copy-start(bf16[1024,2,256]{2,1,0:T(2,128)(2,1)} %param.14) | copy-start | bytes 3145732
  7.2 11.9 %copy-start.7 = (s32[1,1024]{1,0:T(1,128)S(1)}, s32[1,1024]{1,0:T(1,128)}, u32[]{:S(2)}) copy-start(s32[1,1024]{1,0:T(1,128)} %segment_row_ref.1) | copy-start | bytes 12292
  7.2 59.7 %all-gather.3.cloned.1.call-start = ((), (), s32[]{:S(2)}) async-start(), calls=%async_computation.3 | async-start | bytes 4456448 | tf_op jit(solution)/shard_map/all_gather | solution.py:367
  7.9 43.4 %collective-permute-start = (bf16[4096,768]{1,0:T(8,128)(2,1)}, bf16[4096,768]{1,0:T(8,128)(2,1)}, u32[]{:S(2)}, u32[]{:S(2)}) collective-permute-start(bf16[4096,768]{1,0:T(8,128)(2,1)} %bitcast.51), channel_id=1, source_target_pairs={{0,1},{1,0},{2,3},{3,2},{4,5},{5,4},{6,7},{7,6},{8,9},{9,8},{10,11... | collective-permute-start | bytes 18874376 | tf_op jit(solution)/shard_map/ppermute | solution.py:390
  8.0 43.3 %collective-permute-start.1 = (bf16[4096,768]{1,0:T(8,128)(2,1)}, bf16[4096,768]{1,0:T(8,128)(2,1)}, u32[]{:S(2)}, u32[]{:S(2)}) collective-permute-start(bf16[4096,768]{1,0:T(8,128)(2,1)} %bitcast.55), channel_id=1, source_target_pairs={{0,1},{1,0},{2,3},{3,2},{4,5},{5,4},{6,7},{7,6},{8,9},{9,8},{10,11... | collective-permute-start | bytes 18874376 | tf_op jit(solution)/shard_map/ppermute | solution.py:390
  8.5 42.9 %collective-permute-start.2 = (bf16[768,4096]{1,0:T(8,128)(2,1)}, bf16[768,4096]{1,0:T(8,128)(2,1)}, u32[]{:S(2)}, u32[]{:S(2)}) collective-permute-start(bf16[768,4096]{1,0:T(8,128)(2,1)} %bitcast.62), channel_id=1, source_target_pairs={{0,1},{1,0},{2,3},{3,2},{4,5},{5,4},{6,7},{7,6},{8,9},{9,8},{10,11... | collective-permute-start | bytes 18874376 | tf_op jit(solution)/shard_map/ppermute | solution.py:390
  10.4 25.9 %all-to-all-start = ((bf16[16,96,256]{2,1,0:T(8,128)(2,1)}), bf16[16,96,256]{2,1,0:T(8,128)(2,1)S(1)}, u32[]{:S(2)}, u32[]{:S(2)}) async-start(bf16[16,96,256]{2,1,0:T(8,128)(2,1)} %broadcast_in_dim.9), calls=%async_computation | async-start | bytes 1572864 | tf_op jit(solution)/shard_map/all_to_all | solution.py:360
  36.3 1.2 copy-start.5
  66.9 2.2 copy-start.2
  72.7 23.9 %collective-permute-start.7 = (bf16[256,4096]{1,0:T(8,128)(2,1)S(1)}, bf16[256,4096]{1,0:T(8,128)(2,1)S(1)}, u32[]{:S(2)}, u32[]{:S(2)}) collective-permute-start(bf16[256,4096]{1,0:T(8,128)(2,1)S(1)} %get-tuple-element.32), channel_id=1, source_target_pairs={{0,1},{1,0},{2,3},{3,2},{4,5},{5,4},{6,7},{7,6},{8,9},{9,8},{10,11... | collective-permute-start | bytes 6291464 | tf_op jit(solution)/shard_map/ppermute | solution.py:300
  72.8 5.6 %collective-permute-start.4 = (bf16[128,4096]{1,0:T(8,128)(2,1)S(1)}, bf16[128,4096]{1,0:T(8,128)(2,1)S(1)}, u32[]{:S(2)}, u32[]{:S(2)}) collective-permute-start(bf16[128,4096]{1,0:T(8,128)(2,1)S(1)} %get-tuple-element.30), channel_id=1, source_target_pairs={{0,1},{1,0},{2,3},{3,2},{4,5},{5,4},{6,7},{7,6},{8,9},{9,8},{10,11... | collective-permute-start | bytes 3145736 | tf_op jit(solution)/shard_map/ppermute | solution.py:300
  78.9 14.2 %collective-permute-start.6 = (bf16[128,2048]{1,0:T(8,128)(2,1)S(1)}, bf16[128,2048]{1,0:T(8,128)(2,1)S(1)}, u32[]{:S(2)}, u32[]{:S(2)}) collective-permute-start(bf16[128,2048]{1,0:T(8,128)(2,1)S(1)} %get-tuple-element.46), channel_id=1, source_target_pairs={{0,6},{2,0},{4,2},{6,4},{1,7},{3,1},{5,3},{7,5},{8,14},{10,8},{12,... | collective-permute-start | bytes 1572872 | tf_op jit(solution)/shard_map/ppermute | solution.py:306
  81.7 14.9 %collective-permute-start.5 = (bf16[128,2048]{1,0:T(8,128)(2,1)S(1)}, bf16[128,2048]{1,0:T(8,128)(2,1)S(1)}, u32[]{:S(2)}, u32[]{:S(2)}) collective-permute-start(bf16[128,2048]{1,0:T(8,128)(2,1)S(1)} %get-tuple-element.47), channel_id=1, source_target_pairs={{0,2},{2,4},{4,6},{6,0},{1,3},{3,5},{5,7},{7,1},{8,10},{10,12},{12... | collective-permute-start | bytes 1572872 | tf_op jit(solution)/shard_map/ppermute | solution.py:303
  83.9 19.7 %copy-start.9 = (s32[128,2]{0,1:T(2,128)S(1)}, s32[128,2]{0,1:T(2,128)}, u32[]{:S(2)}) copy-start(s32[128,2]{0,1:T(2,128)} %param.19) | copy-start | bytes 3076
  83.9 20.1 %copy-start.8 = (bf16[4096]{0:T(1024)(128)(2,1)S(1)}, bf16[4096]{0:T(1024)(128)(2,1)}, u32[]{:S(2)}) copy-start(bf16[4096]{0:T(1024)(128)(2,1)} %param.18) | copy-start | bytes 24580
  83.9 40.2 %copy-start.6 = (bf16[128,4096]{1,0:T(8,128)(2,1)S(1)}, bf16[128,4096]{1,0:T(8,128)(2,1)}, u32[]{:S(2)}) copy-start(bf16[128,4096]{1,0:T(8,128)(2,1)} %hidden_ref.1) | copy-start | bytes 3145732
  83.9 21.5 %collective-permute-start.3 = (bf16[128,4096]{1,0:T(8,128)(2,1)}, bf16[128,4096]{1,0:T(8,128)(2,1)S(1)}, u32[]{:S(2)}, u32[]{:S(2)}) collective-permute-start(bf16[128,4096]{1,0:T(8,128)(2,1)} %get-tuple-element.28), channel_id=1, source_target_pairs={{0,1},{1,0},{2,3},{3,2},{4,5},{5,4},{6,7},{7,6},{8,9},{9,8},{10,11... | collective-permute-start | bytes 3145736 | tf_op jit(solution)/shard_map/ppermute | solution.py:300
  98.2 15.2 %collective-permute-start.11 = (bf16[128,2048]{1,0:T(8,128)(2,1)}, bf16[128,2048]{1,0:T(8,128)(2,1)}, u32[]{:S(2)}, u32[]{:S(2)}) collective-permute-start(bf16[128,2048]{1,0:T(8,128)(2,1)} %get-tuple-element.42), channel_id=1, source_target_pairs={{0,6},{2,0},{4,2},{6,4},{1,7},{3,1},{5,3},{7,5},{8,14},{10,8},{12,... | collective-permute-start | bytes 1572872 | tf_op jit(solution)/shard_map/ppermute | solution.py:306
  98.4 16.4 %collective-permute-start.8 = (bf16[128,2048]{1,0:T(8,128)(2,1)}, bf16[128,2048]{1,0:T(8,128)(2,1)}, u32[]{:S(2)}, u32[]{:S(2)}) collective-permute-start(bf16[128,2048]{1,0:T(8,128)(2,1)} %get-tuple-element.43), channel_id=1, source_target_pairs={{0,2},{2,4},{4,6},{6,0},{1,3},{3,5},{5,7},{7,1},{8,10},{10,12},{12... | collective-permute-start | bytes 1572872 | tf_op jit(solution)/shard_map/ppermute | solution.py:303
  101.6 20.9 %collective-permute-start.10 = (bf16[128,2048]{1,0:T(8,128)(2,1)}, bf16[128,2048]{1,0:T(8,128)(2,1)}, u32[]{:S(2)}, u32[]{:S(2)}) collective-permute-start(bf16[128,2048]{1,0:T(8,128)(2,1)} %get-tuple-element.44), channel_id=1, source_target_pairs={{0,6},{2,0},{4,2},{6,4},{1,7},{3,1},{5,3},{7,5},{8,14},{10,8},{12,... | collective-permute-start | bytes 1572872 | tf_op jit(solution)/shard_map/ppermute | solution.py:306
  103.1 21.0 %collective-permute-start.9 = (bf16[128,2048]{1,0:T(8,128)(2,1)}, bf16[128,2048]{1,0:T(8,128)(2,1)}, u32[]{:S(2)}, u32[]{:S(2)}) collective-permute-start(bf16[128,2048]{1,0:T(8,128)(2,1)} %get-tuple-element.45), channel_id=1, source_target_pairs={{0,2},{2,4},{4,6},{6,0},{1,3},{3,5},{5,7},{7,1},{8,10},{10,12},{12... | collective-permute-start | bytes 1572872 | tf_op jit(solution)/shard_map/ppermute | solution.py:303
  124.1 61.3 %slice-start = ((s8[6291456]{0:T(1024)(128)(4,1)}), s8[4194304]{0:T(1024)(128)(4,1)S(1)}, s32[]{:S(2)}) async-start(s8[6291456]{0:T(1024)(128)(4,1)} %bitcast.52), calls=%async_computation.4 | async-start | bytes 8388608
  128.0 57.4 %slice-start.1 = ((s8[6291456]{0:T(1024)(128)(4,1)}), s8[2097152]{0:T(1024)(128)(4,1)S(1)}, s32[]{:S(2)}) async-start(s8[6291456]{0:T(1024)(128)(4,1)} %bitcast.52), calls=%async_computation.5 | async-start | bytes 4194304
  185.4 2.8 copy-start.4
  209.3 2.0 copy-start.3
  211.3 5.8 %copy-start.10 = (f32[128,2]{0,1:T(2,128)S(1)}, f32[128,2]{0,1:T(2,128)}, u32[]{:S(2)}) copy-start(f32[128,2]{0,1:T(2,128)} %param.20) | copy-start | bytes 3076
  211.3 58.8 %all-to-all-start.2 = ((bf16[64,8,4096]{2,1,0:T(8,128)(2,1)}), bf16[64,8,4096]{2,1,0:T(8,128)(2,1)}, u32[]{:S(2)}, u32[]{:S(2)}) async-start(bf16[64,8,4096]{2,1,0:T(8,128)(2,1)} %bitcast.49), calls=%async_computation.2 | async-start | bytes 8388608 | tf_op jit(solution)/shard_map/all_to_all | solution.py:397
  217.1 58.0 %copy-start.1 = (bf16[1024,2,256]{2,1,0:T(2,128)(2,1)S(1)}, bf16[1024,2,256]{2,1,0:T(2,128)(2,1)}, u32[]{:S(2)}) copy-start(bf16[1024,2,256]{2,1,0:T(2,128)(2,1)} %param.14) | copy-start | bytes 3145732
Sparse Core Ops, SparseCore 0:
  10.2 56.7 all-gather.2

commit v4 on v3

--- a/solution.py
+++ b/solution.py
@@ -25,7 +25,8 @@
 
 masked_score = -1e30
 MIB = 1 << 20
-EXPERT_MIB = 32
+EXPERT_MIB = 38
+NEAR_FLOPS = 10**10
 
 
 def attention_kernel(
@@ -87,27 +88,46 @@
     )(order, query, prefix, cand, segment.reshape(tokens, 1), segment.reshape(1, tokens))
 
 
+def near_sum_kernel(hidden_ref, keep_ref, swap_ref, left_down_ref, right_up_ref, out_ref):
+    mid = left_down_ref.shape[1]
+    for at, near in ((slice(0, mid), left_down_ref), (slice(mid, 2 * mid), right_up_ref)):
+        own = keep_ref[:, at].astype(jnp.float32) + swap_ref[:, at].astype(jnp.float32)
+        out_ref[:, at] = (hidden_ref[:, at].astype(jnp.float32) + own) + near[...].astype(
+            jnp.float32
+        )
+
+
+def near_sum(hidden, keep, swap, left_down, right_up):
+    whole = pl.BlockSpec(memory_space=pltpu.VMEM)
+    return pl.pallas_call(
+        near_sum_kernel,
+        out_shape=jax.ShapeDtypeStruct(hidden.shape, jnp.float32),
+        in_specs=[whole] * 5,
+        out_specs=whole,
+        compiler_params=pltpu.CompilerParams(vmem_limit_bytes=24 * MIB),
+        cost_estimate=pl.CostEstimate(
+            flops=NEAR_FLOPS, bytes_accessed=8 * MIB, transcendentals=0
+        ),
+        name="near_sum",
+    )(hidden, keep, swap, left_down, right_up)
+
+
 def norm_pack_kernel(
-    hidden_ref,
-    keep_ref,
-    swap_ref,
+    near_ref,
     left_up_ref,
-    right_up_ref,
-    left_down_ref,
     right_down_ref,
     gain_ref,
     row_ref,
+    weight_ref,
     attended_ref,
     packed_ref,
+    weight_out_ref,
 ):
-    def wide(ref):
-        return ref[...].astype(jnp.float32)
-
+    weight_out_ref[...] = weight_ref[...]
     ringed = jnp.concatenate(
-        [wide(left_up_ref) + wide(left_down_ref), wide(right_up_ref) + wide(right_down_ref)],
-        axis=1,
-    )
-    attended = (wide(hidden_ref) + (wide(keep_ref) + wide(swap_ref)) + ringed).astype(jnp.bfloat16)
+        [left_up_ref[...].astype(jnp.float32), right_down_ref[...].astype(jnp.float32)], axis=1
+    )
+    attended = (near_ref[...] + ringed).astype(jnp.bfloat16)
     attended_ref[...] = attended
     widened = attended.astype(jnp.float32)
     mean_square = jnp.mean(widened * widened, axis=-1, keepdims=True)
@@ -122,18 +142,22 @@
     packed_ref[...] = jnp.dot(pick, normed, preferred_element_type=jnp.float32).astype(jnp.bfloat16)
 
 
-def norm_pack(hidden, parts, gain, rows):
-    tokens, width = hidden.shape
+def norm_pack(near, left_up, right_down, gain, rows, weights):
+    tokens, width = near.shape
     slots = 64 * CAP
+    whole = pl.BlockSpec(memory_space=pltpu.VMEM)
     return pl.pallas_call(
         norm_pack_kernel,
         out_shape=(
             jax.ShapeDtypeStruct((tokens, width), jnp.bfloat16),
             jax.ShapeDtypeStruct((slots, width), jnp.bfloat16),
+            jax.ShapeDtypeStruct(weights.shape, jnp.float32),
         ),
+        in_specs=[whole] * 6,
+        out_specs=(whole, whole, whole),
         compiler_params=pltpu.CompilerParams(vmem_limit_bytes=24 * MIB),
         name="norm_pack",
-    )(hidden, *parts, gain.reshape(1, width), rows.T)
+    )(near, left_up, right_down, gain.reshape(1, width), rows.T, weights)
 
 
 def combine_kernel(back_ref, row_ref, weight_ref, out_ref):
@@ -149,19 +173,12 @@
 
 
 def combine(back, rows, weights):
-    slots, width = back.shape
-    tokens = rows.shape[0]
-    step = 1024
+    whole = pl.BlockSpec(memory_space=pltpu.VMEM)
     return pl.pallas_call(
         combine_kernel,
-        out_shape=jax.ShapeDtypeStruct((tokens, width), jnp.bfloat16),
-        grid=(width // step,),
-        in_specs=[
-            pl.BlockSpec((slots, step), lambda i: (0, i)),
-            pl.BlockSpec((tokens, TOP), lambda i: (0, 0)),
-            pl.BlockSpec((tokens, TOP), lambda i: (0, 0)),
-        ],
-        out_specs=pl.BlockSpec((tokens, step), lambda i: (0, i)),
+        out_shape=jax.ShapeDtypeStruct((rows.shape[0], back.shape[1]), jnp.bfloat16),
+        in_specs=[whole] * 3,
+        out_specs=whole,
         compiler_params=pltpu.CompilerParams(vmem_limit_bytes=24 * MIB),
         name="combine",
     )(back, rows, weights)
@@ -170,12 +187,13 @@
 def expert_kernel(
     x_ref,
     gate_ref,
-    up_ref,
+    up_hbm,
     down_hbm,
     gate2_hbm,
     up2_hbm,
     down2_hbm,
     out_ref,
+    up_ref,
     gate2_ref,
     up2_ref,
     down_ref,
@@ -188,6 +206,10 @@
     step, wide = 256, 1024
     per_half = hidden_units // step
 
+    def own_copies(j):
+        at = pl.ds(j * step, step)
+        return (pltpu.make_async_copy(up_hbm.at[:, at], up_ref.at[:, at], in_sem.at[2, j]),)
+
     def first_copies(j):
         at = pl.ds(j * step, step)
         return (
@@ -206,19 +228,27 @@
             for half, down in enumerate((down_hbm, down2_hbm))
         )
 
-    loads = [()] * per_half + [first_copies(j) for j in range(per_half)]
+    loads = [own_copies(j) for j in range(per_half)]
+    loads += [first_copies(j) for j in range(per_half)]
     loads += [second_copies(j) for j in range(width // wide)]
-    ahead = 3
+    ahead = 2
+    for copies in loads[:ahead]:
+        for copy in copies:
+            copy.start()
     for j, copies in enumerate(loads):
         for copy in loads[j + ahead] if j + ahead < len(loads) else ():
             copy.start()
-        for copy in copies:
-            copy.wait()
+        if j >= per_half:
+            for copy in copies:
+                copy.wait()
         if j < 2 * per_half:
             gate, up = (gate_ref, up_ref) if j < per_half else (gate2_ref, up2_ref)
             at = slice((j % per_half) * step, (j % per_half + 1) * step)
             x = x_ref[...]
             gated = jnp.dot(x, gate[:, at], preferred_element_type=jnp.float32)
+            if j < per_half:
+                for copy in copies:
+                    copy.wait()
             upward = jnp.dot(x, up[:, at], preferred_element_type=jnp.float32)
             act_ref[:, j * step : (j + 1) * step] = (
                 gated / (1.0 + jnp.exp(-gated)) * upward
@@ -238,14 +268,15 @@
     return pl.pallas_call(
         expert_kernel,
         out_shape=jax.ShapeDtypeStruct(rows.shape, jnp.bfloat16),
-        in_specs=[whole] * 3 + [anywhere] * 4,
+        in_specs=[whole] * 2 + [anywhere] * 5,
         out_specs=whole,
         scratch_shapes=[
             pltpu.VMEM((width, units), jnp.bfloat16),
             pltpu.VMEM((width, units), jnp.bfloat16),
+            pltpu.VMEM((width, units), jnp.bfloat16),
             pltpu.VMEM((2 * units, width), jnp.bfloat16),
             pltpu.VMEM((slots, 2 * units), jnp.bfloat16),
-            pltpu.SemaphoreType.DMA((2, 3)),
+            pltpu.SemaphoreType.DMA((3, 3)),
             pltpu.SemaphoreType.DMA((2, 4)),
         ],
         compiler_params=pltpu.CompilerParams(vmem_limit_bytes=EXPERT_MIB * MIB),
@@ -278,9 +309,7 @@
         out_specs=(whole, whole),
         compiler_params=pltpu.CompilerParams(vmem_limit_bytes=24 * MIB),
         cost_estimate=pl.CostEstimate(
-            flops=2 * tokens * width * pieces * wide,
-            bytes_accessed=2 * (width + tokens) * pieces * wide,
-            transcendentals=0,
+            flops=1, bytes_accessed=2 * (width + tokens) * pieces * wide, transcendentals=0
         ),
         name="project",
     )(heads, weight)
@@ -391,7 +420,11 @@
     heads_out, swapped = lax.optimization_barrier((heads_out, swapped))
     parts = reduce_over_experts(heads_out, wo_pieces)
     rows = slots_of(routes)
-    attended, packed = norm_pack(hidden, parts, norm_gain, rows)
+    own_keep, own_swap, left_up, right_up, left_down, right_down = parts
+    near = near_sum(hidden, own_keep, own_swap, left_down, right_up)
+    attended, packed, weights = norm_pack(
+        near, left_up, right_down, norm_gain, rows, route_weights
+    )
 
     def across(slots):
         return lax.all_to_all(
@@ -399,7 +432,7 @@
         ).reshape(64 * CAP, D)
 
     back = across(whole_expert(across(packed), own, swapped))
-    return attended, combine(back, rows, route_weights)
+    return attended, combine(back, rows, weights)
 
 
 def solution(mesh):

time: 283 us -> 272 us (0.961)
  waiting for transfers between devices: 123 us -> 54.5 us
  blocking collectives: 57.4 us -> 112 us
  other arithmetic: 4.2 us -> 7.31 us
    all_to_all x1 -> x2, blocking collectives: 57.4 us -> 112 us  [across(): lax.all_to_all(slots.reshape(64, CAP, D), CHIP, split_axis=0, concat_axis...]
    all_to_all x1 -> x0, waiting for transfers between devices: 52.9 us -> none  [across(): lax.all_to_all(slots.reshape(64, CAP, D), CHIP, split_axis=0, concat_axis...]
    ppermute x3, waiting for transfers between devices: 24.9 us -> 6.76 us  [down(): return lax.ppermute(part, 'x', [(i, (i - 1) % 4) for i in range(4)])]
    ppermute x3, waiting for transfers between devices: 6.44 us -> 14.7 us  [up(): return lax.ppermute(part, 'x', [(i, (i + 1) % 4) for i in range(4)])]
    all_to_all x1 -> x0, starting transfers between devices: 5.79 us -> none  [across(): lax.all_to_all(slots.reshape(64, CAP, D), CHIP, split_axis=0, concat_axis...]
    ppermute x3, waiting for transfers between devices: 5.15 us -> 0.01 us  [swapped(): return lax.ppermute(part, 'core', SWAP)]
    ppermute x3, starting transfers between devices: 4.54 us -> 7.77 us  [down(): return lax.ppermute(part, 'x', [(i, (i - 1) % 4) for i in range(4)])]
    convert_element_type x3, other arithmetic: 3.42 us -> 6.54 us  [added(): return total.astype(jnp.bfloat16)]
  transfers between devices with their start and end apart: 15 -> 14, of which waited for: 10 -> 6; matrix products, arithmetic and copies ran while one was open for 3% -> 4% of each run, Pallas kernels for 6% -> 8%
where the time goes in v4:
time: 272 us; the launch traced here: 271 us
  blocking collectives  112 us (41%)
  waiting for transfers between devices  54.5 us (20%)
  Pallas kernels  51.8 us (19%)
  starting transfers between devices  19.2 us (7%)
  between operations  14.3 us (5%)
  local copies, waits for them, and re-layouts  12.4 us (5%)
  other arithmetic  7.31 us (3%)
    all_to_all x2, blocking collectives, across(): lax.all_to_all(slots.reshape(64, CAP, D), CHIP, split_axis=0, concat_axis...  112 us
    pallas_call x1, Pallas kernels, whole_expert(): pl.pallas_call(expert_kernel, out_shape=jax.ShapeDtypeStruct(rows.shape,...  24 us
    all_to_all x1, waiting for transfers between devices, local(): lax.all_to_all(jnp.broadcast_to(own_prefix[None], (n_list,) + own_prefix....  16.9 us
    all_gather x1, waiting for transfers between devices, local(): wo_pieces = lax.all_gather(o_weight, LIST, axis=0, tiled=False)  15.5 us
    ppermute x3, waiting for transfers between devices, up(): return lax.ppermute(part, 'x', [(i, (i + 1) % 4) for i in range(4)])  14.7 us
    pallas_call x1, Pallas kernels, attention(): pl.pallas_call(attention_kernel, out_shape=jax.ShapeDtypeStruct((tokens,...  13.9 us
    unnamed x34, local copies, waits for them, and re-layouts  9.15 us
    all_to_all x1, starting transfers between devices, local(): lax.all_to_all(jnp.broadcast_to(own_prefix[None], (n_list,) + own_prefix....  8.13 us
  transfers between devices with their start and end apart: 14, of which 6 were waited for; matrix products, arithmetic and copies ran while one was open for 4% of the time, Pallas kernels for 8%

profile of v4, /device:TPU:0, one launch (start us, length us, event | category | flops | bytes accessed | tf_op | source)
XLA Modules:
  0.0 271.3 jit_solution(15462221881455619578)
XLA Ops:
  7.2 0.0 copy-start
  7.2 0.0 all-gather.3.cloned.1.call-start
  7.2 0.7 all-gather.3.cloned.1.call-update
  7.9 0.1 collective-permute-start
  8.0 0.5 collective-permute-start.1
  8.5 0.1 collective-permute-start.2
  8.6 0.8 constant_dynamic-slice_fusion.1
  9.5 1.0 broadcast_in_dim.9
  10.4 8.1 %all-to-all-start = ((bf16[16,96,256]{2,1,0:T(8,128)(2,1)}), bf16[16,96,256]{2,1,0:T(8,128)(2,1)S(1)}, u32[]{:S(2)}, u32[]{:S(2)}) async-start(bf16[16,96,256]{2,1,0:T(8,128)(2,1)} %broadcast_in_dim.9), calls=%async_computation | async-start | bytes 1572864 | tf_op jit(solution)/shard_map/all_to_all | solution.py:389
  18.6 0.4 constant_dynamic-slice_fusion
  19.0 0.1 copy.39
  19.1 0.2 copy.26.segment_col_ref
  19.3 0.1 stack.35.order_ref
  19.4 16.9 %all-to-all-done = bf16[16,96,256]{2,1,0:T(8,128)(2,1)S(1)} async-done(((bf16[16,96,256]{2,1,0:T(8,128)(2,1)}), bf16[16,96,256]{2,1,0:T(8,128)(2,1)S(1)}, u32[]{:S(2)}, u32[]{:S(2)}) %all-to-all-start) | async-done | bytes 786464 | tf_op jit(solution)/shard_map/all_to_all | solution.py:389
  36.3 1.2 copy-done.4
  37.5 13.9 %attention.1.heads_ref = bf16[1024,512]{1,0:T(8,128)(2,1)S(1)} custom-call(s32[8]{0:T(128)S(1)} %stack.35.order_ref, bf16[1024,512]{1,0:T(8,128)(2,1)S(1)} %copy-done.4, bf16[1536,256]{1,0:T(8,128)(2,1)S(1)} %bitcast.57, bf16[1024,256]{1,0:T(8,128)(2,1)S(1)} %bitcast.58, s32[1024,1]{1,0:T(8,128)S(1)} %copy.26.segment_col_ref, s32[1,1024]{1,0:T(1,128)S(1)} %copy-done.6), custom_call_target="tpu_custom_call" | custom-call | tf_op jit(solution)/shard_map/attention/pallas_call | solution.py:71
  51.4 0.0 collective-permute-done.gate2_hbm
  51.4 0.0 collective-permute-done.2.down2_hbm
  51.4 15.5 %all-gather.3.cloned.1.call-done = bf16[8192,256]{1,0:T(8,128)(2,1)} async-done(((bf16[512,256]{1,0:T(8,128)(2,1)}), bf16[8192,256]{1,0:T(8,128)(2,1)}) %all-gather.3.cloned.1.call-update) | async-done | bytes 4194320 | tf_op jit(solution)/shard_map/all_gather | solution.py:396
  66.9 2.2 copy-done.2
  69.1 2.2 project.3
  71.3 1.0 copy-done.5
  72.3 0.0 collective-permute-start.7
  72.3 3.7 %project.4 = (bf16[256,4096]{1,0:T(8,128)(2,1)}, bf16[256,4096]{1,0:T(8,128)(2,1)S(1)}) custom-call(bf16[1024,512]{1,0:T(8,128)(2,1)S(1)} %attention.1.heads_ref, bf16[16,512,256]{2,1,0:T(8,128)(2,1)S(1)} %bitcast.47), custom_call_target="tpu_custom_call" | custom-call | flops 1 | bytes 8388608 | tf_op jit(solution)/shard_map/project/pallas_call | solution.py:305
  76.0 0.5 collective-permute-start.4
  76.5 0.1 copy.27
  76.6 0.1 eq.38
  76.7 0.0 copy-start.12
  76.7 0.0 copy-start.10
  76.8 2.9 %add_convert_fusion.2 = (bf16[128,2048]{1,0:T(8,128)(2,1)}, bf16[128,2048]{1,0:T(8,128)(2,1)}) fusion(bf16[128,4096]{1,0:T(8,128)(2,1)} %collective-permute-done.7, bf16[128,4096]{1,0:T(8,128)(2,1)} %copy-done.5), kind=kLoop, calls=%fused_computation.2 | loop fusion | flops 2097152 | bytes 3145728 | tf_op jit(solution)/shard_map/convert_element_type | solution.py:322
  79.7 1.5 collective-permute-start.8
  81.1 1.8 collective-permute-start.9
  82.9 0.1 eq.34
  83.1 0.6 reduce-window.6
  83.7 0.2 slice_reduce_fusion
  83.9 2.2 copy-done.3
  86.1 2.2 project.5
  88.3 1.0 copy-done.8
  89.3 0.0 collective-permute-start.3
  89.3 0.1 fusion.2
  89.4 0.1 reduce_sum.12
  89.5 0.1 copy.30
  89.6 0.1 copy.31.row_ref
  89.7 0.1 copy.32.weight_ref
  89.9 5.2 %collective-permute-done.8 = bf16[128,2048]{1,0:T(8,128)(2,1)} collective-permute-done((bf16[128,2048]{1,0:T(8,128)(2,1)}, bf16[128,2048]{1,0:T(8,128)(2,1)}, u32[]{:S(2)}, u32[]{:S(2)}) %collective-permute-start.8) | collective-permute-done | bytes 524320 | tf_op jit(solution)/shard_map/ppermute | solution.py:332
  95.0 0.0 collective-permute-done.9
  95.0 0.0 collective-permute-done.4
  95.0 1.6 add_convert_fusion.4
  96.6 3.0 %collective-permute-start.5 = (bf16[128,2048]{1,0:T(8,128)(2,1)S(1)}, bf16[128,2048]{1,0:T(8,128)(2,1)S(1)}, u32[]{:S(2)}, u32[]{:S(2)}) collective-permute-start(bf16[128,2048]{1,0:T(8,128)(2,1)S(1)} %get-tuple-element.47), channel_id=1, source_target_pairs={{0,6},{2,0},{4,2},{6,4},{1,7},{3,1},{5,3},{7,5},{8,14},{10,8},{12,... | collective-permute-start | bytes 1572872 | tf_op jit(solution)/shard_map/ppermute | solution.py:335
  99.7 2.0 add_convert_fusion
  101.7 0.6 collective-permute-start.10
  102.3 3.0 %collective-permute-start.11 = (bf16[128,2048]{1,0:T(8,128)(2,1)S(1)}, bf16[128,2048]{1,0:T(8,128)(2,1)S(1)}, u32[]{:S(2)}, u32[]{:S(2)}) collective-permute-start(bf16[128,2048]{1,0:T(8,128)(2,1)S(1)} %get-tuple-element.44), channel_id=1, source_target_pairs={{0,6},{2,0},{4,2},{6,4},{1,7},{3,1},{5,3},{7,5},{8,14},{10,8},{12,... | collective-permute-start | bytes 1572872 | tf_op jit(solution)/shard_map/ppermute | solution.py:335
  105.3 6.8 %collective-permute-done.5.left_down_ref = bf16[128,2048]{1,0:T(8,128)(2,1)S(1)} collective-permute-done((bf16[128,2048]{1,0:T(8,128)(2,1)S(1)}, bf16[128,2048]{1,0:T(8,128)(2,1)S(1)}, u32[]{:S(2)}, u32[]{:S(2)}) %collective-permute-start.5) | collective-permute-done | bytes 524320 | tf_op jit(solution)/shard_map/ppermute | solution.py:335
  112.0 3.7 %collective-permute-done.6.right_up_ref = bf16[128,2048]{1,0:T(8,128)(2,1)S(1)} collective-permute-done((bf16[128,2048]{1,0:T(8,128)(2,1)S(1)}, bf16[128,2048]{1,0:T(8,128)(2,1)S(1)}, u32[]{:S(2)}, u32[]{:S(2)}) %collective-permute-start.6) | collective-permute-done | bytes 524320 | tf_op jit(solution)/shard_map/ppermute | solution.py:332
  115.7 1.2 copy-done.7
  117.0 1.7 near_sum.1.near_ref
  118.7 5.8 %collective-permute-done.10.left_up_ref = bf16[128,2048]{1,0:T(8,128)(2,1)S(1)} collective-permute-done((bf16[128,2048]{1,0:T(8,128)(2,1)S(1)}, bf16[128,2048]{1,0:T(8,128)(2,1)S(1)}, u32[]{:S(2)}, u32[]{:S(2)}) %collective-permute-start.10) | collective-permute-done | bytes 524320 | tf_op jit(solution)/shard_map/ppermute | solution.py:332
  124.5 1.7 norm_pack.1
  126.2 0.0 slice-start.1
  126.2 57.2 %all_to_all.15 = bf16[64,8,4096]{2,1,0:T(8,128)(2,1)S(1)} all-to-all(bf16[64,8,4096]{2,1,0:T(8,128)(2,1)S(1)} %bitcast.56), channel_id=1, replica_groups=mesh['y'=4,'z'=4,'x'=4,'core'=2] {'y','z','x'}, dimensions={0} | all-to-all | bytes 8388608 | tf_op jit(solution)/shard_map/all_to_all | solution.py:430
  183.5 24.0 %whole_expert.1 = bf16[512,4096]{1,0:T(8,128)(2,1)S(1)} custom-call(bf16[512,4096]{1,0:T(8,128)(2,1)S(1)} %bitcast.50, bf16[4096,768]{1,0:T(8,128)(2,1)S(1)} %bitcast.55, bf16[4096,768]{1,0:T(8,128)(2,1)} %bitcast.62, bf16[768,4096]{1,0:T(8,128)(2,1)} %bitcast.64, bf16[4096,768]{1,0:T(8,128)(2,1)} %collective-permute-done.gate2_hbm, ...), custom_call_target="tpu_custom_call" | custom-call | tf_op jit(solution)/shard_map/whole_expert/pallas_call | solution.py:268
  207.5 0.0 copy-start.1
  207.5 54.6 %all_to_all.16 = bf16[64,8,4096]{2,1,0:T(8,128)(2,1)S(1)} all-to-all(bf16[64,8,4096]{2,1,0:T(8,128)(2,1)S(1)} %bitcast.51), channel_id=1, replica_groups=mesh['y'=4,'z'=4,'x'=4,'core'=2] {'y','z','x'}, dimensions={0} | all-to-all | bytes 8388608 | tf_op jit(solution)/shard_map/all_to_all | solution.py:430
  262.2 2.3 combine.1
  (32 shorter events, 0.1 us)
Async XLA Ops:
  7.2 11.5 %copy-start = (bf16[1024,2,256]{2,1,0:T(2,128)(2,1)S(1)}, bf16[1024,2,256]{2,1,0:T(2,128)(2,1)}, u32[]{:S(2)}) copy-start(bf16[1024,2,256]{2,1,0:T(2,128)(2,1)} %param.14) | copy-start | bytes 3145732
  7.2 11.9 %copy-start.6 = (s32[1,1024]{1,0:T(1,128)S(1)}, s32[1,1024]{1,0:T(1,128)}, u32[]{:S(2)}) copy-start(s32[1,1024]{1,0:T(1,128)} %segment_row_ref.1) | copy-start | bytes 12292
  7.2 59.7 %all-gather.3.cloned.1.call-start = ((), (), s32[]{:S(2)}) async-start(), calls=%async_computation.3 | async-start | bytes 4456448 | tf_op jit(solution)/shard_map/all_gather | solution.py:396
  7.9 43.5 %collective-permute-start = (bf16[4096,768]{1,0:T(8,128)(2,1)}, bf16[4096,768]{1,0:T(8,128)(2,1)}, u32[]{:S(2)}, u32[]{:S(2)}) collective-permute-start(bf16[4096,768]{1,0:T(8,128)(2,1)} %bitcast.52), channel_id=1, source_target_pairs={{0,1},{1,0},{2,3},{3,2},{4,5},{5,4},{6,7},{7,6},{8,9},{9,8},{10,11... | collective-permute-start | bytes 18874376 | tf_op jit(solution)/shard_map/ppermute | solution.py:419
  8.0 43.4 %collective-permute-start.1 = (bf16[4096,768]{1,0:T(8,128)(2,1)}, bf16[4096,768]{1,0:T(8,128)(2,1)}, u32[]{:S(2)}, u32[]{:S(2)}) collective-permute-start(bf16[4096,768]{1,0:T(8,128)(2,1)} %bitcast.61), channel_id=1, source_target_pairs={{0,1},{1,0},{2,3},{3,2},{4,5},{5,4},{6,7},{7,6},{8,9},{9,8},{10,11... | collective-permute-start | bytes 18874376 | tf_op jit(solution)/shard_map/ppermute | solution.py:419
  8.5 42.9 %collective-permute-start.2 = (bf16[768,4096]{1,0:T(8,128)(2,1)}, bf16[768,4096]{1,0:T(8,128)(2,1)}, u32[]{:S(2)}, u32[]{:S(2)}) collective-permute-start(bf16[768,4096]{1,0:T(8,128)(2,1)} %bitcast.63), channel_id=1, source_target_pairs={{0,1},{1,0},{2,3},{3,2},{4,5},{5,4},{6,7},{7,6},{8,9},{9,8},{10,11... | collective-permute-start | bytes 18874376 | tf_op jit(solution)/shard_map/ppermute | solution.py:419
  10.4 25.9 %all-to-all-start = ((bf16[16,96,256]{2,1,0:T(8,128)(2,1)}), bf16[16,96,256]{2,1,0:T(8,128)(2,1)S(1)}, u32[]{:S(2)}, u32[]{:S(2)}) async-start(bf16[16,96,256]{2,1,0:T(8,128)(2,1)} %broadcast_in_dim.9), calls=%async_computation | async-start | bytes 1572864 | tf_op jit(solution)/shard_map/all_to_all | solution.py:389
  36.3 1.2 copy-start.4
  66.9 2.2 copy-start.2
  69.1 7.4 %copy-start.11 = (s32[128,2]{0,1:T(2,128)S(1)}, s32[128,2]{0,1:T(2,128)}, u32[]{:S(2)}) copy-start(s32[128,2]{0,1:T(2,128)} %param.19) | copy-start | bytes 3076
  71.3 1.0 copy-start.5
  72.3 4.5 %collective-permute-start.7 = (bf16[128,4096]{1,0:T(8,128)(2,1)}, bf16[128,4096]{1,0:T(8,128)(2,1)}, u32[]{:S(2)}, u32[]{:S(2)}) collective-permute-start(bf16[128,4096]{1,0:T(8,128)(2,1)} %get-tuple-element.33), channel_id=1, source_target_pairs={{0,1},{1,0},{2,3},{3,2},{4,5},{5,4},{6,7},{7,6},{8,9},{9,8},{10,11... | collective-permute-start | bytes 3145736 | tf_op jit(solution)/shard_map/ppermute | solution.py:329
  76.0 19.1 %collective-permute-start.4 = (bf16[256,4096]{1,0:T(8,128)(2,1)}, bf16[256,4096]{1,0:T(8,128)(2,1)}, u32[]{:S(2)}, u32[]{:S(2)}) collective-permute-start(bf16[256,4096]{1,0:T(8,128)(2,1)} %get-tuple-element.31), channel_id=1, source_target_pairs={{0,1},{1,0},{2,3},{3,2},{4,5},{5,4},{6,7},{7,6},{8,9},{9,8},{10,11... | collective-permute-start | bytes 6291464 | tf_op jit(solution)/shard_map/ppermute | solution.py:329
  76.7 13.0 %copy-start.12 = (f32[128,2]{0,1:T(2,128)S(1)}, f32[128,2]{0,1:T(2,128)}, u32[]{:S(2)}) copy-start(f32[128,2]{0,1:T(2,128)} %param.20) | copy-start | bytes 3076
  76.7 13.1 %copy-start.10 = (bf16[4096]{0:T(1024)(128)(2,1)S(1)}, bf16[4096]{0:T(1024)(128)(2,1)}, u32[]{:S(2)}) copy-start(bf16[4096]{0:T(1024)(128)(2,1)} %param.18) | copy-start | bytes 24580
  79.7 15.4 %collective-permute-start.8 = (bf16[128,2048]{1,0:T(8,128)(2,1)}, bf16[128,2048]{1,0:T(8,128)(2,1)}, u32[]{:S(2)}, u32[]{:S(2)}) collective-permute-start(bf16[128,2048]{1,0:T(8,128)(2,1)} %get-tuple-element.49), channel_id=1, source_target_pairs={{0,2},{2,4},{4,6},{6,0},{1,3},{3,5},{5,7},{7,1},{8,10},{10,12},{12... | collective-permute-start | bytes 1572872 | tf_op jit(solution)/shard_map/ppermute | solution.py:332
  81.1 13.9 %collective-permute-start.9 = (bf16[128,2048]{1,0:T(8,128)(2,1)}, bf16[128,2048]{1,0:T(8,128)(2,1)}, u32[]{:S(2)}, u32[]{:S(2)}) collective-permute-start(bf16[128,2048]{1,0:T(8,128)(2,1)} %get-tuple-element.48), channel_id=1, source_target_pairs={{0,6},{2,0},{4,2},{6,4},{1,7},{3,1},{5,3},{7,5},{8,14},{10,8},{12,... | collective-permute-start | bytes 1572872 | tf_op jit(solution)/shard_map/ppermute | solution.py:335
  83.9 2.2 copy-start.3
  88.3 1.0 copy-start.8
  89.3 26.5 %copy-start.9 = (bf16[128,4096]{1,0:T(8,128)(2,1)S(1)}, bf16[128,4096]{1,0:T(8,128)(2,1)}, u32[]{:S(2)}) copy-start(bf16[128,4096]{1,0:T(8,128)(2,1)} %copy-done.8) | copy-start | bytes 3145732
  89.3 16.0 %collective-permute-start.3 = (bf16[128,4096]{1,0:T(8,128)(2,1)}, bf16[128,4096]{1,0:T(8,128)(2,1)}, u32[]{:S(2)}, u32[]{:S(2)}) collective-permute-start(bf16[128,4096]{1,0:T(8,128)(2,1)} %get-tuple-element.29), channel_id=1, source_target_pairs={{0,1},{1,0},{2,3},{3,2},{4,5},{5,4},{6,7},{7,6},{8,9},{9,8},{10,11... | collective-permute-start | bytes 3145736 | tf_op jit(solution)/shard_map/ppermute | solution.py:329
  96.6 15.4 %collective-permute-start.5 = (bf16[128,2048]{1,0:T(8,128)(2,1)S(1)}, bf16[128,2048]{1,0:T(8,128)(2,1)S(1)}, u32[]{:S(2)}, u32[]{:S(2)}) collective-permute-start(bf16[128,2048]{1,0:T(8,128)(2,1)S(1)} %get-tuple-element.47), channel_id=1, source_target_pairs={{0,6},{2,0},{4,2},{6,4},{1,7},{3,1},{5,3},{7,5},{8,14},{10,8},{12,... | collective-permute-start | bytes 1572872 | tf_op jit(solution)/shard_map/ppermute | solution.py:335
  99.7 16.1 %collective-permute-start.6 = (bf16[128,2048]{1,0:T(8,128)(2,1)S(1)}, bf16[128,2048]{1,0:T(8,128)(2,1)S(1)}, u32[]{:S(2)}, u32[]{:S(2)}) collective-permute-start(bf16[128,2048]{1,0:T(8,128)(2,1)S(1)} %get-tuple-element.46), channel_id=1, source_target_pairs={{0,2},{2,4},{4,6},{6,0},{1,3},{3,5},{5,7},{7,1},{8,10},{10,12},{12... | collective-permute-start | bytes 1572872 | tf_op jit(solution)/shard_map/ppermute | solution.py:332
  101.7 22.8 %collective-permute-start.10 = (bf16[128,2048]{1,0:T(8,128)(2,1)S(1)}, bf16[128,2048]{1,0:T(8,128)(2,1)S(1)}, u32[]{:S(2)}, u32[]{:S(2)}) collective-permute-start(bf16[128,2048]{1,0:T(8,128)(2,1)S(1)} %get-tuple-element.45), channel_id=1, source_target_pairs={{0,2},{2,4},{4,6},{6,0},{1,3},{3,5},{5,7},{7,1},{8,10},{10,12},{12... | collective-permute-start | bytes 1572872 | tf_op jit(solution)/shard_map/ppermute | solution.py:332
  102.3 22.2 %collective-permute-start.11 = (bf16[128,2048]{1,0:T(8,128)(2,1)S(1)}, bf16[128,2048]{1,0:T(8,128)(2,1)S(1)}, u32[]{:S(2)}, u32[]{:S(2)}) collective-permute-start(bf16[128,2048]{1,0:T(8,128)(2,1)S(1)} %get-tuple-element.44), channel_id=1, source_target_pairs={{0,6},{2,0},{4,2},{6,4},{1,7},{3,1},{5,3},{7,5},{8,14},{10,8},{12,... | collective-permute-start | bytes 1572872 | tf_op jit(solution)/shard_map/ppermute | solution.py:335
  115.7 1.2 copy-start.7
  124.5 59.0 %slice-start = ((s8[6291456]{0:T(1024)(128)(4,1)}), s8[4194304]{0:T(1024)(128)(4,1)S(1)}, s32[]{:S(2)}) async-start(s8[6291456]{0:T(1024)(128)(4,1)} %bitcast.53), calls=%async_computation.4 | async-start | bytes 8388608
  126.2 57.2 %slice-start.1 = ((s8[6291456]{0:T(1024)(128)(4,1)}), s8[2097152]{0:T(1024)(128)(4,1)S(1)}, s32[]{:S(2)}) async-start(s8[6291456]{0:T(1024)(128)(4,1)} %bitcast.53), calls=%async_computation.5 | async-start | bytes 4194304
  207.5 57.0 %copy-start.1 = (bf16[1024,2,256]{2,1,0:T(2,128)(2,1)S(1)}, bf16[1024,2,256]{2,1,0:T(2,128)(2,1)}, u32[]{:S(2)}) copy-start(bf16[1024,2,256]{2,1,0:T(2,128)(2,1)} %param.14) | copy-start | bytes 3145732
Sparse Core Ops, SparseCore 0:
  10.2 56.7 all-gather.2

commit v5 on v4

--- a/solution.py
+++ b/solution.py
@@ -142,7 +142,7 @@
     packed_ref[...] = jnp.dot(pick, normed, preferred_element_type=jnp.float32).astype(jnp.bfloat16)
 
 
-def norm_pack(near, left_up, right_down, gain, rows, weights):
+def norm_pack(near, left_up, right_down, gain, rows_t, weights):
     tokens, width = near.shape
     slots = 64 * CAP
     whole = pl.BlockSpec(memory_space=pltpu.VMEM)
@@ -157,7 +157,7 @@
         out_specs=(whole, whole, whole),
         compiler_params=pltpu.CompilerParams(vmem_limit_bytes=24 * MIB),
         name="norm_pack",
-    )(near, left_up, right_down, gain.reshape(1, width), rows.T, weights)
+    )(near, left_up, right_down, gain, rows_t, weights)
 
 
 def combine_kernel(back_ref, row_ref, weight_ref, out_ref):
@@ -335,13 +335,18 @@
         return lax.ppermute(part, "x", [(i, (i - 1) % 4) for i in range(4)])
 
     far_send, far_keep = project(heads_out, wo_pieces, 2 * BLOCK, 4 * BLOCK)
-    far_send, heads_out = lax.optimization_barrier((far_send, heads_out))
     far_swap = swapped(far_send)
+    far_left, far_right, heads_out = lax.optimization_barrier(
+        (
+            added(far_keep[:, :mid], far_swap[:, :mid]),
+            added(far_keep[:, mid:], far_swap[:, mid:]),
+            heads_out,
+        )
+    )
+    far_up, far_down = up(far_left), down(far_right)
     next_send, next_keep = project(heads_out, wo_pieces, 4 * BLOCK, 0)
     next_send, heads_out = lax.optimization_barrier((next_send, heads_out))
     next_swap = swapped(next_send)
-    far_up = up(added(far_keep[:, :mid], far_swap[:, :mid]))
-    far_down = down(added(far_keep[:, mid:], far_swap[:, mid:]))
     right_up = up(added(next_keep[:BLOCK, mid:], next_swap[:BLOCK, mid:]))
     left_down = down(added(next_keep[BLOCK:, :mid], next_swap[BLOCK:, :mid]))
     own_send, own_keep = project(heads_out, wo_pieces, 2 * BLOCK, 6 * BLOCK)
@@ -417,13 +422,15 @@
     heads_out = attention(query, prefix, of_head(candidate_key_value), segment_ids[0], order)
     own = (w_gate[0], w_up[0], w_down[0])
     swapped = tuple(lax.ppermute(w, "core", SWAP) for w in own)
-    heads_out, swapped = lax.optimization_barrier((heads_out, swapped))
+    rows = slots_of(routes)
+    heads_out, swapped, rows, rows_t, gain = lax.optimization_barrier(
+        (heads_out, swapped, rows, rows.T, norm_gain.reshape(1, D))
+    )
     parts = reduce_over_experts(heads_out, wo_pieces)
-    rows = slots_of(routes)
     own_keep, own_swap, left_up, right_up, left_down, right_down = parts
     near = near_sum(hidden, own_keep, own_swap, left_down, right_up)
     attended, packed, weights = norm_pack(
-        near, left_up, right_down, norm_gain, rows, route_weights
+        near, left_up, right_down, gain, rows_t, route_weights
     )
 
     def across(slots):

time: 272 us -> 270 us (level)
  blocking collectives: 112 us -> 118 us
    all_to_all x2, blocking collectives: 112 us -> 118 us  [across(): lax.all_to_all(slots.reshape(64, CAP, D), CHIP, split_axis=0, concat_axis...]
    unnamed x34 -> x30, local copies, waits for them, and re-layouts: 9.15 us -> 6.65 us
  transfers between devices with their start and end apart: 14 -> 14, of which waited for: 6 -> 7; matrix products, arithmetic and copies ran while one was open for 4% -> 3% of each run, Pallas kernels for 8% -> 6%
where the time goes in v5:
time: 270 us; the launch traced here: 269 us
  blocking collectives  118 us (44%)
  waiting for transfers between devices  53.2 us (20%)
  Pallas kernels  50 us (19%)
  starting transfers between devices  17.9 us (7%)
  between operations  14.3 us (5%)
  local copies, waits for them, and re-layouts  9.92 us (4%)
  other arithmetic  6.03 us (2%)
    all_to_all x2, blocking collectives, across(): lax.all_to_all(slots.reshape(64, CAP, D), CHIP, split_axis=0, concat_axis...  118 us
    pallas_call x1, Pallas kernels, whole_expert(): pl.pallas_call(expert_kernel, out_shape=jax.ShapeDtypeStruct(rows.shape,...  23.9 us
    all_gather x1, waiting for transfers between devices, local(): wo_pieces = lax.all_gather(o_weight, LIST, axis=0, tiled=False)  16.2 us
    all_to_all x1, waiting for transfers between devices, local(): lax.all_to_all(jnp.broadcast_to(own_prefix[None], (n_list,) + own_prefix....  14.5 us
    ppermute x3, waiting for transfers between devices, up(): return lax.ppermute(part, 'x', [(i, (i + 1) % 4) for i in range(4)])  13.3 us
    pallas_call x1, Pallas kernels, attention(): pl.pallas_call(attention_kernel, out_shape=jax.ShapeDtypeStruct((tokens,...  13.2 us
    all_to_all x1, starting transfers between devices, local(): lax.all_to_all(jnp.broadcast_to(own_prefix[None], (n_list,) + own_prefix....  8.13 us
    pallas_call x3, Pallas kernels, project(): pl.pallas_call(functools.partial(project_kernel, first), out_shape=(half,...  7.08 us
  transfers between devices with their start and end apart: 14, of which 7 were waited for; matrix products, arithmetic and copies ran while one was open for 3% of the time, Pallas kernels for 6%

profile of v5, /device:TPU:0, one launch (start us, length us, event | category | flops | bytes accessed | tf_op | source)
XLA Modules:
  0.0 269.2 jit_solution(15268247576442911709)
XLA Ops:
  7.2 0.0 copy-start
  7.2 0.0 copy-start.9
  7.2 0.0 all-gather.3.cloned.1.call-start
  7.3 0.7 all-gather.3.cloned.1.call-update
  7.9 0.1 collective-permute-start
  8.0 0.5 collective-permute-start.1
  8.5 0.1 collective-permute-start.2
  8.6 0.8 constant_dynamic-slice_fusion.1
  9.5 1.0 broadcast_in_dim.9
  10.4 8.1 %all-to-all-start = ((bf16[16,96,256]{2,1,0:T(8,128)(2,1)}), bf16[16,96,256]{2,1,0:T(8,128)(2,1)S(1)}, u32[]{:S(2)}, u32[]{:S(2)}) async-start(bf16[16,96,256]{2,1,0:T(8,128)(2,1)} %broadcast_in_dim.9), calls=%async_computation | async-start | bytes 1572864 | tf_op jit(solution)/shard_map/all_to_all | solution.py:394
  18.6 0.4 constant_dynamic-slice_fusion
  19.0 0.8 copy.27
  19.8 0.1 eq.34
  20.0 0.1 eq.38
  20.1 0.1 copy.39
  20.2 0.2 copy.26.segment_col_ref
  20.4 0.1 copy.30
  20.6 0.6 reduce-window.6
  21.2 0.2 slice_reduce_fusion
  21.4 0.1 fusion.2
  21.5 0.1 reduce_sum.12
  21.7 0.1 stack.35.order_ref
  21.8 14.5 %all-to-all-done = bf16[16,96,256]{2,1,0:T(8,128)(2,1)S(1)} async-done(((bf16[16,96,256]{2,1,0:T(8,128)(2,1)}), bf16[16,96,256]{2,1,0:T(8,128)(2,1)S(1)}, u32[]{:S(2)}, u32[]{:S(2)}) %all-to-all-start) | async-done | bytes 786464 | tf_op jit(solution)/shard_map/all_to_all | solution.py:394
  36.3 1.2 copy-done.3
  37.5 13.2 %attention.1.heads_ref = bf16[1024,512]{1,0:T(8,128)(2,1)S(1)} custom-call(s32[8]{0:T(128)S(1)} %stack.35.order_ref, bf16[1024,512]{1,0:T(8,128)(2,1)S(1)} %copy-done.3, bf16[1536,256]{1,0:T(8,128)(2,1)S(1)} %bitcast.57, bf16[1024,256]{1,0:T(8,128)(2,1)S(1)} %bitcast.58, s32[1024,1]{1,0:T(8,128)S(1)} %copy.26.segment_col_ref, s32[1,1024]{1,0:T(1,128)S(1)} %copy-done.4), custom_call_target="tpu_custom_call" | custom-call | tf_op jit(solution)/shard_map/attention/pallas_call | solution.py:71
  50.8 0.0 collective-permute-done.gate2_hbm
  50.8 0.0 collective-permute-done.1.up2_hbm
  50.8 0.0 collective-permute-done.2.down2_hbm
  50.8 16.2 %all-gather.3.cloned.1.call-done = bf16[8192,256]{1,0:T(8,128)(2,1)} async-done(((bf16[512,256]{1,0:T(8,128)(2,1)}), bf16[8192,256]{1,0:T(8,128)(2,1)}) %all-gather.3.cloned.1.call-update) | async-done | bytes 4194320 | tf_op jit(solution)/shard_map/all_gather | solution.py:401
  66.9 2.2 copy-done.2
  69.1 1.3 project.3
  70.4 0.1 collective-permute-start.3
  70.5 2.6 collective-permute-done.3
  73.1 1.5 add_convert_fusion.4
  74.6 3.6 %project.4 = (bf16[256,4096]{1,0:T(8,128)(2,1)}, bf16[256,4096]{1,0:T(8,128)(2,1)S(1)}) custom-call(bf16[1024,512]{1,0:T(8,128)(2,1)S(1)} %attention.1.heads_ref, bf16[16,512,256]{2,1,0:T(8,128)(2,1)S(1)} %bitcast.47), custom_call_target="tpu_custom_call" | custom-call | flops 1 | bytes 8388608 | tf_op jit(solution)/shard_map/project/pallas_call | solution.py:305
  78.3 0.1 collective-permute-start.5
  78.4 1.5 collective-permute-start.8
  79.9 1.8 collective-permute-start.9
  81.6 2.2 project.5
  83.8 1.0 copy-done.6
  84.8 0.0 collective-permute-start.4
  84.8 0.1 copy.32.weight_ref
  84.9 0.1 copy.31.row_ref
  85.0 0.0 collective-permute-done.5
  85.0 1.7 add_convert_fusion.2
  86.7 1.5 collective-permute-start.6
  88.3 0.5 collective-permute-start.7
  88.8 5.9 %collective-permute-done.8 = bf16[128,2048]{1,0:T(8,128)(2,1)} collective-permute-done((bf16[128,2048]{1,0:T(8,128)(2,1)}, bf16[128,2048]{1,0:T(8,128)(2,1)}, u32[]{:S(2)}, u32[]{:S(2)}) %collective-permute-start.8) | collective-permute-done | bytes 524320 | tf_op jit(solution)/shard_map/ppermute | solution.py:332
  94.7 0.3 collective-permute-done.9
  95.0 2.1 add_convert_fusion
  97.0 1.7 collective-permute-start.10
  98.8 1.8 collective-permute-start.11
  100.5 0.0 collective-permute-done.4.swap_ref
  100.5 5.6 %collective-permute-done.6.left_down_ref = bf16[128,2048]{1,0:T(8,128)(2,1)S(1)} collective-permute-done((bf16[128,2048]{1,0:T(8,128)(2,1)S(1)}, bf16[128,2048]{1,0:T(8,128)(2,1)S(1)}, u32[]{:S(2)}, u32[]{:S(2)}) %collective-permute-start.6) | collective-permute-done | bytes 524320 | tf_op jit(solution)/shard_map/ppermute | solution.py:335
  106.1 1.2 copy-done.5
  107.3 1.7 near_sum.1.near_ref
  109.0 7.5 %collective-permute-done.10.left_up_ref = bf16[128,2048]{1,0:T(8,128)(2,1)S(1)} collective-permute-done((bf16[128,2048]{1,0:T(8,128)(2,1)S(1)}, bf16[128,2048]{1,0:T(8,128)(2,1)S(1)}, u32[]{:S(2)}, u32[]{:S(2)}) %collective-permute-start.10) | collective-permute-done | bytes 524320 | tf_op jit(solution)/shard_map/ppermute | solution.py:332
  116.5 1.8 norm_pack.1
  118.3 0.0 slice-start.1
  118.3 61.0 %all_to_all.15 = bf16[64,8,4096]{2,1,0:T(8,128)(2,1)S(1)} all-to-all(bf16[64,8,4096]{2,1,0:T(8,128)(2,1)S(1)} %bitcast.56), channel_id=1, replica_groups=mesh['y'=4,'z'=4,'x'=4,'core'=2] {'y','z','x'}, dimensions={0} | all-to-all | bytes 8388608 | tf_op jit(solution)/shard_map/all_to_all | solution.py:437
  179.2 23.9 %whole_expert.1 = bf16[512,4096]{1,0:T(8,128)(2,1)S(1)} custom-call(bf16[512,4096]{1,0:T(8,128)(2,1)S(1)} %bitcast.50, bf16[4096,768]{1,0:T(8,128)(2,1)S(1)} %bitcast.55, bf16[4096,768]{1,0:T(8,128)(2,1)} %bitcast.62, bf16[768,4096]{1,0:T(8,128)(2,1)} %bitcast.64, bf16[4096,768]{1,0:T(8,128)(2,1)} %collective-permute-done.gate2_hbm, ...), custom_call_target="tpu_custom_call" | custom-call | tf_op jit(solution)/shard_map/whole_expert/pallas_call | solution.py:268
  203.2 0.0 copy-start.1
  203.2 56.9 %all_to_all.16 = bf16[64,8,4096]{2,1,0:T(8,128)(2,1)S(1)} all-to-all(bf16[64,8,4096]{2,1,0:T(8,128)(2,1)S(1)} %bitcast.51), channel_id=1, replica_groups=mesh['y'=4,'z'=4,'x'=4,'core'=2] {'y','z','x'}, dimensions={0} | all-to-all | bytes 8388608 | tf_op jit(solution)/shard_map/all_to_all | solution.py:437
  260.0 2.3 combine.1
  (28 shorter events, 0.1 us)
Async XLA Ops:
  7.2 11.4 %copy-start = (bf16[1024,2,256]{2,1,0:T(2,128)(2,1)S(1)}, bf16[1024,2,256]{2,1,0:T(2,128)(2,1)}, u32[]{:S(2)}) copy-start(bf16[1024,2,256]{2,1,0:T(2,128)(2,1)} %param.14) | copy-start | bytes 3145732
  7.2 13.2 %copy-start.9 = (s32[128,2]{0,1:T(2,128)S(1)}, s32[128,2]{0,1:T(2,128)}, u32[]{:S(2)}) copy-start(s32[128,2]{0,1:T(2,128)} %param.19) | copy-start | bytes 3076
  7.2 13.0 %copy-start.4 = (s32[1,1024]{1,0:T(1,128)S(1)}, s32[1,1024]{1,0:T(1,128)}, u32[]{:S(2)}) copy-start(s32[1,1024]{1,0:T(1,128)} %segment_row_ref.1) | copy-start | bytes 12292
  7.2 14.5 %copy-start.8 = (bf16[4096]{0:T(1024)(128)(2,1)S(1)}, bf16[4096]{0:T(1024)(128)(2,1)}, u32[]{:S(2)}) copy-start(bf16[4096]{0:T(1024)(128)(2,1)} %param.18) | copy-start | bytes 24580
  7.2 59.7 %all-gather.3.cloned.1.call-start = ((), (), s32[]{:S(2)}) async-start(), calls=%async_computation.3 | async-start | bytes 4456448 | tf_op jit(solution)/shard_map/all_gather | solution.py:401
  7.9 42.8 %collective-permute-start = (bf16[4096,768]{1,0:T(8,128)(2,1)}, bf16[4096,768]{1,0:T(8,128)(2,1)}, u32[]{:S(2)}, u32[]{:S(2)}) collective-permute-start(bf16[4096,768]{1,0:T(8,128)(2,1)} %bitcast.52), channel_id=1, source_target_pairs={{0,1},{1,0},{2,3},{3,2},{4,5},{5,4},{6,7},{7,6},{8,9},{9,8},{10,11... | collective-permute-start | bytes 18874376 | tf_op jit(solution)/shard_map/ppermute | solution.py:424
  8.0 42.7 %collective-permute-start.1 = (bf16[4096,768]{1,0:T(8,128)(2,1)}, bf16[4096,768]{1,0:T(8,128)(2,1)}, u32[]{:S(2)}, u32[]{:S(2)}) collective-permute-start(bf16[4096,768]{1,0:T(8,128)(2,1)} %bitcast.61), channel_id=1, source_target_pairs={{0,1},{1,0},{2,3},{3,2},{4,5},{5,4},{6,7},{7,6},{8,9},{9,8},{10,11... | collective-permute-start | bytes 18874376 | tf_op jit(solution)/shard_map/ppermute | solution.py:424
  8.5 42.2 %collective-permute-start.2 = (bf16[768,4096]{1,0:T(8,128)(2,1)}, bf16[768,4096]{1,0:T(8,128)(2,1)}, u32[]{:S(2)}, u32[]{:S(2)}) collective-permute-start(bf16[768,4096]{1,0:T(8,128)(2,1)} %bitcast.63), channel_id=1, source_target_pairs={{0,1},{1,0},{2,3},{3,2},{4,5},{5,4},{6,7},{7,6},{8,9},{9,8},{10,11... | collective-permute-start | bytes 18874376 | tf_op jit(solution)/shard_map/ppermute | solution.py:424
  10.4 25.8 %all-to-all-start = ((bf16[16,96,256]{2,1,0:T(8,128)(2,1)}), bf16[16,96,256]{2,1,0:T(8,128)(2,1)S(1)}, u32[]{:S(2)}, u32[]{:S(2)}) async-start(bf16[16,96,256]{2,1,0:T(8,128)(2,1)} %broadcast_in_dim.9), calls=%async_computation | async-start | bytes 1572864 | tf_op jit(solution)/shard_map/all_to_all | solution.py:394
  36.3 1.2 copy-start.3
  66.9 2.2 copy-start.2
  70.4 2.7 %collective-permute-start.3 = (bf16[128,4096]{1,0:T(8,128)(2,1)S(1)}, bf16[128,4096]{1,0:T(8,128)(2,1)S(1)}, u32[]{:S(2)}, u32[]{:S(2)}) collective-permute-start(bf16[128,4096]{1,0:T(8,128)(2,1)S(1)} %get-tuple-element.29), channel_id=1, source_target_pairs={{0,1},{1,0},{2,3},{3,2},{4,5},{5,4},{6,7},{7,6},{8,9},{9,8},{10,11... | collective-permute-start | bytes 3145736 | tf_op jit(solution)/shard_map/ppermute | solution.py:329
  74.6 10.2 %copy-start.10 = (f32[128,2]{0,1:T(2,128)S(1)}, f32[128,2]{0,1:T(2,128)}, u32[]{:S(2)}) copy-start(f32[128,2]{0,1:T(2,128)} %param.20) | copy-start | bytes 3076
  78.3 6.7 %collective-permute-start.5 = (bf16[256,4096]{1,0:T(8,128)(2,1)}, bf16[256,4096]{1,0:T(8,128)(2,1)}, u32[]{:S(2)}, u32[]{:S(2)}) collective-permute-start(bf16[256,4096]{1,0:T(8,128)(2,1)} %get-tuple-element.36), channel_id=1, source_target_pairs={{0,1},{1,0},{2,3},{3,2},{4,5},{5,4},{6,7},{7,6},{8,9},{9,8},{10,11... | collective-permute-start | bytes 6291464 | tf_op jit(solution)/shard_map/ppermute | solution.py:329
  78.4 16.3 %collective-permute-start.8 = (bf16[128,2048]{1,0:T(8,128)(2,1)}, bf16[128,2048]{1,0:T(8,128)(2,1)}, u32[]{:S(2)}, u32[]{:S(2)}) collective-permute-start(bf16[128,2048]{1,0:T(8,128)(2,1)} %get-tuple-element.37), channel_id=1, source_target_pairs={{0,2},{2,4},{4,6},{6,0},{1,3},{3,5},{5,7},{7,1},{8,10},{10,12},{12... | collective-permute-start | bytes 1572872 | tf_op jit(solution)/shard_map/ppermute | solution.py:332
  79.9 15.1 %collective-permute-start.9 = (bf16[128,2048]{1,0:T(8,128)(2,1)}, bf16[128,2048]{1,0:T(8,128)(2,1)}, u32[]{:S(2)}, u32[]{:S(2)}) collective-permute-start(bf16[128,2048]{1,0:T(8,128)(2,1)} %get-tuple-element.38), channel_id=1, source_target_pairs={{0,6},{2,0},{4,2},{6,4},{1,7},{3,1},{5,3},{7,5},{8,14},{10,8},{12,... | collective-permute-start | bytes 1572872 | tf_op jit(solution)/shard_map/ppermute | solution.py:335
  83.8 1.0 copy-start.6
  84.8 21.3 %copy-start.7 = (bf16[128,4096]{1,0:T(8,128)(2,1)S(1)}, bf16[128,4096]{1,0:T(8,128)(2,1)}, u32[]{:S(2)}) copy-start(bf16[128,4096]{1,0:T(8,128)(2,1)} %copy-done.6) | copy-start | bytes 3145732
  84.8 15.7 %collective-permute-start.4 = (bf16[128,4096]{1,0:T(8,128)(2,1)}, bf16[128,4096]{1,0:T(8,128)(2,1)}, u32[]{:S(2)}, u32[]{:S(2)}) collective-permute-start(bf16[128,4096]{1,0:T(8,128)(2,1)} %get-tuple-element.34), channel_id=1, source_target_pairs={{0,1},{1,0},{2,3},{3,2},{4,5},{5,4},{6,7},{7,6},{8,9},{9,8},{10,11... | collective-permute-start | bytes 3145736 | tf_op jit(solution)/shard_map/ppermute | solution.py:329
  86.7 19.4 %collective-permute-start.6 = (bf16[128,2048]{1,0:T(8,128)(2,1)S(1)}, bf16[128,2048]{1,0:T(8,128)(2,1)S(1)}, u32[]{:S(2)}, u32[]{:S(2)}) collective-permute-start(bf16[128,2048]{1,0:T(8,128)(2,1)S(1)} %get-tuple-element.55), channel_id=1, source_target_pairs={{0,6},{2,0},{4,2},{6,4},{1,7},{3,1},{5,3},{7,5},{8,14},{10,8},{12,... | collective-permute-start | bytes 1572872 | tf_op jit(solution)/shard_map/ppermute | solution.py:335
  88.3 17.8 %collective-permute-start.7 = (bf16[128,2048]{1,0:T(8,128)(2,1)S(1)}, bf16[128,2048]{1,0:T(8,128)(2,1)S(1)}, u32[]{:S(2)}, u32[]{:S(2)}) collective-permute-start(bf16[128,2048]{1,0:T(8,128)(2,1)S(1)} %get-tuple-element.54), channel_id=1, source_target_pairs={{0,2},{2,4},{4,6},{6,0},{1,3},{3,5},{5,7},{7,1},{8,10},{10,12},{12... | collective-permute-start | bytes 1572872 | tf_op jit(solution)/shard_map/ppermute | solution.py:332
  97.0 19.5 %collective-permute-start.10 = (bf16[128,2048]{1,0:T(8,128)(2,1)S(1)}, bf16[128,2048]{1,0:T(8,128)(2,1)S(1)}, u32[]{:S(2)}, u32[]{:S(2)}) collective-permute-start(bf16[128,2048]{1,0:T(8,128)(2,1)S(1)} %get-tuple-element.53), channel_id=1, source_target_pairs={{0,2},{2,4},{4,6},{6,0},{1,3},{3,5},{5,7},{7,1},{8,10},{10,12},{12... | collective-permute-start | bytes 1572872 | tf_op jit(solution)/shard_map/ppermute | solution.py:332
  98.8 17.7 %collective-permute-start.11 = (bf16[128,2048]{1,0:T(8,128)(2,1)S(1)}, bf16[128,2048]{1,0:T(8,128)(2,1)S(1)}, u32[]{:S(2)}, u32[]{:S(2)}) collective-permute-start(bf16[128,2048]{1,0:T(8,128)(2,1)S(1)} %get-tuple-element.52), channel_id=1, source_target_pairs={{0,6},{2,0},{4,2},{6,4},{1,7},{3,1},{5,3},{7,5},{8,14},{10,8},{12,... | collective-permute-start | bytes 1572872 | tf_op jit(solution)/shard_map/ppermute | solution.py:335
  106.1 1.2 copy-start.5
  116.5 62.7 %slice-start = ((s8[6291456]{0:T(1024)(128)(4,1)}), s8[4194304]{0:T(1024)(128)(4,1)S(1)}, s32[]{:S(2)}) async-start(s8[6291456]{0:T(1024)(128)(4,1)} %bitcast.53), calls=%async_computation.4 | async-start | bytes 8388608
  118.3 61.0 %slice-start.1 = ((s8[6291456]{0:T(1024)(128)(4,1)}), s8[2097152]{0:T(1024)(128)(4,1)S(1)}, s32[]{:S(2)}) async-start(s8[6291456]{0:T(1024)(128)(4,1)} %bitcast.53), calls=%async_computation.5 | async-start | bytes 4194304
  203.2 59.2 %copy-start.1 = (bf16[1024,2,256]{2,1,0:T(2,128)(2,1)S(1)}, bf16[1024,2,256]{2,1,0:T(2,128)(2,1)}, u32[]{:S(2)}) copy-start(bf16[1024,2,256]{2,1,0:T(2,128)(2,1)} %param.14) | copy-start | bytes 3145732
Sparse Core Ops, SparseCore 0:
  10.2 56.7 all-gather.2

commit v6 on v5

--- a/solution.py
+++ b/solution.py
@@ -203,7 +203,7 @@
 ):
     hidden_units = gate_ref.shape[1]
     width = x_ref.shape[1]
-    step, wide = 256, 1024
+    step, wide = 256, 512
     per_half = hidden_units // step
 
     def own_copies(j):
@@ -277,7 +277,7 @@
             pltpu.VMEM((2 * units, width), jnp.bfloat16),
             pltpu.VMEM((slots, 2 * units), jnp.bfloat16),
             pltpu.SemaphoreType.DMA((3, 3)),
-            pltpu.SemaphoreType.DMA((2, 4)),
+            pltpu.SemaphoreType.DMA((2, 8)),
         ],
         compiler_params=pltpu.CompilerParams(vmem_limit_bytes=EXPERT_MIB * MIB),
         name="whole_expert",

time: 270 us -> 270 us (level)
  no operation moved by 1% of the time
where the time goes in v6:
time: 270 us
  blocking collectives  118 us (44%)
  waiting for transfers between devices  53.2 us (20%)
  Pallas kernels  50.7 us (19%)
  starting transfers between devices  17.9 us (7%)
  between operations  14.3 us (5%)
  local copies, waits for them, and re-layouts  9.92 us (4%)
  other arithmetic  6.03 us (2%)
    all_to_all x2, blocking collectives, across(): lax.all_to_all(slots.reshape(64, CAP, D), CHIP, split_axis=0, concat_axis...  118 us
    pallas_call x1, Pallas kernels, whole_expert(): pl.pallas_call(expert_kernel, out_shape=jax.ShapeDtypeStruct(rows.shape,...  24.7 us
    all_gather x1, waiting for transfers between devices, local(): wo_pieces = lax.all_gather(o_weight, LIST, axis=0, tiled=False)  16.2 us
    all_to_all x1, waiting for transfers between devices, local(): lax.all_to_all(jnp.broadcast_to(own_prefix[None], (n_list,) + own_prefix....  14.5 us
    ppermute x3, waiting for transfers between devices, up(): return lax.ppermute(part, 'x', [(i, (i + 1) % 4) for i in range(4)])  13.3 us
    pallas_call x1, Pallas kernels, attention(): pl.pallas_call(attention_kernel, out_shape=jax.ShapeDtypeStruct((tokens,...  13.2 us
    all_to_all x1, starting transfers between devices, local(): lax.all_to_all(jnp.broadcast_to(own_prefix[None], (n_list,) + own_prefix....  8.13 us
    pallas_call x3, Pallas kernels, project(): pl.pallas_call(functools.partial(project_kernel, first), out_shape=(half,...  7.08 us
  transfers between devices with their start and end apart: 14, of which 7 were waited for; matrix products, arithmetic and copies ran while one was open for 3% of the time, Pallas kernels for 6%

profile of v6, /device:TPU:0, one launch (start us, length us, event | category | flops | bytes accessed | tf_op | source)
XLA Modules:
  0.0 269.9 jit_solution(970730792469925223)
XLA Ops:
  7.2 0.0 copy-start
  7.2 0.0 copy-start.9
  7.2 0.0 all-gather.3.cloned.1.call-start
  7.3 0.7 all-gather.3.cloned.1.call-update
  7.9 0.1 collective-permute-start
  8.0 0.5 collective-permute-start.1
  8.5 0.1 collective-permute-start.2
  8.6 0.8 constant_dynamic-slice_fusion.1
  9.5 1.0 broadcast_in_dim.9
  10.4 8.1 %all-to-all-start = ((bf16[16,96,256]{2,1,0:T(8,128)(2,1)}), bf16[16,96,256]{2,1,0:T(8,128)(2,1)S(1)}, u32[]{:S(2)}, u32[]{:S(2)}) async-start(bf16[16,96,256]{2,1,0:T(8,128)(2,1)} %broadcast_in_dim.9), calls=%async_computation | async-start | bytes 1572864 | tf_op jit(solution)/shard_map/all_to_all | solution.py:394
  18.6 0.4 constant_dynamic-slice_fusion
  19.0 0.8 copy.27
  19.8 0.1 eq.34
  20.0 0.1 eq.38
  20.1 0.1 copy.39
  20.2 0.2 copy.26.segment_col_ref
  20.4 0.1 copy.30
  20.6 0.6 reduce-window.6
  21.2 0.2 slice_reduce_fusion
  21.4 0.1 fusion.2
  21.5 0.1 reduce_sum.12
  21.7 0.1 stack.35.order_ref
  21.8 14.5 %all-to-all-done = bf16[16,96,256]{2,1,0:T(8,128)(2,1)S(1)} async-done(((bf16[16,96,256]{2,1,0:T(8,128)(2,1)}), bf16[16,96,256]{2,1,0:T(8,128)(2,1)S(1)}, u32[]{:S(2)}, u32[]{:S(2)}) %all-to-all-start) | async-done | bytes 786464 | tf_op jit(solution)/shard_map/all_to_all | solution.py:394
  36.3 1.2 copy-done.3
  37.5 13.2 %attention.1.heads_ref = bf16[1024,512]{1,0:T(8,128)(2,1)S(1)} custom-call(s32[8]{0:T(128)S(1)} %stack.35.order_ref, bf16[1024,512]{1,0:T(8,128)(2,1)S(1)} %copy-done.3, bf16[1536,256]{1,0:T(8,128)(2,1)S(1)} %bitcast.57, bf16[1024,256]{1,0:T(8,128)(2,1)S(1)} %bitcast.58, s32[1024,1]{1,0:T(8,128)S(1)} %copy.26.segment_col_ref, s32[1,1024]{1,0:T(1,128)S(1)} %copy-done.4), custom_call_target="tpu_custom_call" | custom-call | tf_op jit(solution)/shard_map/attention/pallas_call | solution.py:71
  50.8 0.0 collective-permute-done.gate2_hbm
  50.8 0.0 collective-permute-done.1.up2_hbm
  50.8 0.0 collective-permute-done.2.down2_hbm
  50.8 16.2 %all-gather.3.cloned.1.call-done = bf16[8192,256]{1,0:T(8,128)(2,1)} async-done(((bf16[512,256]{1,0:T(8,128)(2,1)}), bf16[8192,256]{1,0:T(8,128)(2,1)}) %all-gather.3.cloned.1.call-update) | async-done | bytes 4194320 | tf_op jit(solution)/shard_map/all_gather | solution.py:401
  66.9 2.2 copy-done.2
  69.1 1.3 project.3
  70.4 0.1 collective-permute-start.3
  70.5 2.6 collective-permute-done.3
  73.1 1.5 add_convert_fusion.4
  74.6 3.6 %project.4 = (bf16[256,4096]{1,0:T(8,128)(2,1)}, bf16[256,4096]{1,0:T(8,128)(2,1)S(1)}) custom-call(bf16[1024,512]{1,0:T(8,128)(2,1)S(1)} %attention.1.heads_ref, bf16[16,512,256]{2,1,0:T(8,128)(2,1)S(1)} %bitcast.47), custom_call_target="tpu_custom_call" | custom-call | flops 1 | bytes 8388608 | tf_op jit(solution)/shard_map/project/pallas_call | solution.py:305
  78.3 0.1 collective-permute-start.5
  78.4 1.5 collective-permute-start.8
  79.9 1.8 collective-permute-start.9
  81.6 2.2 project.5
  83.8 1.0 copy-done.6
  84.8 0.0 collective-permute-start.4
  84.8 0.1 copy.32.weight_ref
  84.9 0.1 copy.31.row_ref
  85.0 0.0 collective-permute-done.5
  85.0 1.7 add_convert_fusion.2
  86.7 1.5 collective-permute-start.6
  88.3 0.5 collective-permute-start.7
  88.8 5.9 %collective-permute-done.8 = bf16[128,2048]{1,0:T(8,128)(2,1)} collective-permute-done((bf16[128,2048]{1,0:T(8,128)(2,1)}, bf16[128,2048]{1,0:T(8,128)(2,1)}, u32[]{:S(2)}, u32[]{:S(2)}) %collective-permute-start.8) | collective-permute-done | bytes 524320 | tf_op jit(solution)/shard_map/ppermute | solution.py:332
  94.7 0.3 collective-permute-done.9
  95.0 2.1 add_convert_fusion
  97.0 1.7 collective-permute-start.10
  98.8 1.8 collective-permute-start.11
  100.5 0.0 collective-permute-done.4.swap_ref
  100.5 5.6 %collective-permute-done.6.left_down_ref = bf16[128,2048]{1,0:T(8,128)(2,1)S(1)} collective-permute-done((bf16[128,2048]{1,0:T(8,128)(2,1)S(1)}, bf16[128,2048]{1,0:T(8,128)(2,1)S(1)}, u32[]{:S(2)}, u32[]{:S(2)}) %collective-permute-start.6) | collective-permute-done | bytes 524320 | tf_op jit(solution)/shard_map/ppermute | solution.py:335
  106.1 1.2 copy-done.5
  107.3 1.7 near_sum.1.near_ref
  109.0 7.5 %collective-permute-done.10.left_up_ref = bf16[128,2048]{1,0:T(8,128)(2,1)S(1)} collective-permute-done((bf16[128,2048]{1,0:T(8,128)(2,1)S(1)}, bf16[128,2048]{1,0:T(8,128)(2,1)S(1)}, u32[]{:S(2)}, u32[]{:S(2)}) %collective-permute-start.10) | collective-permute-done | bytes 524320 | tf_op jit(solution)/shard_map/ppermute | solution.py:332
  116.5 1.8 norm_pack.1
  118.3 0.0 slice-start.1
  118.3 61.0 %all_to_all.15 = bf16[64,8,4096]{2,1,0:T(8,128)(2,1)S(1)} all-to-all(bf16[64,8,4096]{2,1,0:T(8,128)(2,1)S(1)} %bitcast.56), channel_id=1, replica_groups=mesh['y'=4,'z'=4,'x'=4,'core'=2] {'y','z','x'}, dimensions={0} | all-to-all | bytes 8388608 | tf_op jit(solution)/shard_map/all_to_all | solution.py:437
  179.2 24.7 %whole_expert.1 = bf16[512,4096]{1,0:T(8,128)(2,1)S(1)} custom-call(bf16[512,4096]{1,0:T(8,128)(2,1)S(1)} %bitcast.50, bf16[4096,768]{1,0:T(8,128)(2,1)S(1)} %bitcast.55, bf16[4096,768]{1,0:T(8,128)(2,1)} %bitcast.62, bf16[768,4096]{1,0:T(8,128)(2,1)} %bitcast.64, bf16[4096,768]{1,0:T(8,128)(2,1)} %collective-permute-done.gate2_hbm, ...), custom_call_target="tpu_custom_call" | custom-call | tf_op jit(solution)/shard_map/whole_expert/pallas_call | solution.py:268
  203.9 0.0 copy-start.1
  203.9 56.9 %all_to_all.16 = bf16[64,8,4096]{2,1,0:T(8,128)(2,1)S(1)} all-to-all(bf16[64,8,4096]{2,1,0:T(8,128)(2,1)S(1)} %bitcast.51), channel_id=1, replica_groups=mesh['y'=4,'z'=4,'x'=4,'core'=2] {'y','z','x'}, dimensions={0} | all-to-all | bytes 8388608 | tf_op jit(solution)/shard_map/all_to_all | solution.py:437
  260.8 2.3 combine.1
  (28 shorter events, 0.1 us)
Async XLA Ops:
  7.2 11.4 %copy-start = (bf16[1024,2,256]{2,1,0:T(2,128)(2,1)S(1)}, bf16[1024,2,256]{2,1,0:T(2,128)(2,1)}, u32[]{:S(2)}) copy-start(bf16[1024,2,256]{2,1,0:T(2,128)(2,1)} %param.14) | copy-start | bytes 3145732
  7.2 13.2 %copy-start.9 = (s32[128,2]{0,1:T(2,128)S(1)}, s32[128,2]{0,1:T(2,128)}, u32[]{:S(2)}) copy-start(s32[128,2]{0,1:T(2,128)} %param.19) | copy-start | bytes 3076
  7.2 13.0 %copy-start.4 = (s32[1,1024]{1,0:T(1,128)S(1)}, s32[1,1024]{1,0:T(1,128)}, u32[]{:S(2)}) copy-start(s32[1,1024]{1,0:T(1,128)} %segment_row_ref.1) | copy-start | bytes 12292
  7.2 14.5 %copy-start.8 = (bf16[4096]{0:T(1024)(128)(2,1)S(1)}, bf16[4096]{0:T(1024)(128)(2,1)}, u32[]{:S(2)}) copy-start(bf16[4096]{0:T(1024)(128)(2,1)} %param.18) | copy-start | bytes 24580
  7.2 59.7 %all-gather.3.cloned.1.call-start = ((), (), s32[]{:S(2)}) async-start(), calls=%async_computation.3 | async-start | bytes 4456448 | tf_op jit(solution)/shard_map/all_gather | solution.py:401
  7.9 42.8 %collective-permute-start = (bf16[4096,768]{1,0:T(8,128)(2,1)}, bf16[4096,768]{1,0:T(8,128)(2,1)}, u32[]{:S(2)}, u32[]{:S(2)}) collective-permute-start(bf16[4096,768]{1,0:T(8,128)(2,1)} %bitcast.52), channel_id=1, source_target_pairs={{0,1},{1,0},{2,3},{3,2},{4,5},{5,4},{6,7},{7,6},{8,9},{9,8},{10,11... | collective-permute-start | bytes 18874376 | tf_op jit(solution)/shard_map/ppermute | solution.py:424
  8.0 42.7 %collective-permute-start.1 = (bf16[4096,768]{1,0:T(8,128)(2,1)}, bf16[4096,768]{1,0:T(8,128)(2,1)}, u32[]{:S(2)}, u32[]{:S(2)}) collective-permute-start(bf16[4096,768]{1,0:T(8,128)(2,1)} %bitcast.61), channel_id=1, source_target_pairs={{0,1},{1,0},{2,3},{3,2},{4,5},{5,4},{6,7},{7,6},{8,9},{9,8},{10,11... | collective-permute-start | bytes 18874376 | tf_op jit(solution)/shard_map/ppermute | solution.py:424
  8.5 42.2 %collective-permute-start.2 = (bf16[768,4096]{1,0:T(8,128)(2,1)}, bf16[768,4096]{1,0:T(8,128)(2,1)}, u32[]{:S(2)}, u32[]{:S(2)}) collective-permute-start(bf16[768,4096]{1,0:T(8,128)(2,1)} %bitcast.63), channel_id=1, source_target_pairs={{0,1},{1,0},{2,3},{3,2},{4,5},{5,4},{6,7},{7,6},{8,9},{9,8},{10,11... | collective-permute-start | bytes 18874376 | tf_op jit(solution)/shard_map/ppermute | solution.py:424
  10.4 25.8 %all-to-all-start = ((bf16[16,96,256]{2,1,0:T(8,128)(2,1)}), bf16[16,96,256]{2,1,0:T(8,128)(2,1)S(1)}, u32[]{:S(2)}, u32[]{:S(2)}) async-start(bf16[16,96,256]{2,1,0:T(8,128)(2,1)} %broadcast_in_dim.9), calls=%async_computation | async-start | bytes 1572864 | tf_op jit(solution)/shard_map/all_to_all | solution.py:394
  36.3 1.2 copy-start.3
  66.9 2.2 copy-start.2
  70.4 2.7 %collective-permute-start.3 = (bf16[128,4096]{1,0:T(8,128)(2,1)S(1)}, bf16[128,4096]{1,0:T(8,128)(2,1)S(1)}, u32[]{:S(2)}, u32[]{:S(2)}) collective-permute-start(bf16[128,4096]{1,0:T(8,128)(2,1)S(1)} %get-tuple-element.29), channel_id=1, source_target_pairs={{0,1},{1,0},{2,3},{3,2},{4,5},{5,4},{6,7},{7,6},{8,9},{9,8},{10,11... | collective-permute-start | bytes 3145736 | tf_op jit(solution)/shard_map/ppermute | solution.py:329
  74.6 10.2 %copy-start.10 = (f32[128,2]{0,1:T(2,128)S(1)}, f32[128,2]{0,1:T(2,128)}, u32[]{:S(2)}) copy-start(f32[128,2]{0,1:T(2,128)} %param.20) | copy-start | bytes 3076
  78.3 6.7 %collective-permute-start.5 = (bf16[256,4096]{1,0:T(8,128)(2,1)}, bf16[256,4096]{1,0:T(8,128)(2,1)}, u32[]{:S(2)}, u32[]{:S(2)}) collective-permute-start(bf16[256,4096]{1,0:T(8,128)(2,1)} %get-tuple-element.36), channel_id=1, source_target_pairs={{0,1},{1,0},{2,3},{3,2},{4,5},{5,4},{6,7},{7,6},{8,9},{9,8},{10,11... | collective-permute-start | bytes 6291464 | tf_op jit(solution)/shard_map/ppermute | solution.py:329
  78.4 16.3 %collective-permute-start.8 = (bf16[128,2048]{1,0:T(8,128)(2,1)}, bf16[128,2048]{1,0:T(8,128)(2,1)}, u32[]{:S(2)}, u32[]{:S(2)}) collective-permute-start(bf16[128,2048]{1,0:T(8,128)(2,1)} %get-tuple-element.37), channel_id=1, source_target_pairs={{0,2},{2,4},{4,6},{6,0},{1,3},{3,5},{5,7},{7,1},{8,10},{10,12},{12... | collective-permute-start | bytes 1572872 | tf_op jit(solution)/shard_map/ppermute | solution.py:332
  79.9 15.1 %collective-permute-start.9 = (bf16[128,2048]{1,0:T(8,128)(2,1)}, bf16[128,2048]{1,0:T(8,128)(2,1)}, u32[]{:S(2)}, u32[]{:S(2)}) collective-permute-start(bf16[128,2048]{1,0:T(8,128)(2,1)} %get-tuple-element.38), channel_id=1, source_target_pairs={{0,6},{2,0},{4,2},{6,4},{1,7},{3,1},{5,3},{7,5},{8,14},{10,8},{12,... | collective-permute-start | bytes 1572872 | tf_op jit(solution)/shard_map/ppermute | solution.py:335
  83.8 1.0 copy-start.6
  84.8 21.3 %copy-start.7 = (bf16[128,4096]{1,0:T(8,128)(2,1)S(1)}, bf16[128,4096]{1,0:T(8,128)(2,1)}, u32[]{:S(2)}) copy-start(bf16[128,4096]{1,0:T(8,128)(2,1)} %copy-done.6) | copy-start | bytes 3145732
  84.8 15.7 %collective-permute-start.4 = (bf16[128,4096]{1,0:T(8,128)(2,1)}, bf16[128,4096]{1,0:T(8,128)(2,1)}, u32[]{:S(2)}, u32[]{:S(2)}) collective-permute-start(bf16[128,4096]{1,0:T(8,128)(2,1)} %get-tuple-element.34), channel_id=1, source_target_pairs={{0,1},{1,0},{2,3},{3,2},{4,5},{5,4},{6,7},{7,6},{8,9},{9,8},{10,11... | collective-permute-start | bytes 3145736 | tf_op jit(solution)/shard_map/ppermute | solution.py:329
  86.7 19.4 %collective-permute-start.6 = (bf16[128,2048]{1,0:T(8,128)(2,1)S(1)}, bf16[128,2048]{1,0:T(8,128)(2,1)S(1)}, u32[]{:S(2)}, u32[]{:S(2)}) collective-permute-start(bf16[128,2048]{1,0:T(8,128)(2,1)S(1)} %get-tuple-element.55), channel_id=1, source_target_pairs={{0,6},{2,0},{4,2},{6,4},{1,7},{3,1},{5,3},{7,5},{8,14},{10,8},{12,... | collective-permute-start | bytes 1572872 | tf_op jit(solution)/shard_map/ppermute | solution.py:335
  88.3 17.8 %collective-permute-start.7 = (bf16[128,2048]{1,0:T(8,128)(2,1)S(1)}, bf16[128,2048]{1,0:T(8,128)(2,1)S(1)}, u32[]{:S(2)}, u32[]{:S(2)}) collective-permute-start(bf16[128,2048]{1,0:T(8,128)(2,1)S(1)} %get-tuple-element.54), channel_id=1, source_target_pairs={{0,2},{2,4},{4,6},{6,0},{1,3},{3,5},{5,7},{7,1},{8,10},{10,12},{12... | collective-permute-start | bytes 1572872 | tf_op jit(solution)/shard_map/ppermute | solution.py:332
  97.0 19.5 %collective-permute-start.10 = (bf16[128,2048]{1,0:T(8,128)(2,1)S(1)}, bf16[128,2048]{1,0:T(8,128)(2,1)S(1)}, u32[]{:S(2)}, u32[]{:S(2)}) collective-permute-start(bf16[128,2048]{1,0:T(8,128)(2,1)S(1)} %get-tuple-element.53), channel_id=1, source_target_pairs={{0,2},{2,4},{4,6},{6,0},{1,3},{3,5},{5,7},{7,1},{8,10},{10,12},{12... | collective-permute-start | bytes 1572872 | tf_op jit(solution)/shard_map/ppermute | solution.py:332
  98.8 17.7 %collective-permute-start.11 = (bf16[128,2048]{1,0:T(8,128)(2,1)S(1)}, bf16[128,2048]{1,0:T(8,128)(2,1)S(1)}, u32[]{:S(2)}, u32[]{:S(2)}) collective-permute-start(bf16[128,2048]{1,0:T(8,128)(2,1)S(1)} %get-tuple-element.52), channel_id=1, source_target_pairs={{0,6},{2,0},{4,2},{6,4},{1,7},{3,1},{5,3},{7,5},{8,14},{10,8},{12,... | collective-permute-start | bytes 1572872 | tf_op jit(solution)/shard_map/ppermute | solution.py:335
  106.1 1.2 copy-start.5
  116.5 62.7 %slice-start = ((s8[6291456]{0:T(1024)(128)(4,1)}), s8[4194304]{0:T(1024)(128)(4,1)S(1)}, s32[]{:S(2)}) async-start(s8[6291456]{0:T(1024)(128)(4,1)} %bitcast.53), calls=%async_computation.4 | async-start | bytes 8388608
  118.3 61.0 %slice-start.1 = ((s8[6291456]{0:T(1024)(128)(4,1)}), s8[2097152]{0:T(1024)(128)(4,1)S(1)}, s32[]{:S(2)}) async-start(s8[6291456]{0:T(1024)(128)(4,1)} %bitcast.53), calls=%async_computation.5 | async-start | bytes 4194304
  203.9 59.2 %copy-start.1 = (bf16[1024,2,256]{2,1,0:T(2,128)(2,1)S(1)}, bf16[1024,2,256]{2,1,0:T(2,128)(2,1)}, u32[]{:S(2)}) copy-start(bf16[1024,2,256]{2,1,0:T(2,128)(2,1)} %param.14) | copy-start | bytes 3145732
Sparse Core Ops, SparseCore 0:
  10.2 56.7 all-gather.2
